TPU v7x, 32 devices: a whole 2x2x4 slice. The times are simulated.
32 devices in a mesh: row: 4 (over x, core), col: 8 (over z, y).
Axes of the slice: x: 2, y: 2, z: 4, core: 2. Of those that a mesh axis runs over, the one named last changes fastest.
Arguments:
- activations: bfloat16 [1024, 8192], P('col', 'row'), may hold values from -6 to 6
- out_grads: bfloat16 [1024, 22016], P('row', 'col'), may hold values from -48 to 48
- basis: float32 [8192, 512], P('row'), may hold values from -0.0625 to 0.0625
- row_moment: float32 [512], P('row'), may hold values from 10240 to 102400
- col_moment: float32 [22016], P('col'), may hold values from 1024 to 204800
Outputs:
- weight_update: float32 [8192, 22016], P('row', 'col')
- row_next: float32 [512], P('row')
- col_next: float32 [22016], P('col')
All inputs are finite; a program needn't handle non-finite values.
Results may differ from a plain program's by a relative error of at most 0.0003.
Values may be sent and summed in bfloat16 or wider, within the bound.
No kernel may reach another device: no remote copies, remote signals or barrier semaphores. Data moves between devices by JAX's collectives and lax.ppermute only.
A program may use at most 128 MiB of HBM per device.

v0:
```python
import jax
import jax.numpy as jnp
from jax import lax
from jax.sharding import PartitionSpec as P

F = 22016
R = 512


beta_two = 0.8
scale_alpha = 0.25
epsilon = 1e-30
highest = lax.Precision.HIGHEST


def per_device(activations, out_grads, basis, row_moment, col_moment):
    grads_all = lax.all_gather(out_grads, "row", axis=0, tiled=True)
    gradient = lax.dot_general(
        lax.all_gather(activations, "col", axis=0, tiled=True),
        grads_all,
        (((0,), (0,)), ((), ())),
        preferred_element_type=jnp.float32,
    )
    columns = basis
    projected = lax.psum_scatter(
        lax.dot_general(columns, gradient, (((0,), (0,)), ((), ())), precision=highest),
        "row",
        scatter_dimension=0,
        tiled=True,
    )
    squares = projected * projected + epsilon
    col_total = lax.psum(jnp.sum(squares, axis=0), "row")
    row_total = lax.psum(jnp.sum(squares, axis=1), "col")
    row_next = beta_two * row_moment + (1.0 - beta_two) * (row_total / F)
    col_next = beta_two * col_moment + (1.0 - beta_two) * (col_total / R)
    row_mean = lax.psum(jnp.sum(row_next), "row") / R
    second = row_next[:, None] * col_next[None, :] / row_mean
    normalized = projected / jnp.sqrt(second)
    columns = basis
    summed = jnp.dot(
        columns, lax.all_gather(normalized, "row", axis=0, tiled=True), precision=highest
    )
    weight_update = scale_alpha * summed
    return (weight_update, row_next, col_next)


def solution(mesh):
    in_specs = (P("col", "row"), P("row", "col"), P("row", None), P("row"), P("col"))
    out_specs = (P("row", "col"), P("row"), P("col"))
    return jax.shard_map(
        per_device, mesh=mesh, in_specs=in_specs, out_specs=out_specs, check_vma=False
    )
```

profile of v0, /device:TPU:0, one launch (start us, length us, event | category | flops | bytes accessed | tf_op | source)
XLA Modules:
  0.0 372.9 jit_solution(2871300236771576171)
XLA Ops:
  7.2 0.0 all-gather.4.cloned.1.call-start
  7.2 0.7 all-gather.4.cloned.1.call-update
  7.9 0.0 all-gather.6.cloned.1.call-start
  7.9 0.7 all-gather.6.cloned.1.call-update
  8.6 0.0 reduce-scatter.2.cloned.1.call-start
  8.7 77.6 %all-gather.4.cloned.1.call-done = bf16[1024,2048]{1,0:T(8,128)(2,1)} async-done(((bf16[128,2048]{1,0:T(8,128)(2,1)}), bf16[1024,2048]{1,0:T(8,128)(2,1)}) %all-gather.4.cloned.1.call-update) | async-done | bytes 4194320 | tf_op jit(solution)/shard_map/all_gather | solution.py:19
  86.3 43.2 %all-gather.6.cloned.1.call-done = bf16[1024,2752]{0,1:T(8,128)(2,1)} async-done(((bf16[256,2752]{0,1:T(8,128)(2,1)}), bf16[1024,2752]{0,1:T(8,128)(2,1)}) %all-gather.6.cloned.1.call-update) | async-done | bytes 5636112 | tf_op jit(solution)/shard_map/all_gather | solution.py:17
  129.5 20.0 %fusion.3 = f32[2048,2752]{1,0:T(8,128)} fusion(bf16[1024,2048]{1,0:T(8,128)(2,1)} %all-gather.4.cloned.1.call-done, bf16[1024,2752]{0,1:T(8,128)(2,1)} %all-gather.6.cloned.1.call-done), kind=kOutput, calls=%fused_computation.9 | convolution fusion | flops 11542724608 | bytes 32374784 | tf_op jit(solution)/shard_map/dot_general | solution.py:18
  149.5 0.0 copy-done.4
  149.5 42.7 %convolution_bitcast_fusion = f32[512,2752]{0,1:T(8,128)} fusion(f32[2048,2752]{1,0:T(8,128)} %fusion.3, f32[2048,512]{1,0:T(8,128)S(1)} %copy-done.4), kind=kOutput, calls=%fused_computation.1 | convolution fusion | flops 34628173824 | bytes 32374784 | tf_op jit(solution)/shard_map/dot_general | solution.py:26
  192.2 0.0 reduce-scatter.2.cloned.1.call-update
  192.3 0.0 all-gather.8.cloned.1.call-start
  192.3 54.1 %reduce-scatter.2.cloned.1.call-done = f32[128,2752]{0,1:T(8,128)} async-done(((f32[512,2752]{0,1:T(8,128)}), f32[128,2752]{0,1:T(8,128)}) %reduce-scatter.2.cloned.1.call-update) | async-done | bytes 1409040 | tf_op jit(solution)/shard_map/reduce_scatter | solution.py:25
  246.4 1.8 fusion
  248.2 21.4 %psum.21 = f32[128]{0:T(128)S(1)} all-reduce(f32[128]{0:T(128)S(1)} %get-tuple-element.4), channel_id=1, replica_groups=mesh['row'=4,'col'=8] {'col'}, use_global_device_ids=true, to_apply=%region_2.0 | all-reduce | flops 128 | bytes 1024 | tf_op jit(solution)/shard_map/psum | solution.py:33
  269.6 0.0 copy-done.3
  269.6 0.6 fusion.2
  270.2 11.4 %all-reduce = (f32[]{:T(128)}, f32[2752]{0:T(1024)S(1)}) all-reduce(f32[]{:T(128)} %get-tuple-element.7, f32[2752]{0:T(1024)S(1)} %get-tuple-element.3), channel_id=1, replica_groups=mesh['row'=4,'col'=8] {'row'}, use_global_device_ids=true, to_apply=%region_6.0 | all-reduce | flops 2753 | bytes 22024 | tf_op jit(solution)/shard_map/psum | solution.py:36
  282.2 0.0 copy-done.1
  282.2 0.0 copy-start
  282.2 2.9 rsqrt_multiply_fusion
  285.1 0.0 all-gather.8.cloned.1.call-update
  285.1 39.4 %all-gather.8.cloned.1.call-done = f32[512,2752]{0,1:T(8,128)} async-done(((f32[128,2752]{0,1:T(8,128)}), f32[512,2752]{0,1:T(8,128)}) %all-gather.8.cloned.1.call-update) | async-done | bytes 5636112 | tf_op jit(solution)/shard_map/all_gather | solution.py:41
  324.6 41.8 %multiply_bitcast_fusion = f32[2048,2752]{0,1:T(8,128)} fusion(f32[512,2752]{0,1:T(8,128)} %all-gather.8.cloned.1.call-done, f32[2048,512]{1,0:T(8,128)} %param.7), kind=kOutput, calls=%fused_computation | convolution fusion | flops 34633809920 | bytes 32374784 | tf_op jit(solution)/shard_map/dot_general | solution.py:40
  (7 shorter events, 0.0 us)
Async XLA Ops:
  7.2 79.1 %all-gather.4.cloned.1.call-start = ((), (), s32[]{:S(2)}) async-start(), calls=%async_computation.1 | async-start | bytes 4718592 | tf_op jit(solution)/shard_map/all_gather | solution.py:19
  7.9 121.6 %all-gather.6.cloned.1.call-start = ((), (), s32[]{:S(2)}) async-start(), calls=%async_computation.2 | async-start | bytes 7045120 | tf_op jit(solution)/shard_map/all_gather | solution.py:17
  8.6 237.7 %reduce-scatter.2.cloned.1.call-start = ((), (), s32[]{:S(2)}) async-start(), calls=%async_computation.3 | async-start | bytes 7045120 | tf_op jit(solution)/shard_map/reduce_scatter | solution.py:25
  129.5 20.0 %copy-start.4 = (f32[2048,512]{1,0:T(8,128)S(1)}, f32[2048,512]{1,0:T(8,128)}, u32[]{:S(2)}) copy-start(f32[2048,512]{1,0:T(8,128)} %param.7) | copy-start | bytes 12582916
  192.2 77.3 %copy-start.3 = (f32[128]{0:T(128)S(1)}, f32[128]{0:T(128)}, u32[]{:S(2)}) copy-start(f32[128]{0:T(128)} %param.8) | copy-start | bytes 1540
  192.2 90.0 %copy-start.1 = (f32[2752]{0:T(1024)S(1)}, f32[2752]{0:T(1024)}, u32[]{:S(2)}) copy-start(f32[2752]{0:T(1024)} %param.9) | copy-start | bytes 33028
  192.3 132.3 %all-gather.8.cloned.1.call-start = ((), (), s32[]{:S(2)}) async-start(), calls=%async_computation.4 | async-start | bytes 7045120 | tf_op jit(solution)/shard_map/all_gather | solution.py:41
  270.2 96.2 %copy-start.2 = (f32[128]{0:T(128)}, f32[128]{0:T(128)S(1)}, u32[]{:S(2)}) copy-start(f32[128]{0:T(128)S(1)} %get-tuple-element.8) | copy-start | bytes 1540
  282.2 84.2 %copy-start = (f32[2752]{0:T(1024)}, f32[2752]{0:T(1024)S(1)}, u32[]{:S(2)}) copy-start(f32[2752]{0:T(1024)S(1)} %multiply_add_fusion.1) | copy-start | bytes 33028
Sparse Core Ops, SparseCore 0:
  10.1 76.0 all-gather.3
  87.8 41.6 all-gather.5
  192.4 53.9 reduce-scatter.1
  285.3 39.2 all-gather.7
where the time goes:
time: 373 us
  waiting for transfers between devices  216 us (58%)
  matrix products  105 us (28%)
  blocking collectives  32.7 us (9%)
  between operations  14.4 us (4%)
  other arithmetic  5.29 us (1%)
    all_gather x1, waiting for transfers between devices, per_device(): lax.all_gather(activations, 'col', axis=0, tiled=True)  77.6 us
    reduce_scatter x1, waiting for transfers between devices, per_device(): lax.psum_scatter(lax.dot_general(columns, gradient, (((0,), (0,)), ((), (...  54.1 us
    all_gather x1, waiting for transfers between devices, per_device(): grads_all = lax.all_gather(out_grads, 'row', axis=0, tiled=True)  43.2 us
    dot_general x1, matrix products, per_device(): lax.dot_general(columns, gradient, (((0,), (0,)), ((), ())), precision=hi...  42.7 us
    dot_general x1, matrix products, per_device(): jnp.dot(columns, lax.all_gather(normalized, 'row', axis=0, tiled=True), p...  41.8 us
    all_gather x1, waiting for transfers between devices, per_device(): lax.all_gather(normalized, 'row', axis=0, tiled=True)  39.4 us
    psum x1, blocking collectives, per_device(): row_total = lax.psum(jnp.sum(squares, axis=1), 'col')  21.4 us
    dot_general x1, matrix products, per_device(): lax.dot_general(lax.all_gather(activations, 'col', axis=0, tiled=True), g...  20 us
  transfers between devices with their start and end apart: 4, of which 4 were waited for; matrix products, arithmetic and copies ran while one was open for 0% of the time, Pallas kernels for 0%

commit v1 on v0

v1 whole, which is shorter than its diff:
```python
import functools

import jax
import jax.numpy as jnp
import numpy as np
from jax import lax
from jax.experimental import pallas as pl
from jax.experimental.pallas import tpu as pltpu
from jax.sharding import PartitionSpec as P

beta_two = 0.8
scale_alpha = 0.25
epsilon = 1e-30
CORES = 2
CHUNKS = 2
TILES = 2
f32 = jnp.float32
bf16 = jnp.bfloat16
f8 = jnp.float8_e4m3fn
MIB = 1 << 20
CODE_TOP = 181.0
TOP_ROWS = 16
VMEM = pl.BlockSpec(memory_space=pltpu.VMEM)
SMEM = pl.BlockSpec(memory_space=pltpu.SMEM)


def split(value):
    high = value.astype(bf16)
    return high, (value - high.astype(f32)).astype(bf16)


def tile_of(size, most, unit):
    return max(t for t in range(unit, most + 1, unit) if size % t == 0)


def low_kernel(streams, where_ref, act_ref, *refs):
    basis = refs[:streams]
    mine_ref, other_ref, acc_ref = refs[streams:]
    step = pl.program_id(0)

    @pl.when(step == 0)
    def _():
        acc_ref[...] = jnp.zeros_like(acc_ref)

    tile = basis[0].shape[0]
    total = acc_ref[...]
    for n, ref in enumerate(basis):
        high, low = split(ref[...])
        acts = act_ref[:, n * tile : (n + 1) * tile]
        total = total + jnp.dot(acts, high, preferred_element_type=f32)
        total = total + jnp.dot(acts, low, preferred_element_type=f32)
    acc_ref[...] = total

    @pl.when(step == pl.num_programs(0) - 1)
    def _():
        half = mine_ref.shape[1]
        core = where_ref[0]
        mine_ref[...] = acc_ref[:, pl.ds(pl.multiple_of(core * half, half), half)]
        other_ref[...] = acc_ref[:, pl.ds(pl.multiple_of((1 - core) * half, half), half)]


def low_partial(where, acts, basis):
    tokens, depth = acts.shape
    rank = basis.shape[1]
    steps, streams = 2, 4
    tile = depth // (steps * streams)
    half = jax.ShapeDtypeStruct((tokens, rank // 2), f32)

    def stream(n):
        return pl.BlockSpec((tile, rank), lambda i, s: (i * streams + n, 0))

    return pl.pallas_call(
        functools.partial(low_kernel, streams),
        out_shape=(half, half),
        grid_spec=pltpu.PrefetchScalarGridSpec(
            num_scalar_prefetch=1,
            grid=(steps,),
            in_specs=[pl.BlockSpec((tokens, tile * streams), lambda i, s: (0, i))]
            + [stream(n) for n in range(streams)],
            out_specs=[pl.BlockSpec((tokens, rank // 2), lambda i, s: (0, 0))] * 2,
            scratch_shapes=[pltpu.VMEM((tokens, rank), f32)],
        ),
        compiler_params=pltpu.CompilerParams(vmem_limit_bytes=56 * MIB),
        cost_estimate=pl.CostEstimate(
            flops=4 * tokens * depth * rank, bytes_accessed=6 * depth * rank, transcendentals=0
        ),
        name="low_partial",
    )(where, acts, *[basis] * streams)


def turn_kernel(basis_ref, high_ref, small_ref):
    rank = basis_ref.shape[1]
    turned = basis_ref[...].T
    high = turned.astype(bf16)
    high_ref[...] = high
    small_ref[:rank, :] = ((turned - high.astype(f32)) * 2.0**20).astype(f8)
    small_ref[rank:, :] = (turned * 2.0**12).astype(f8)


def turn_basis(basis):
    rows, rank = basis.shape
    tile = tile_of(rows, 256, 128)
    return pl.pallas_call(
        turn_kernel,
        out_shape=[
            jax.ShapeDtypeStruct((rank, rows), bf16),
            jax.ShapeDtypeStruct((2 * rank, rows), f8),
        ],
        grid=(rows // tile,),
        in_specs=[pl.BlockSpec((tile, rank), lambda i: (i, 0))],
        out_specs=[
            pl.BlockSpec((rank, tile), lambda i: (0, i)),
            pl.BlockSpec((2 * rank, tile), lambda i: (0, i)),
        ],
        compiler_params=pltpu.CompilerParams(vmem_limit_bytes=8 * MIB),
        cost_estimate=pl.CostEstimate(flops=0, bytes_accessed=8 * rows * rank, transcendentals=0),
        name="turn_basis",
    )(basis)


def encode_kernel(*refs):
    out_ref = refs[-1]
    tokens, lanes = refs[0].shape
    value = refs[0][...]
    for ref in refs[1:-1]:
        value = value + ref[...]
    size = jnp.abs(value)
    top = (jnp.max(size, axis=0, keepdims=True) * (1.0 + 2.0**-7)).astype(bf16).astype(f32)
    top = jnp.maximum(top, 1e-36)
    code = size * (CODE_TOP / top)
    for _ in range(4):
        code = code * code
    out_ref[:tokens, :] = jnp.where(value < 0, -code, code).astype(bf16)
    out_ref[tokens:, :] = jnp.broadcast_to(top, (TOP_ROWS, lanes)).astype(bf16)


def encode(*blocks):
    tokens, lanes = blocks[0].shape
    return pl.pallas_call(
        encode_kernel,
        out_shape=jax.ShapeDtypeStruct((tokens + TOP_ROWS, lanes), bf16),
        in_specs=[VMEM] * len(blocks),
        out_specs=VMEM,
        compiler_params=pltpu.CompilerParams(vmem_limit_bytes=4 * MIB),
        cost_estimate=pl.CostEstimate(
            flops=0, bytes_accessed=8 * tokens * lanes, transcendentals=0
        ),
        name="encode",
    )(*blocks)


def decode(ref):
    tokens = ref.shape[0] - TOP_ROWS
    code = ref[:tokens, :].astype(f32)
    size = jnp.abs(code)
    for _ in range(4):
        size = lax.rsqrt(size)
    size = size * (ref[tokens : tokens + 1, :].astype(f32) * (1.0 / CODE_TOP))
    return jnp.where(code < 0, -size, size)


def assemble_kernel(blocks, offset, where_ref, *refs):
    mine, other = refs[:blocks], refs[blocks : 2 * blocks]
    high_ref, low_ref = refs[2 * blocks :]
    half = high_ref.shape[1] // 2
    core = where_ref[0]
    for refs_of, at in ((mine, core), (other, 1 - core)):
        lanes = pl.ds(pl.multiple_of(at * half, half), half)
        for b in range(blocks):
            tokens = refs_of[b].shape[0] - TOP_ROWS
            rows = pl.ds(pl.multiple_of(where_ref[offset + b] * tokens, tokens), tokens)
            high, low = split(decode(refs_of[b]))
            high_ref[rows, lanes] = high
            low_ref[rows, lanes] = low


def assemble(where, mine, other, offset):
    blocks = len(mine)
    tokens, half = mine[0].shape
    shape = (blocks * (tokens - TOP_ROWS), 2 * half)
    return pl.pallas_call(
        functools.partial(assemble_kernel, blocks, offset),
        out_shape=[jax.ShapeDtypeStruct(shape, bf16)] * 2,
        in_specs=[SMEM] + [VMEM] * (2 * blocks),
        out_specs=[VMEM] * 2,
        compiler_params=pltpu.CompilerParams(vmem_limit_bytes=4 * MIB),
        cost_estimate=pl.CostEstimate(
            flops=0, bytes_accessed=8 * shape[0] * shape[1], transcendentals=0
        ),
        name="assemble",
    )(where, *mine, *other)


def cut_kernel(starts_at, counts, where_ref, grads_ref, *refs):
    outs, sem = refs[:-1], refs[-1]
    copies = []
    for n, out in enumerate(outs):
        rows = out.shape[0]
        at = pl.ds(pl.multiple_of(where_ref[starts_at + n] * 16, 16), rows)
        copies.append(pltpu.make_async_copy(grads_ref.at[at, :], out, sem.at[n]))
    for copy in copies:
        copy.start()
    for copy in copies:
        copy.wait()


def cut(where, grads, sizes, starts_at):
    return pl.pallas_call(
        functools.partial(cut_kernel, starts_at, len(sizes)),
        out_shape=[jax.ShapeDtypeStruct((size, grads.shape[1]), bf16) for size in sizes],
        in_specs=[SMEM, pl.BlockSpec(memory_space=pl.ANY)],
        out_specs=[VMEM] * len(sizes),
        scratch_shapes=[pltpu.SemaphoreType.DMA((len(sizes),))],
        compiler_params=pltpu.CompilerParams(vmem_limit_bytes=4 * MIB),
        cost_estimate=pl.CostEstimate(
            flops=0, bytes_accessed=4 * sum(sizes) * grads.shape[1], transcendentals=0
        ),
        name="cut",
    )(where, grads)


def project_kernel(
    pieces, step, start_at, rows_at, first, where_ref, high_ref, low_ref, moment_ref, most_ref, *refs
):
    out_ref, colnext_ref, sums_ref, top_ref = refs[len(refs) - 4 :]
    grads, moments = refs[:pieces], refs[pieces : len(refs) - 4]
    rows, rank = out_ref.shape
    tokens = grads[0].shape[1]
    order = [
        pl.ds(pl.multiple_of(where_ref[rows_at + p] * tokens, tokens), tokens)
        for p in range(pieces)
    ]
    high = jnp.concatenate([high_ref[at, :] for at in order], axis=0)
    low = jnp.concatenate([low_ref[at, :] for at in order], axis=0)
    sums = jnp.zeros((1, rank), f32)
    if first:
        lanes = moments[0].shape[1]
        owner = lax.broadcasted_iota(jnp.int32, (1, rank), 1) // lanes
        for n, ref in enumerate(moments):
            wide = jnp.concatenate([ref[...]] * (rank // lanes), axis=1)
            sums = jnp.where(owner == where_ref[rows_at + n], wide, sums)
        sums = sums * jnp.where(where_ref[1] == 1, first, 0.0)
    top = most_ref[...]
    for begin in range(0, rows, step):
        at = pl.ds(pl.multiple_of(where_ref[start_at] * 16 + begin, 16), step)
        here = slice(begin, begin + step)
        grad = jnp.concatenate(
            [g[at, :] for g in grads[:2]] + [g[here, :] for g in grads[2:]], axis=1
        )
        total = jnp.dot(grad, high, preferred_element_type=f32) + jnp.dot(
            grad, low, preferred_element_type=f32
        )
        squares = total * total
        sums = sums + jnp.sum(squares, axis=0, keepdims=True)
        quarter = sum(squares[:, n : n + 128] for n in range(0, rank, 128))
        col_next = beta_two * moment_ref[at, :] + (1.0 - beta_two) * (
            jnp.sum(quarter, axis=1, keepdims=True) / rank + epsilon
        )
        part = total * lax.rsqrt(col_next)
        top = jnp.maximum(top, jnp.max(jnp.abs(part), axis=0, keepdims=True))
        out_ref[here, :] = part
        long = colnext_ref.shape[1]
        wide = jnp.broadcast_to(col_next, (step, 128))
        if long > step:
            wide = jnp.concatenate([wide, jnp.zeros((long - step, 128), f32)], axis=0)
        colnext_ref[begin // step : begin // step + 1, :] = wide.T[:1, :]
    sums_ref[...] = sums
    top_ref[...] = top


def project(where, high, low, moment, most, grads, moments, rows, step, start_at, rows_at, first):
    tokens, rank = high.shape
    long = -(-step // 128) * 128
    return pl.pallas_call(
        functools.partial(project_kernel, len(grads), step, start_at, rows_at, first),
        out_shape=[
            jax.ShapeDtypeStruct((rows, rank), f32),
            jax.ShapeDtypeStruct((rows // step, long), f32),
            jax.ShapeDtypeStruct((1, rank), f32),
            jax.ShapeDtypeStruct((1, rank), f32),
        ],
        in_specs=[SMEM] + [VMEM] * (4 + len(grads) + len(moments)),
        out_specs=[VMEM] * 4,
        compiler_params=pltpu.CompilerParams(vmem_limit_bytes=16 * MIB),
        cost_estimate=pl.CostEstimate(
            flops=4 * tokens * rows * rank,
            bytes_accessed=2 * rows * tokens + 4 * tokens * rank + 4 * rows * rank,
            transcendentals=0,
        ),
        name="project",
    )(where, high, low, moment, most, *grads, *moments)


def update_kernel(
    count, parts, rows_at, order_at, where_ref, sums_ref, most_ref, high_ref, small_ref, *refs
):
    part_refs, col_refs = refs[:parts], refs[parts : 2 * parts]
    out_ref, rownext_ref, colnext_ref, lhs_ref, lhs_small_ref, scale_ref = refs[2 * parts :]
    tile, rank = lhs_ref.shape
    step = pl.program_id(0)

    @pl.when(step == 0)
    def _():
        row_next = (1.0 - beta_two) * (sums_ref[...] / count + epsilon)
        rows = rownext_ref.shape[1]
        held = jnp.zeros((1, rows), f32)
        for r in range(rank // rows):
            held = jnp.where(where_ref[rows_at] == r, row_next[:, r * rows : (r + 1) * rows], held)
        rownext_ref[...] = held
        scale = scale_alpha * lax.rsqrt(row_next) * jnp.sqrt(
            jnp.mean(row_next, axis=1, keepdims=True)
        )
        strip = colnext_ref.shape[1]
        number = 0
        for ref in col_refs:
            for n in range(ref.shape[0]):
                at = pl.ds(where_ref[order_at + number * TILES] // TILES, 1)
                colnext_ref[at, :] = ref[n : n + 1, :strip]
                number += 1
        top = jnp.maximum(jnp.max(scale * most_ref[...], axis=1, keepdims=True), 1e-30)
        scale_ref[0:1, :] = scale
        scale_ref[1:2, :] = jnp.broadcast_to(2.0**7 / top, (1, rank))
        scale_ref[2:3, :] = jnp.broadcast_to(top * 2.0**-27, (1, rank))

    first = 0
    for part_ref in part_refs:
        tiles = part_ref.shape[0] // tile

        @pl.when((step >= first) & (step < first + tiles))
        def _():
            at = pl.ds(pl.multiple_of((step - first) * tile, 8), tile)
            value = part_ref[at, :] * scale_ref[0:1, :]
            high = value.astype(bf16)
            grow = scale_ref[1:2, :]
            lhs_ref[...] = high
            lhs_small_ref[:, :rank] = (value * grow).astype(f8)
            lhs_small_ref[:, rank:] = ((value - high.astype(f32)) * (grow * 2.0**8)).astype(f8)

        first += tiles

    out_ref[...] = jnp.dot(
        lhs_ref[...], high_ref[...], preferred_element_type=f32
    ) + scale_ref[2:3, 0:1] * jnp.dot(
        lhs_small_ref[...], small_ref[...], preferred_element_type=f32
    )


def update(where, sums, most, high, small, parts, cols, strip, hidden, n_row, rows_at, order_at):
    rank, rows = high.shape
    columns = sum(part.shape[0] for part in parts)
    tile = strip // TILES
    steps = columns // tile
    return pl.pallas_call(
        functools.partial(update_kernel, float(hidden), len(parts), rows_at, order_at),
        out_shape=[
            jax.ShapeDtypeStruct((columns, rows), f32),
            jax.ShapeDtypeStruct((1, rank // n_row), f32),
            jax.ShapeDtypeStruct((columns // strip, strip), f32),
        ],
        grid_spec=pltpu.PrefetchScalarGridSpec(
            num_scalar_prefetch=1,
            grid=(steps,),
            in_specs=[VMEM] * (4 + 2 * len(parts)),
            out_specs=[
                pl.BlockSpec((tile, rows), lambda i, s: (s[order_at + i], 0)),
                pl.BlockSpec((1, rank // n_row), lambda i, s: (0, 0)),
                pl.BlockSpec((columns // strip, strip), lambda i, s: (0, 0)),
            ],
            scratch_shapes=[
                pltpu.VMEM((tile, rank), bf16),
                pltpu.VMEM((tile, 2 * rank), f8),
                pltpu.VMEM((8, rank), f32),
            ],
        ),
        compiler_params=pltpu.CompilerParams(vmem_limit_bytes=20 * MIB),
        cost_estimate=pl.CostEstimate(
            flops=4 * columns * rank * rows, bytes_accessed=4 * columns * rows, transcendentals=0
        ),
        name="update",
    )(where, sums, most, high, small, *parts, *cols)


def per_device(n_row, n_col, activations, out_grads, basis, row_moment, col_moment):
    chips = n_row // CORES
    columns = col_moment.shape[0]
    hidden = columns * n_col
    rank = basis.shape[1]
    width = -(-columns // (32 * chips)) * 32
    pad = width * chips - columns
    rows = width // CHUNKS
    ring = [0, 2, 4, 6, 7, 5, 3, 1] if n_col == 8 else list(range(n_col))
    forward, backward = n_col // 2, (n_col - 1) // 2
    jobs = [(0, 0, width)] + [(j, q, rows) for j in range(1, chips) for q in range(CHUNKS)]

    def to_sibling(value):
        return lax.ppermute(value, "row", [(r, r ^ 1) for r in range(n_row)])

    def to_chip(value, shift):
        pairs = [(r, (r + CORES * shift) % n_row) for r in range(n_row)]
        return lax.ppermute(value, "row", pairs)

    def around(value, step):
        pairs = [(ring[i], ring[(i + step) % n_col]) for i in range(n_col)]
        return lax.ppermute(value, "col", pairs)

    def after(value, *others):
        return lax.optimization_barrier((value, others))[0]

    table = []
    for r in range(n_row):
        for c in range(n_col):
            p, x, k = ring.index(c), r // CORES, r % CORES
            entry = [k, int(c == 0), r, r ^ 1]
            for s in range(1, chips):
                there = (x - s) % chips
                entry += [CORES * there + k, CORES * there + 1 - k]
            order = [p] + [p - s for s in range(1, forward + 1)]
            order += [p + s for s in range(1, backward + 1)]
            blocks_at = len(entry)
            entry += [ring[i % n_col] for i in order]
            starts_at = len(entry)
            entry += [((x + j) % chips * width + q * rows) // 16 for j, q, _ in jobs]
            sends_at = len(entry)
            entry += [
                ((x + s + j) % chips * width + q * rows) // 16
                for j, q, _ in jobs for s in range(1, chips)
            ]
            order_at = len(entry)
            for j, q, size in jobs:
                first = ((x + j) % chips * CHUNKS + q) * TILES
                entry += [first + t for t in range(size * TILES // rows)]
            table.append(entry)
    flat = lax.axis_index("row") * n_col + lax.axis_index("col")
    where = lax.dynamic_index_in_dim(np.array(table, np.int32), flat, 0, False)
    rows_at = 2

    mine, other = low_partial(where, activations, basis)
    mine = mine + to_sibling(other)
    mine = encode(mine, *[to_chip(mine, s) for s in range(1, chips)])

    grads = out_grads.T
    moment = after(col_moment, mine)[:, None]
    if pad:
        grads = jnp.pad(grads, ((0, pad), (0, 0)))
        moment = jnp.pad(moment, ((0, pad), (0, 0)), constant_values=1.0)
    grads = after(grads, other)
    sends = cut(where, grads, [size for _, _, size in jobs for _ in range(1, chips)], sends_at)
    sends = [sends[n * (chips - 1) : (n + 1) * (chips - 1)] for n in range(len(jobs))]
    sibling = to_sibling(after(grads, mine))
    moments = after(row_moment, mine)[None]
    moments = [moments, to_sibling(moments)]

    def exchange(job, *others):
        return [to_chip(after(value, *others), s) for s, value in enumerate(sends[job], 1)]

    def pass_on(got, *others):
        got = [after(value, *others) for value in got]
        return [both for value in got for both in (value, to_sibling(value))]

    ahead, behind, other_ahead, other_behind = [mine], [mine], [], []
    got = [exchange(0, mine)]
    for hop in range(forward):
        moving = [around(ahead[-1], 1)]
        if hop < backward:
            moving.append(around(behind[-1], -1))
        passing = [to_sibling(ahead[-1])] + ([to_sibling(behind[-1])] if hop else [])
        extra = got[0] if hop == forward - 1 else []
        if hop == 1:
            turned = turn_basis(after(basis, *ahead))
            extra = [*turned]
        moved = lax.optimization_barrier((*moving, *passing, *extra))
        ahead.append(moved[0])
        behind += moved[1 : len(moving)]
        other_ahead.append(moved[len(moving)])
        other_behind += moved[len(moving) + 1 : len(moving) + len(passing)]
        if hop == forward - 1:
            passed = [pass_on(got[0], *moved)]
            got.append(exchange(1, *moved))
    other_ahead.append(to_sibling(ahead[-1]))
    while len(other_behind) < backward:
        other_behind.append(to_sibling(behind[len(other_behind) + 1]))
    high, low = assemble(where, ahead + behind[1:], other_ahead + other_behind, blocks_at)

    found = []

    def project_job(job, most):
        part, col_next, sums, top = project(
            where, high, low, moment, most, [grads, sibling] + passed[job],
            [] if job else moments, jobs[job][2], rows, starts_at + job, rows_at,
            0.0 if job else hidden * beta_two / (1.0 - beta_two),
        )
        found.append((part, col_next))
        return sums, top

    sums, top = project_job(0, jnp.zeros((1, rank), f32))
    sums = after(sums, *got[1])
    sums = sum((to_chip(sums, s) for s in range(1, chips)), sums)
    passed.append(pass_on(got[1], sums))
    for job in range(2, len(jobs)):
        got.append(exchange(job, sums))
    step, job = 1, 1
    while step < n_col:
        arrived = lax.ppermute(sums, "col", [(c, c ^ step) for c in range(n_col)])
        if step > 1 and job < len(jobs):
            _, top = project_job(job, top)
            arrived, top = lax.optimization_barrier((arrived, top))
            job += 1
        sums = sums + arrived
        if step == 2:
            for n in range(2, len(jobs)):
                passed.append(pass_on(got[n], sums))
        step *= 2
    while job < len(jobs):
        _, top = project_job(job, top)
        job += 1

    updated, row_next, col_next = update(
        where, sums, top, *turned, [part for part, _ in found], [col for _, col in found],
        rows, hidden, n_row, rows_at, order_at,
    )
    return (updated[:columns].T, row_next[0], col_next.reshape(-1)[:columns])


def solution(mesh):
    in_specs = (P("col", "row"), P("row", "col"), P("row", None), P("row"), P("col"))
    out_specs = (P("row", "col"), P("row"), P("col"))
    return jax.shard_map(
        functools.partial(per_device, mesh.shape["row"], mesh.shape["col"]),
        mesh=mesh, in_specs=in_specs, out_specs=out_specs, check_vma=False,
    )
```

time: 373 us -> 90.5 us (0.24)
  waiting for transfers between devices: 216 us -> 26.5 us
  matrix products: 105 us -> 0 us
  Pallas kernels: 0 us -> 40.1 us
  blocking collectives: 32.7 us -> 0 us
  starting transfers between devices: 0.16 us -> 19.7 us
  between operations: 14.4 us -> 0.76 us
  other arithmetic: 5.29 us -> 0.94 us
    all_gather x3 -> x0, waiting for transfers between devices: 160 us -> none  [the longest x1 77.6 us: per_device(): lax.all_gather(activations, 'col', axis=0, tiled=True)]
    dot_general x3 -> x0, matrix products: 105 us -> none  [the longest x1 42.7 us: per_device(): lax.dot_general(columns, gradient, (((0,), (0,)), ((), ())), precision=hi...]
    reduce_scatter x1 -> x0, waiting for transfers between devices: 54.1 us -> none  [per_device(): lax.psum_scatter(lax.dot_general(columns, gradient, (((0,), (0,)), ((), (...]
    pallas_call x0 -> x9, Pallas kernels: none -> 40.1 us  [the longest x1 18.5 us: update(): pl.pallas_call(functools.partial(update_kernel, float(hidden), len(parts)...]
    psum x2 -> x0, blocking collectives: 32.7 us -> none  [the longest x1 21.4 us: per_device(): row_total = lax.psum(jnp.sum(squares, axis=1), 'col')]
    ppermute x0 -> x29, waiting for transfers between devices: none -> 26.5 us  [the longest x7 11.2 us: around(): return lax.ppermute(value, 'col', pairs)]
    ppermute x0 -> x29, starting transfers between devices: none -> 19.7 us  [the longest x7 6.59 us: around(): return lax.ppermute(value, 'col', pairs)]
  transfers between devices with their start and end apart: 4 -> 29, of which waited for: 4 -> 19; matrix products, arithmetic and copies ran while one was open for 0% -> 0% of each run, Pallas kernels for 0% -> 19%
where the time goes in v1:
time: 90.5 us; the launch traced here: 90.3 us
  Pallas kernels  40.1 us (44%)
  waiting for transfers between devices  26.5 us (29%)
  starting transfers between devices  19.7 us (22%)
  local copies, waits for them, and re-layouts  2.33 us (3%)
  other arithmetic  0.94 us (1%)
    pallas_call x1, Pallas kernels, update(): pl.pallas_call(functools.partial(update_kernel, float(hidden), len(parts)...  18.5 us
    pallas_call x3, Pallas kernels, project(): pl.pallas_call(functools.partial(project_kernel, len(grads), step, start_...  11.8 us
    ppermute x7, waiting for transfers between devices, around(): return lax.ppermute(value, 'col', pairs)  11.2 us
    ppermute x5, waiting for transfers between devices, to_chip(): return lax.ppermute(value, 'row', pairs)  9.44 us
    ppermute x7, starting transfers between devices, around(): return lax.ppermute(value, 'col', pairs)  6.59 us
    ppermute x5, starting transfers between devices, to_chip(): return lax.ppermute(value, 'row', pairs)  6.39 us
    pallas_call x1, Pallas kernels, low_partial(): pl.pallas_call(functools.partial(low_kernel, streams), out_shape=(half, h...  4.79 us
    ppermute x3, starting transfers between devices, per_device(): arrived = lax.ppermute(sums, 'col', [(c, c ^ step) for c in range(n_col)])  4.23 us
  transfers between devices with their start and end apart: 29, of which 19 were waited for; matrix products, arithmetic and copies ran while one was open for 0% of the time, Pallas kernels for 19%

profile of v1, /device:TPU:0, one launch (start us, length us, event | category | flops | bytes accessed | tf_op | source)
XLA Modules:
  0.0 90.3 jit_solution(7471300199297654179)
XLA Ops:
  1.9 4.8 %low_partial.1 = (f32[128,256]{1,0:T(8,128)}, f32[128,256]{1,0:T(8,128)}) custom-call(s32[28]{0:T(128)} %dynamic-slice_bitcast_fusion.where_ref, bf16[128,2048]{1,0:T(8,128)(2,1)} %act_ref.1, f32[2048,512]{1,0:T(8,128)} %basis_ref, f32[2048,512]{1,0:T(8,128)} %basis_ref, f32[2048,512]{1,0:T(8,128)} %basis_ref, f32[2048,512]{1,0:T(8,128)} %basis_ref), custom_call_target="tpu_custom_call" | custom-call | flops 536870912 | bytes 6291456 | tf_op jit(solution)/shard_map/low_partial/pallas_call | solution.py:72
  9.2 2.9 %collective-permute-start.1 = (f32[128,256]{1,0:T(8,128)S(1)}, f32[128,256]{1,0:T(8,128)S(1)}, u32[]{:S(2)}, u32[]{:S(2)}) collective-permute-start(f32[128,256]{1,0:T(8,128)S(1)} %add.24.refs_0_), channel_id=1, source_target_pairs={{0,16},{8,24},{16,0},{24,8},{1,17},{9,25},{17,1},{25,9},{2,18},{10... | collective-permute-start | bytes 393224 | tf_op jit(solution)/shard_map/ppermute | solution.py:400
  13.3 2.7 %collective-permute-done.1.refs_1_ = f32[128,256]{1,0:T(8,128)S(1)} collective-permute-done((f32[128,256]{1,0:T(8,128)S(1)}, f32[128,256]{1,0:T(8,128)S(1)}, u32[]{:S(2)}, u32[]{:S(2)}) %collective-permute-start.1) | collective-permute-done | bytes 131104 | tf_op jit(solution)/shard_map/ppermute | solution.py:400
  16.0 1.8 %collective-permute-start.16 = (bf16[1376,256]{1,0:T(8,128)(2,1)S(1)}, bf16[1376,256]{1,0:T(8,128)(2,1)S(1)}, u32[]{:S(2)}, u32[]{:S(2)}) collective-permute-start(bf16[1376,256]{1,0:T(8,128)(2,1)S(1)} %get-tuple-element.69), channel_id=1, source_target_pairs={{0,16},{8,24},{16,0},{24,8},{1,17},{9,25},{17,1},{25,9},{2,18},{10... | collective-permute-start | bytes 2113544 | tf_op jit(solution)/shard_map/ppermute | solution.py:400
  18.4 1.5 %collective-permute-start.3 = (bf16[144,256]{1,0:T(8,128)(2,1)S(1)}, bf16[144,256]{1,0:T(8,128)(2,1)S(1)}, u32[]{:S(2)}, u32[]{:S(2)}) collective-permute-start(bf16[144,256]{1,0:T(8,128)(2,1)S(1)} %encode.1.refs_0_), channel_id=1, source_target_pairs={{0,1},{2,0},{4,2},{6,4},{7,6},{5,7},{3,5},{1,3},{8,9},{10,8},{12,1... | collective-permute-start | bytes 221192 | tf_op jit(solution)/shard_map/ppermute | solution.py:404
  21.1 1.6 %collective-permute-done.3.refs_5_ = bf16[144,256]{1,0:T(8,128)(2,1)S(1)} collective-permute-done((bf16[144,256]{1,0:T(8,128)(2,1)S(1)}, bf16[144,256]{1,0:T(8,128)(2,1)S(1)}, u32[]{:S(2)}, u32[]{:S(2)}) %collective-permute-start.3) | collective-permute-done | bytes 73760 | tf_op jit(solution)/shard_map/ppermute | solution.py:404
  22.7 1.5 %collective-permute-done.2.refs_1_ = bf16[144,256]{1,0:T(8,128)(2,1)S(1)} collective-permute-done((bf16[144,256]{1,0:T(8,128)(2,1)S(1)}, bf16[144,256]{1,0:T(8,128)(2,1)S(1)}, u32[]{:S(2)}, u32[]{:S(2)}) %collective-permute-start.2) | collective-permute-done | bytes 73760 | tf_op jit(solution)/shard_map/ppermute | solution.py:404
  24.2 1.6 %collective-permute-start.6 = (bf16[144,256]{1,0:T(8,128)(2,1)S(1)}, bf16[144,256]{1,0:T(8,128)(2,1)S(1)}, u32[]{:S(2)}, u32[]{:S(2)}) collective-permute-start(bf16[144,256]{1,0:T(8,128)(2,1)S(1)} %collective-permute-done.3.refs_5_), channel_id=1, source_target_pairs={{0,1},{2,0},{4,2},{6,4},{7,6},{5,7},{3,5},{1,3},{8,9},{10,8},{12,1... | collective-permute-start | bytes 221192 | tf_op jit(solution)/shard_map/ppermute | solution.py:404
  26.5 2.1 %turn_basis.1 = (bf16[512,2048]{1,0:T(8,128)(2,1)S(1)}, f8e4m3fn[1024,2048]{1,0:T(32,128)(4,1)S(1)}) custom-call(f32[2048,512]{1,0:T(8,128)S(1)} %copy-done), custom_call_target="tpu_custom_call" | custom-call | bytes 8388608 | tf_op jit(solution)/shard_map/turn_basis/pallas_call | solution.py:103
  28.9 1.6 %collective-permute-done.5.refs_2_ = bf16[144,256]{1,0:T(8,128)(2,1)S(1)} collective-permute-done((bf16[144,256]{1,0:T(8,128)(2,1)S(1)}, bf16[144,256]{1,0:T(8,128)(2,1)S(1)}, u32[]{:S(2)}, u32[]{:S(2)}) %collective-permute-start.5) | collective-permute-done | bytes 73760 | tf_op jit(solution)/shard_map/ppermute | solution.py:404
  31.8 1.6 %collective-permute-start.10 = (bf16[144,256]{1,0:T(8,128)(2,1)S(1)}, bf16[144,256]{1,0:T(8,128)(2,1)S(1)}, u32[]{:S(2)}, u32[]{:S(2)}) collective-permute-start(bf16[144,256]{1,0:T(8,128)(2,1)S(1)} %collective-permute-done.6.refs_6_), channel_id=1, source_target_pairs={{0,1},{2,0},{4,2},{6,4},{7,6},{5,7},{3,5},{1,3},{8,9},{10,8},{12,1... | collective-permute-start | bytes 221192 | tf_op jit(solution)/shard_map/ppermute | solution.py:404
  33.3 1.8 %collective-permute-done.9.refs_3_ = bf16[144,256]{1,0:T(8,128)(2,1)S(1)} collective-permute-done((bf16[144,256]{1,0:T(8,128)(2,1)S(1)}, bf16[144,256]{1,0:T(8,128)(2,1)S(1)}, u32[]{:S(2)}, u32[]{:S(2)}) %collective-permute-start.9) | collective-permute-done | bytes 73760 | tf_op jit(solution)/shard_map/ppermute | solution.py:404
  37.5 3.4 %collective-permute-done.13.refs_4_ = bf16[144,256]{1,0:T(8,128)(2,1)S(1)} collective-permute-done((bf16[144,256]{1,0:T(8,128)(2,1)S(1)}, bf16[144,256]{1,0:T(8,128)(2,1)S(1)}, u32[]{:S(2)}, u32[]{:S(2)}) %collective-permute-start.13) | collective-permute-done | bytes 73760 | tf_op jit(solution)/shard_map/ppermute | solution.py:404
  43.3 1.7 %assemble.1 = (bf16[1024,512]{1,0:T(8,128)(2,1)S(1)}, bf16[1024,512]{1,0:T(8,128)(2,1)S(1)}) custom-call(s32[28]{0:T(128)S(1)} %copy-done.2, bf16[144,256]{1,0:T(8,128)(2,1)S(1)} %encode.1.refs_0_, bf16[144,256]{1,0:T(8,128)(2,1)S(1)} %collective-permute-done.2.refs_1_, bf16[144,256]{1,0:T(8,128)(2,1)S(1)} %collective-permute-done.5.refs_2_, ...), custom_call_target="tpu_custom_call" | custom-call | bytes 4194304 | tf_op jit(solution)/shard_map/assemble/pallas_call | solution.py:181
  45.0 4.7 %project.3 = (f32[1376,512]{1,0:T(8,128)S(1)}, f32[2,768]{1,0:T(2,128)S(1)}, f32[1,512]{1,0:T(1,128)S(1)}, f32[1,512]{1,0:T(1,128)S(1)}) custom-call(s32[28]{0:T(128)S(1)} %copy-done.2, bf16[1024,512]{1,0:T(8,128)(2,1)S(1)} %get-tuple-element.78.high_ref, bf16[1024,512]{1,0:T(8,128)(2,1)S(1)} %get-tuple-element.79.low_ref, ...), custom_call_target="tpu_custom_call" | custom-call | flops 2885681152 | bytes 7733248 | tf_op jit(solution)/shard_map/project/pallas_call | solution.py:274
  49.7 2.0 %collective-permute-done.21.refs_2_ = bf16[688,256]{1,0:T(8,128)(2,1)S(1)} collective-permute-done((bf16[688,256]{1,0:T(8,128)(2,1)S(1)}, bf16[688,256]{1,0:T(8,128)(2,1)S(1)}, u32[]{:S(2)}, u32[]{:S(2)}) %collective-permute-start.21) | collective-permute-done | bytes 352288 | tf_op jit(solution)/shard_map/ppermute | solution.py:400
  52.2 3.0 %collective-permute-done.22 = f32[1,512]{1,0:T(1,128)S(1)} collective-permute-done((f32[1,512]{1,0:T(1,128)S(1)}, f32[1,512]{1,0:T(1,128)S(1)}, u32[]{:S(2)}, u32[]{:S(2)}) %collective-permute-start.22) | collective-permute-done | bytes 2080 | tf_op jit(solution)/shard_map/ppermute | solution.py:400
  55.8 1.6 %collective-permute-start.23 = (f32[1,512]{1,0:T(1,128)S(1)}, f32[1,512]{1,0:T(1,128)S(1)}, u32[]{:S(2)}, u32[]{:S(2)}) collective-permute-start(f32[1,512]{1,0:T(1,128)S(1)} %add.25), channel_id=1, source_target_pairs={{0,1},{1,0},{2,3},{3,2},{4,5},{5,4},{6,7},{7,6},{8,9},{9,8},{10,11... | collective-permute-start | bytes 6152 | tf_op jit(solution)/shard_map/ppermute | solution.py:503
  57.4 2.0 %collective-permute-done.23 = f32[1,512]{1,0:T(1,128)S(1)} collective-permute-done((f32[1,512]{1,0:T(1,128)S(1)}, f32[1,512]{1,0:T(1,128)S(1)}, u32[]{:S(2)}, u32[]{:S(2)}) %collective-permute-start.23) | collective-permute-done | bytes 2080 | tf_op jit(solution)/shard_map/ppermute | solution.py:503
  60.6 3.6 %project.4 = (f32[688,512]{1,0:T(8,128)S(1)}, f32[1,768]{1,0:T(1,128)S(1)}, f32[1,512]{1,0:T(1,128)}, f32[1,512]{1,0:T(1,128)S(1)}) custom-call(s32[28]{0:T(128)S(1)} %copy-done.2, bf16[1024,512]{1,0:T(8,128)(2,1)S(1)} %get-tuple-element.78.high_ref, bf16[1024,512]{1,0:T(8,128)(2,1)S(1)} %get-tuple-element.79.low_ref, ...), custom_call_target="tpu_custom_call" | custom-call | flops 1442840576 | bytes 4915200 | tf_op jit(solution)/shard_map/project/pallas_call | solution.py:274
  64.2 1.7 %collective-permute-done.27.refs_2_ = bf16[688,256]{1,0:T(8,128)(2,1)S(1)} collective-permute-done((bf16[688,256]{1,0:T(8,128)(2,1)S(1)}, bf16[688,256]{1,0:T(8,128)(2,1)S(1)}, u32[]{:S(2)}, u32[]{:S(2)}) %collective-permute-start.27) | collective-permute-done | bytes 352288 | tf_op jit(solution)/shard_map/ppermute | solution.py:400
  65.9 1.5 %collective-permute-start.26 = (f32[1,512]{1,0:T(1,128)S(1)}, f32[1,512]{1,0:T(1,128)S(1)}, u32[]{:S(2)}, u32[]{:S(2)}) collective-permute-start(f32[1,512]{1,0:T(1,128)S(1)} %add.27), channel_id=1, source_target_pairs={{0,4},{1,5},{2,6},{3,7},{4,0},{5,1},{6,2},{7,3},{8,12},{9,13},{10,... | collective-permute-start | bytes 6152 | tf_op jit(solution)/shard_map/ppermute | solution.py:503
  67.6 3.6 %project.5 = (f32[688,512]{1,0:T(8,128)S(1)}, f32[1,768]{1,0:T(1,128)S(1)}, f32[1,512]{1,0:T(1,128)}, f32[1,512]{1,0:T(1,128)S(1)}) custom-call(s32[28]{0:T(128)S(1)} %copy-done.2, bf16[1024,512]{1,0:T(8,128)(2,1)S(1)} %get-tuple-element.78.high_ref, bf16[1024,512]{1,0:T(8,128)(2,1)S(1)} %get-tuple-element.79.low_ref, ...), custom_call_target="tpu_custom_call" | custom-call | flops 1442840576 | bytes 4915200 | tf_op jit(solution)/shard_map/project/pallas_call | solution.py:274
  71.2 18.5 %update.1 = (f32[2752,2048]{1,0:T(8,128)}, f32[1,128]{1,0:T(1,128)}, f32[4,688]{1,0:T(4,128)S(1)}) custom-call(s32[28]{0:T(128)S(1)} %copy-done.2, f32[1,512]{1,0:T(1,128)S(1)} %add.28.sums_ref, f32[1,512]{1,0:T(1,128)S(1)} %get-tuple-element.99.most_ref, bf16[512,2048]{1,0:T(8,128)(2,1)S(1)} %get-tuple-element.61.high_ref, ...), custom_call_target="tpu_custom_call" | custom-call | flops 11542724608 | bytes 22544384 | tf_op jit(solution)/shard_map/update/pallas_call | solution.py:353
  (62 shorter events, 16.8 us)
Async XLA Ops:
  9.2 6.7 %collective-permute-start.1 = (f32[128,256]{1,0:T(8,128)S(1)}, f32[128,256]{1,0:T(8,128)S(1)}, u32[]{:S(2)}, u32[]{:S(2)}) collective-permute-start(f32[128,256]{1,0:T(8,128)S(1)} %add.24.refs_0_), channel_id=1, source_target_pairs={{0,16},{8,24},{16,0},{24,8},{1,17},{9,25},{17,1},{25,9},{2,18},{10... | collective-permute-start | bytes 393224 | tf_op jit(solution)/shard_map/ppermute | solution.py:400
  16.0 24.9 %collective-permute-start.16 = (bf16[1376,256]{1,0:T(8,128)(2,1)S(1)}, bf16[1376,256]{1,0:T(8,128)(2,1)S(1)}, u32[]{:S(2)}, u32[]{:S(2)}) collective-permute-start(bf16[1376,256]{1,0:T(8,128)(2,1)S(1)} %get-tuple-element.69), channel_id=1, source_target_pairs={{0,16},{8,24},{16,0},{24,8},{1,17},{9,25},{17,1},{25,9},{2,18},{10... | collective-permute-start | bytes 2113544 | tf_op jit(solution)/shard_map/ppermute | solution.py:400
  17.8 27.1 %collective-permute-start.18 = (bf16[2752,256]{1,0:T(8,128)(2,1)S(1)}, bf16[2752,256]{1,0:T(8,128)(2,1)S(1)}, u32[]{:S(2)}, u32[]{:S(2)}) collective-permute-start(bf16[2752,256]{1,0:T(8,128)(2,1)S(1)} %bitcast.7), channel_id=1, source_target_pairs={{0,8},{8,0},{16,24},{24,16},{1,9},{9,1},{17,25},{25,17},{2,10},{10... | collective-permute-start | bytes 4227080 | tf_op jit(solution)/shard_map/ppermute | solution.py:396
  17.9 3.3 %collective-permute-start.4 = (bf16[144,256]{1,0:T(8,128)(2,1)S(1)}, bf16[144,256]{1,0:T(8,128)(2,1)S(1)}, u32[]{:S(2)}, u32[]{:S(2)}) collective-permute-start(bf16[144,256]{1,0:T(8,128)(2,1)S(1)} %encode.1.refs_0_), channel_id=1, source_target_pairs={{0,8},{8,0},{16,24},{24,16},{1,9},{9,1},{17,25},{25,17},{2,10},{10... | collective-permute-start | bytes 221192 | tf_op jit(solution)/shard_map/ppermute | solution.py:396
  18.4 4.4 %collective-permute-start.3 = (bf16[144,256]{1,0:T(8,128)(2,1)S(1)}, bf16[144,256]{1,0:T(8,128)(2,1)S(1)}, u32[]{:S(2)}, u32[]{:S(2)}) collective-permute-start(bf16[144,256]{1,0:T(8,128)(2,1)S(1)} %encode.1.refs_0_), channel_id=1, source_target_pairs={{0,1},{2,0},{4,2},{6,4},{7,6},{5,7},{3,5},{1,3},{8,9},{10,8},{12,1... | collective-permute-start | bytes 221192 | tf_op jit(solution)/shard_map/ppermute | solution.py:404
  19.9 4.4 %collective-permute-start.2 = (bf16[144,256]{1,0:T(8,128)(2,1)S(1)}, bf16[144,256]{1,0:T(8,128)(2,1)S(1)}, u32[]{:S(2)}, u32[]{:S(2)}) collective-permute-start(bf16[144,256]{1,0:T(8,128)(2,1)S(1)} %encode.1.refs_0_), channel_id=1, source_target_pairs={{0,2},{2,4},{4,6},{6,7},{7,5},{5,3},{3,1},{1,0},{8,10},{10,12},{12... | collective-permute-start | bytes 221192 | tf_op jit(solution)/shard_map/ppermute | solution.py:404
  24.2 1.8 %collective-permute-start.8 = (bf16[144,256]{1,0:T(8,128)(2,1)S(1)}, bf16[144,256]{1,0:T(8,128)(2,1)S(1)}, u32[]{:S(2)}, u32[]{:S(2)}) collective-permute-start(bf16[144,256]{1,0:T(8,128)(2,1)S(1)} %collective-permute-done.3.refs_5_), channel_id=1, source_target_pairs={{0,8},{8,0},{16,24},{24,16},{1,9},{9,1},{17,25},{25,17},{2,10},{10... | collective-permute-start | bytes 221192 | tf_op jit(solution)/shard_map/ppermute | solution.py:396
  24.2 4.7 %collective-permute-start.6 = (bf16[144,256]{1,0:T(8,128)(2,1)S(1)}, bf16[144,256]{1,0:T(8,128)(2,1)S(1)}, u32[]{:S(2)}, u32[]{:S(2)}) collective-permute-start(bf16[144,256]{1,0:T(8,128)(2,1)S(1)} %collective-permute-done.3.refs_5_), channel_id=1, source_target_pairs={{0,1},{2,0},{4,2},{6,4},{7,6},{5,7},{3,5},{1,3},{8,9},{10,8},{12,1... | collective-permute-start | bytes 221192 | tf_op jit(solution)/shard_map/ppermute | solution.py:404
  25.8 3.1 %collective-permute-start.7 = (bf16[144,256]{1,0:T(8,128)(2,1)S(1)}, bf16[144,256]{1,0:T(8,128)(2,1)S(1)}, u32[]{:S(2)}, u32[]{:S(2)}) collective-permute-start(bf16[144,256]{1,0:T(8,128)(2,1)S(1)} %collective-permute-done.2.refs_1_), channel_id=1, source_target_pairs={{0,8},{8,0},{16,24},{24,16},{1,9},{9,1},{17,25},{25,17},{2,10},{10... | collective-permute-start | bytes 221192 | tf_op jit(solution)/shard_map/ppermute | solution.py:396
  26.0 4.5 %collective-permute-start.5 = (bf16[144,256]{1,0:T(8,128)(2,1)S(1)}, bf16[144,256]{1,0:T(8,128)(2,1)S(1)}, u32[]{:S(2)}, u32[]{:S(2)}) collective-permute-start(bf16[144,256]{1,0:T(8,128)(2,1)S(1)} %collective-permute-done.2.refs_1_), channel_id=1, source_target_pairs={{0,2},{2,4},{4,6},{6,7},{7,5},{5,3},{3,1},{1,0},{8,10},{10,12},{12... | collective-permute-start | bytes 221192 | tf_op jit(solution)/shard_map/ppermute | solution.py:404
  30.5 4.7 %collective-permute-start.9 = (bf16[144,256]{1,0:T(8,128)(2,1)S(1)}, bf16[144,256]{1,0:T(8,128)(2,1)S(1)}, u32[]{:S(2)}, u32[]{:S(2)}) collective-permute-start(bf16[144,256]{1,0:T(8,128)(2,1)S(1)} %collective-permute-done.5.refs_2_), channel_id=1, source_target_pairs={{0,2},{2,4},{4,6},{6,7},{7,5},{5,3},{3,1},{1,0},{8,10},{10,12},{12... | collective-permute-start | bytes 221192 | tf_op jit(solution)/shard_map/ppermute | solution.py:404
  31.0 4.2 %collective-permute-start.12 = (bf16[144,256]{1,0:T(8,128)(2,1)S(1)}, bf16[144,256]{1,0:T(8,128)(2,1)S(1)}, u32[]{:S(2)}, u32[]{:S(2)}) collective-permute-start(bf16[144,256]{1,0:T(8,128)(2,1)S(1)} %collective-permute-done.6.refs_6_), channel_id=1, source_target_pairs={{0,8},{8,0},{16,24},{24,16},{1,9},{9,1},{17,25},{25,17},{2,10},{10... | collective-permute-start | bytes 221192 | tf_op jit(solution)/shard_map/ppermute | solution.py:396
  31.8 4.4 %collective-permute-start.10 = (bf16[144,256]{1,0:T(8,128)(2,1)S(1)}, bf16[144,256]{1,0:T(8,128)(2,1)S(1)}, u32[]{:S(2)}, u32[]{:S(2)}) collective-permute-start(bf16[144,256]{1,0:T(8,128)(2,1)S(1)} %collective-permute-done.6.refs_6_), channel_id=1, source_target_pairs={{0,1},{2,0},{4,2},{6,4},{7,6},{5,7},{3,5},{1,3},{8,9},{10,8},{12,1... | collective-permute-start | bytes 221192 | tf_op jit(solution)/shard_map/ppermute | solution.py:404
  36.6 4.4 %collective-permute-start.13 = (bf16[144,256]{1,0:T(8,128)(2,1)S(1)}, bf16[144,256]{1,0:T(8,128)(2,1)S(1)}, u32[]{:S(2)}, u32[]{:S(2)}) collective-permute-start(bf16[144,256]{1,0:T(8,128)(2,1)S(1)} %collective-permute-done.9.refs_3_), channel_id=1, source_target_pairs={{0,2},{2,4},{4,6},{6,7},{7,5},{5,3},{3,1},{1,0},{8,10},{10,12},{12... | collective-permute-start | bytes 221192 | tf_op jit(solution)/shard_map/ppermute | solution.py:404
  41.0 4.0 %collective-permute-start.19 = (bf16[1376,256]{1,0:T(8,128)(2,1)S(1)}, bf16[1376,256]{1,0:T(8,128)(2,1)S(1)}, u32[]{:S(2)}, u32[]{:S(2)}) collective-permute-start(bf16[1376,256]{1,0:T(8,128)(2,1)S(1)} %collective-permute-done.16.refs_2_), channel_id=1, source_target_pairs={{0,8},{8,0},{16,24},{24,16},{1,9},{9,1},{17,25},{25,17},{2,10},{10... | collective-permute-start | bytes 2113544 | tf_op jit(solution)/shard_map/ppermute | solution.py:396
  41.0 10.7 %collective-permute-start.21 = (bf16[688,256]{1,0:T(8,128)(2,1)S(1)}, bf16[688,256]{1,0:T(8,128)(2,1)S(1)}, u32[]{:S(2)}, u32[]{:S(2)}) collective-permute-start(bf16[688,256]{1,0:T(8,128)(2,1)S(1)} %get-tuple-element.87), channel_id=1, source_target_pairs={{0,16},{8,24},{16,0},{24,8},{1,17},{9,25},{17,1},{25,9},{2,18},{10... | collective-permute-start | bytes 1056776 | tf_op jit(solution)/shard_map/ppermute | solution.py:400
  41.5 1.7 %collective-permute-start.17 = (bf16[144,256]{1,0:T(8,128)(2,1)S(1)}, bf16[144,256]{1,0:T(8,128)(2,1)S(1)}, u32[]{:S(2)}, u32[]{:S(2)}) collective-permute-start(bf16[144,256]{1,0:T(8,128)(2,1)S(1)} %collective-permute-done.13.refs_4_), channel_id=1, source_target_pairs={{0,8},{8,0},{16,24},{24,16},{1,9},{9,1},{17,25},{25,17},{2,10},{10... | collective-permute-start | bytes 221192 | tf_op jit(solution)/shard_map/ppermute | solution.py:396
  41.8 3.2 %collective-permute-start.20 = (f32[1,128]{1,0:T(1,128)S(1)}, f32[1,128]{1,0:T(1,128)S(1)}, u32[]{:S(2)}, u32[]{:S(2)}) collective-permute-start(f32[1,128]{1,0:T(1,128)S(1)} %bitcast.11), channel_id=1, source_target_pairs={{0,8},{8,0},{16,24},{24,16},{1,9},{9,1},{17,25},{25,17},{2,10},{10... | collective-permute-start | bytes 1544 | tf_op jit(solution)/shard_map/ppermute | solution.py:396
  51.6 3.6 %collective-permute-start.22 = (f32[1,512]{1,0:T(1,128)S(1)}, f32[1,512]{1,0:T(1,128)S(1)}, u32[]{:S(2)}, u32[]{:S(2)}) collective-permute-start(f32[1,512]{1,0:T(1,128)S(1)} %get-tuple-element.88), channel_id=1, source_target_pairs={{0,16},{8,24},{16,0},{24,8},{1,17},{9,25},{17,1},{25,9},{2,18},{10... | collective-permute-start | bytes 6152 | tf_op jit(solution)/shard_map/ppermute | solution.py:400
  55.2 5.3 %collective-permute-start.25 = (bf16[688,256]{1,0:T(8,128)(2,1)S(1)}, bf16[688,256]{1,0:T(8,128)(2,1)S(1)}, u32[]{:S(2)}, u32[]{:S(2)}) collective-permute-start(bf16[688,256]{1,0:T(8,128)(2,1)S(1)} %collective-permute-done.21.refs_2_), channel_id=1, source_target_pairs={{0,8},{8,0},{16,24},{24,16},{1,9},{9,1},{17,25},{25,17},{2,10},{10... | collective-permute-start | bytes 1056776 | tf_op jit(solution)/shard_map/ppermute | solution.py:396
  55.2 10.6 %collective-permute-start.27 = (bf16[688,256]{1,0:T(8,128)(2,1)S(1)}, bf16[688,256]{1,0:T(8,128)(2,1)S(1)}, u32[]{:S(2)}, u32[]{:S(2)}) collective-permute-start(bf16[688,256]{1,0:T(8,128)(2,1)S(1)} %get-tuple-element.95), channel_id=1, source_target_pairs={{0,16},{8,24},{16,0},{24,8},{1,17},{9,25},{17,1},{25,9},{2,18},{10... | collective-permute-start | bytes 1056776 | tf_op jit(solution)/shard_map/ppermute | solution.py:400
  55.8 3.6 %collective-permute-start.23 = (f32[1,512]{1,0:T(1,128)S(1)}, f32[1,512]{1,0:T(1,128)S(1)}, u32[]{:S(2)}, u32[]{:S(2)}) collective-permute-start(f32[1,512]{1,0:T(1,128)S(1)} %add.25), channel_id=1, source_target_pairs={{0,1},{1,0},{2,3},{3,2},{4,5},{5,4},{6,7},{7,6},{8,9},{9,8},{10,11... | collective-permute-start | bytes 6152 | tf_op jit(solution)/shard_map/ppermute | solution.py:503
  59.4 4.7 %collective-permute-start.24 = (f32[1,512]{1,0:T(1,128)S(1)}, f32[1,512]{1,0:T(1,128)S(1)}, u32[]{:S(2)}, u32[]{:S(2)}) collective-permute-start(f32[1,512]{1,0:T(1,128)S(1)} %add.26), channel_id=1, source_target_pairs={{0,2},{1,3},{2,0},{3,1},{4,6},{5,7},{6,4},{7,5},{8,10},{9,11},{10,... | collective-permute-start | bytes 6152 | tf_op jit(solution)/shard_map/ppermute | solution.py:503
  65.9 5.3 %collective-permute-start.26 = (f32[1,512]{1,0:T(1,128)S(1)}, f32[1,512]{1,0:T(1,128)S(1)}, u32[]{:S(2)}, u32[]{:S(2)}) collective-permute-start(f32[1,512]{1,0:T(1,128)S(1)} %add.27), channel_id=1, source_target_pairs={{0,4},{1,5},{2,6},{3,7},{4,0},{5,1},{6,2},{7,3},{8,12},{9,13},{10,... | collective-permute-start | bytes 6152 | tf_op jit(solution)/shard_map/ppermute | solution.py:503
  (10 other events, 104.2 us)

commit v2 on v1

v2 whole, which is shorter than its diff:
```python
import functools

import jax
import jax.numpy as jnp
import numpy as np
from jax import lax
from jax.experimental import pallas as pl
from jax.experimental.pallas import tpu as pltpu
from jax.sharding import PartitionSpec as P

beta_two = 0.8
scale_alpha = 0.25
epsilon = 1e-30
CORES = 2
CHUNKS = 2
HALVES = 2
f32 = jnp.float32
bf16 = jnp.bfloat16
f8 = jnp.float8_e4m3fn
MIB = 1 << 20
CODE_TOP = 181.0
TOP_ROWS = 16
VMEM = pl.BlockSpec(memory_space=pltpu.VMEM)
SMEM = pl.BlockSpec(memory_space=pltpu.SMEM)


def split(value):
    high = value.astype(bf16)
    return high, (value - high.astype(f32)).astype(bf16)


def tile_of(size, most, unit):
    return max(t for t in range(unit, most + 1, unit) if size % t == 0)


def low_kernel(steps, n_col, here_ref, act_ref, basis_ref, mine_ref, other_ref, kept_ref, sem):
    depth = basis_ref.shape[0]
    tile = depth // steps
    half = mine_ref.shape[1]
    copies = []
    for n in range(steps):
        at = pl.ds(n * tile, tile)
        copies.append(pltpu.make_async_copy(basis_ref.at[at, :], kept_ref.at[at, :], sem.at[n]))
    for copy in copies:
        copy.start()
    total = None
    for n in range(steps):
        copies[n].wait()
        at = slice(n * tile, (n + 1) * tile)
        high, low = split(kept_ref[at, :])
        left = act_ref[:, at]
        one = jnp.dot(left, high, preferred_element_type=f32)
        one = one + jnp.dot(left, low, preferred_element_type=f32)
        total = one if total is None else total + one
    second = here_ref[0] // n_col % CORES == 1
    mine_ref[...] = jnp.where(second, total[:, half:], total[:, :half])
    other_ref[...] = jnp.where(second, total[:, :half], total[:, half:])


def low_partial(here, acts, basis, n_col):
    tokens, depth = acts.shape
    rank = basis.shape[1]
    steps = 8
    half = jax.ShapeDtypeStruct((tokens, rank // 2), f32)
    return pl.pallas_call(
        functools.partial(low_kernel, steps, n_col),
        out_shape=(half, half),
        grid_spec=pltpu.PrefetchScalarGridSpec(
            num_scalar_prefetch=1,
            grid=(1,),
            in_specs=[
                pl.BlockSpec((tokens, depth), lambda i, s: (0, 0)),
                pl.BlockSpec(memory_space=pl.ANY),
            ],
            out_specs=[VMEM] * 2,
            scratch_shapes=[
                pltpu.VMEM((depth, rank), f32),
                pltpu.SemaphoreType.DMA((steps,)),
            ],
        ),
        compiler_params=pltpu.CompilerParams(vmem_limit_bytes=60 * MIB),
        cost_estimate=pl.CostEstimate(
            flops=4 * tokens * depth * rank, bytes_accessed=6 * depth * rank, transcendentals=0
        ),
        name="low_partial",
    )(here, acts, basis)


def turn_kernel(basis_ref, high_ref, small_ref):
    rows, rank = basis_ref.shape
    tile = tile_of(rows, 256, 128)
    for begin in range(0, rows, tile):
        at = slice(begin, begin + tile)
        turned = basis_ref[at, :].T
        high = turned.astype(bf16)
        high_ref[:, at] = high
        small_ref[:rank, at] = ((turned - high.astype(f32)) * 2.0**20).astype(f8)
        small_ref[rank:, at] = (turned * 2.0**12).astype(f8)


def turn_basis(basis):
    rows, rank = basis.shape
    return pl.pallas_call(
        turn_kernel,
        out_shape=[
            jax.ShapeDtypeStruct((rank, rows), bf16),
            jax.ShapeDtypeStruct((2 * rank, rows), f8),
        ],
        in_specs=[VMEM],
        out_specs=[VMEM] * 2,
        compiler_params=pltpu.CompilerParams(vmem_limit_bytes=4 * MIB),
        cost_estimate=pl.CostEstimate(flops=0, bytes_accessed=8 * rows * rank, transcendentals=0),
        name="turn_basis",
    )(basis)


def encode_kernel(*refs):
    out_ref = refs[-1]
    tokens, lanes = refs[0].shape
    value = refs[0][...]
    for ref in refs[1:-1]:
        value = value + ref[...]
    size = jnp.abs(value)
    top = (jnp.max(size, axis=0, keepdims=True) * (1.0 + 2.0**-7)).astype(bf16).astype(f32)
    top = jnp.maximum(top, 1e-36)
    code = size * (CODE_TOP / top)
    for _ in range(4):
        code = code * code
    out_ref[:tokens, :] = jnp.where(value < 0, -code, code).astype(bf16)
    out_ref[tokens:, :] = jnp.broadcast_to(top, (TOP_ROWS, lanes)).astype(bf16)


def encode(*blocks):
    tokens, lanes = blocks[0].shape
    return pl.pallas_call(
        encode_kernel,
        out_shape=jax.ShapeDtypeStruct((tokens + TOP_ROWS, lanes), bf16),
        in_specs=[VMEM] * len(blocks),
        out_specs=VMEM,
        compiler_params=pltpu.CompilerParams(vmem_limit_bytes=4 * MIB),
        cost_estimate=pl.CostEstimate(
            flops=0, bytes_accessed=8 * tokens * lanes, transcendentals=0
        ),
        name="encode",
    )(*blocks)


def decode(ref):
    tokens = ref.shape[0] - TOP_ROWS
    code = ref[:tokens, :].astype(f32)
    size = jnp.abs(code)
    for _ in range(4):
        size = lax.rsqrt(size)
    size = size * (ref[tokens : tokens + 1, :].astype(f32) * (1.0 / CODE_TOP))
    return jnp.where(code < 0, -size, size)


def join_kernel(where_ref, mine_ref, other_ref, out_ref):
    half = mine_ref.shape[1]
    core = where_ref[0]
    out_ref[:, pl.ds(pl.multiple_of(core * half, half), half)] = mine_ref[...]
    out_ref[:, pl.ds(pl.multiple_of((1 - core) * half, half), half)] = other_ref[...]


def join(where, mine, other):
    rows, half = mine.shape
    return pl.pallas_call(
        join_kernel,
        out_shape=jax.ShapeDtypeStruct((rows, 2 * half), bf16),
        in_specs=[SMEM, VMEM, VMEM],
        out_specs=VMEM,
        compiler_params=pltpu.CompilerParams(vmem_limit_bytes=4 * MIB),
        cost_estimate=pl.CostEstimate(flops=0, bytes_accessed=8 * rows * half, transcendentals=0),
        name="join",
    )(where, mine, other)


def assemble_kernel(blocks, offset, where_ref, *refs):
    high_ref, low_ref = refs[blocks:]
    for b, ref in enumerate(refs[:blocks]):
        tokens = ref.shape[0] - TOP_ROWS
        rows = pl.ds(pl.multiple_of(where_ref[offset + b] * tokens, tokens), tokens)
        high_ref[rows, :], low_ref[rows, :] = split(decode(ref))


def assemble(where, found, offset):
    blocks = len(found)
    rows, rank = found[0].shape
    shape = (blocks * (rows - TOP_ROWS), rank)
    return pl.pallas_call(
        functools.partial(assemble_kernel, blocks, offset),
        out_shape=[jax.ShapeDtypeStruct(shape, bf16)] * 2,
        in_specs=[SMEM] + [VMEM] * blocks,
        out_specs=[VMEM] * 2,
        compiler_params=pltpu.CompilerParams(vmem_limit_bytes=4 * MIB),
        cost_estimate=pl.CostEstimate(flops=0, bytes_accessed=0, transcendentals=0),
        name="assemble",
    )(where, *found)


def cut_kernel(starts_at, counts, where_ref, grads_ref, *refs):
    outs, sem = refs[:-1], refs[-1]
    copies = []
    for n, out in enumerate(outs):
        rows = out.shape[0]
        at = pl.ds(pl.multiple_of(where_ref[starts_at + n] * 16, 16), rows)
        copies.append(pltpu.make_async_copy(grads_ref.at[at, :], out, sem.at[n]))
    for copy in copies:
        copy.start()
    for copy in copies:
        copy.wait()


def cut(where, grads, sizes, starts_at):
    return pl.pallas_call(
        functools.partial(cut_kernel, starts_at, len(sizes)),
        out_shape=[jax.ShapeDtypeStruct((size, grads.shape[1]), bf16) for size in sizes],
        in_specs=[SMEM, pl.BlockSpec(memory_space=pl.ANY)],
        out_specs=[VMEM] * len(sizes),
        scratch_shapes=[pltpu.SemaphoreType.DMA((len(sizes),))],
        compiler_params=pltpu.CompilerParams(vmem_limit_bytes=4 * MIB),
        cost_estimate=pl.CostEstimate(
            flops=0, bytes_accessed=4 * sum(sizes) * grads.shape[1], transcendentals=0
        ),
        name="cut",
    )(where, grads)


def project_kernel(
    pieces, skip, step, start_at, rows_at, first, where_ref, high_ref, low_ref, moment_ref,
    most_ref, *refs
):
    out_ref, colnext_ref, sums_ref, top_ref = refs[len(refs) - 4 :]
    grads, moments = refs[:pieces], refs[pieces : len(refs) - 4]
    rows, rank = out_ref.shape
    tokens = grads[0].shape[1]
    order = [
        pl.ds(pl.multiple_of(where_ref[rows_at + p] * tokens, tokens), tokens)
        for p in range(pieces)
    ]
    high = jnp.concatenate([high_ref[at, :] for at in order], axis=0)
    low = jnp.concatenate([low_ref[at, :] for at in order], axis=0)
    sums = jnp.zeros((1, rank), f32)
    if first:
        lanes = moments[0].shape[1]
        owner = lax.broadcasted_iota(jnp.int32, (1, rank), 1) // lanes
        for n, ref in enumerate(moments):
            wide = jnp.concatenate([ref[...]] * (rank // lanes), axis=1)
            sums = jnp.where(owner == where_ref[rows_at + n], wide, sums)
        sums = sums * jnp.where(where_ref[1] == 1, first, 0.0)
    top = most_ref[...]
    for begin in range(0, rows, step):
        at = pl.ds(pl.multiple_of(where_ref[start_at] * 16 + begin, 16), step)
        here = slice(begin, begin + step)
        there = slice(skip + begin, skip + begin + step)
        grad = jnp.concatenate(
            [g[at, :] for g in grads[:2]] + [g[there, :] for g in grads[2:]], axis=1
        )
        total = jnp.dot(grad, high, preferred_element_type=f32) + jnp.dot(
            grad, low, preferred_element_type=f32
        )
        squares = total * total
        sums = sums + jnp.sum(squares, axis=0, keepdims=True)
        quarter = sum(squares[:, n : n + 128] for n in range(0, rank, 128))
        col_next = beta_two * moment_ref[at, :] + (1.0 - beta_two) * (
            jnp.sum(quarter, axis=1, keepdims=True) / rank + epsilon
        )
        part = total * lax.rsqrt(col_next)
        top = jnp.maximum(top, jnp.max(jnp.abs(part), axis=0, keepdims=True))
        out_ref[here, :] = part
        long = colnext_ref.shape[1]
        wide = jnp.broadcast_to(col_next, (step, 128))
        if long > step:
            wide = jnp.concatenate([wide, jnp.zeros((long - step, 128), f32)], axis=0)
        colnext_ref[begin // step : begin // step + 1, :] = wide.T[:1, :]
    sums_ref[...] = sums
    top_ref[...] = top


def project(
    where, high, low, moment, most, grads, skip, moments, rows, step, start_at, rows_at, first
):
    tokens, rank = high.shape
    long = -(-step // 128) * 128
    return pl.pallas_call(
        functools.partial(
            project_kernel, len(grads), skip, step, start_at, rows_at, first
        ),
        out_shape=[
            jax.ShapeDtypeStruct((rows, rank), f32),
            jax.ShapeDtypeStruct((rows // step, long), f32),
            jax.ShapeDtypeStruct((1, rank), f32),
            jax.ShapeDtypeStruct((1, rank), f32),
        ],
        in_specs=[SMEM] + [VMEM] * (4 + len(grads) + len(moments)),
        out_specs=[VMEM] * 4,
        compiler_params=pltpu.CompilerParams(vmem_limit_bytes=16 * MIB),
        cost_estimate=pl.CostEstimate(flops=0, bytes_accessed=0, transcendentals=0),
        name="project",
    )(where, high, low, moment, most, *grads, *moments)


def segments(refs, part_refs, tile):
    found, done = [], 0
    for ref, part_ref in zip(refs, part_refs):
        rows = part_ref.shape[0]
        for row in range(0, rows, tile):
            size = min(tile, rows - row)
            found.append((done // tile, done % tile, size, ref, row))
            done += size
    return found


def update_kernel(
    count, parts, rows_at, order_at, where_ref, sums_ref, most_ref, high_ref, small_ref, *refs
):
    part_refs, col_refs = refs[:parts], refs[parts : 2 * parts]
    out_ref, rownext_ref, colnext_ref, lhs_ref, lhs_small_ref, scale_ref = refs[2 * parts :]
    tiles, tile, rank = lhs_ref.shape
    step = pl.program_id(0)

    @pl.when(step == 0)
    def _():
        row_next = (1.0 - beta_two) * (sums_ref[...] / count + epsilon)
        rows = rownext_ref.shape[1]
        held = jnp.zeros((1, rows), f32)
        for r in range(rank // rows):
            held = jnp.where(where_ref[rows_at] == r, row_next[:, r * rows : (r + 1) * rows], held)
        rownext_ref[...] = held
        scale = scale_alpha * lax.rsqrt(row_next) * jnp.sqrt(
            jnp.mean(row_next, axis=1, keepdims=True)
        )
        strip = colnext_ref.shape[1]
        for n, begin, size, ref, row in segments(col_refs, part_refs, tile):
            strip = pl.ds(where_ref[order_at + n], 1)
            colnext_ref[strip, begin : begin + size] = ref[row // tile : row // tile + 1, :size]
        top = jnp.maximum(jnp.max(scale * most_ref[...], axis=1, keepdims=True), 1e-30)
        scale_ref[0:1, :] = scale
        scale_ref[1:2, :] = jnp.broadcast_to(2.0**7 / top, (1, rank))
        scale_ref[2:3, :] = jnp.broadcast_to(top * 2.0**-27, (1, rank))

    for number in range(tiles):

        @pl.when(step == number)
        def _():
            for n, begin, size, ref, row in segments(part_refs, part_refs, tile):
                if n != number:
                    continue
                value = ref[row : row + size, :] * scale_ref[0:1, :]
                high = value.astype(bf16)
                grow = scale_ref[1:2, :]
                at = slice(begin, begin + size)
                lhs_ref[number, at, :] = high
                lhs_small_ref[number, at, :rank] = (value * grow).astype(f8)
                lhs_small_ref[number, at, rank:] = (
                    (value - high.astype(f32)) * (grow * 2.0**8)
                ).astype(f8)

    now = step % tiles
    lanes = pl.ds(pl.multiple_of(step // tiles * out_ref.shape[1], 128), out_ref.shape[1])
    out_ref[...] = jnp.dot(
        lhs_ref[now], high_ref[:, lanes], preferred_element_type=f32
    ) + scale_ref[2:3, 0:1] * jnp.dot(
        lhs_small_ref[now], small_ref[:, lanes], preferred_element_type=f32
    )


def update(where, sums, most, high, small, parts, cols, strip, hidden, n_row, rows_at, order_at):
    rank, rows = high.shape
    columns = sum(part.shape[0] for part in parts)
    tiles = columns // strip
    wide = rows // HALVES
    return pl.pallas_call(
        functools.partial(update_kernel, float(hidden), len(parts), rows_at, order_at),
        out_shape=[
            jax.ShapeDtypeStruct((columns, rows), f32),
            jax.ShapeDtypeStruct((1, rank // n_row), f32),
            jax.ShapeDtypeStruct((tiles, strip), f32),
        ],
        grid_spec=pltpu.PrefetchScalarGridSpec(
            num_scalar_prefetch=1,
            grid=(tiles * HALVES,),
            in_specs=[VMEM] * (4 + 2 * len(parts)),
            out_specs=[
                pl.BlockSpec((strip, wide), lambda i, s: (s[order_at + i % tiles], i // tiles)),
                pl.BlockSpec((1, rank // n_row), lambda i, s: (0, 0)),
                pl.BlockSpec((tiles, strip), lambda i, s: (0, 0)),
            ],
            scratch_shapes=[
                pltpu.VMEM((tiles, strip, rank), bf16),
                pltpu.VMEM((tiles, strip, 2 * rank), f8),
                pltpu.VMEM((8, rank), f32),
            ],
        ),
        compiler_params=pltpu.CompilerParams(vmem_limit_bytes=28 * MIB),
        cost_estimate=pl.CostEstimate(
            flops=4 * columns * rank * rows, bytes_accessed=4 * columns * rows, transcendentals=0
        ),
        name="update",
    )(where, sums, most, high, small, *parts, *cols)


def per_device(n_row, n_col, activations, out_grads, basis, row_moment, col_moment):
    chips = n_row // CORES
    columns = col_moment.shape[0]
    hidden = columns * n_col
    rank = basis.shape[1]
    width = -(-columns // (32 * chips)) * 32
    pad = width * chips - columns
    rows = width // CHUNKS
    ring = [0, 2, 4, 6, 7, 5, 3, 1] if n_col == 8 else list(range(n_col))
    hops = n_col // 2
    jobs, moves = [(0, 0, width, 0, 0)], [(0, 0, width)]
    for j in range(1, chips):
        for q in range(CHUNKS):
            at, part = q * rows, rows * (3 - q) // 5 // 128 * 128
            if j > 1 or part == 0:
                jobs.append((j, at, rows, len(moves), 0))
                moves.append((j, at, rows))
                continue
            jobs.append((j, at, part, len(moves), 0))
            if q == 0:
                jobs.append((j, at + part, rows - part, len(moves), part))
                moves.append((j, at, rows))
            else:
                jobs.append((j, at + part, rows - part, len(moves) + 1, 0))
                moves += [(j, at, part), (j, at + part, rows - part)]

    def to_sibling(value):
        return lax.ppermute(value, "row", [(r, r ^ 1) for r in range(n_row)])

    def to_chip(value, shift):
        pairs = [(r, (r + CORES * shift) % n_row) for r in range(n_row)]
        return lax.ppermute(value, "row", pairs)

    def around(value):
        pairs = [
            (r * n_col + ring[i], r * n_col + ring[(i + 1 - r % CORES * 2) % n_col])
            for r in range(n_row) for i in range(n_col)
        ]
        return lax.ppermute(value, ("row", "col"), pairs)

    def after(value, *others):
        return lax.optimization_barrier((value, others))[0]

    table = []
    for r in range(n_row):
        for c in range(n_col):
            p, x, k = ring.index(c), r // CORES, r % CORES
            entry = [k, int(c == 0), r, r ^ 1]
            for s in range(1, chips):
                there = (x - s) % chips
                entry += [CORES * there + k, CORES * there + 1 - k]
            way = 1 - 2 * k
            order = [p] + [p - way * s for s in range(1, hops + 1)]
            order += [p + way * s for s in range(1, hops + 1) if 2 * s != n_col]
            blocks_at = len(entry)
            entry += [ring[i % n_col] for i in order]
            starts_at = len(entry)
            entry += [((x + j) % chips * width + at) // 16 for j, at, *_ in jobs]
            sends_at = len(entry)
            entry += [
                ((x + s + j) % chips * width + at) // 16
                for j, at, _ in moves for s in range(1, chips)
            ]
            order_at = len(entry)
            entry += [(x + j) % chips * CHUNKS + q for j in range(chips) for q in range(CHUNKS)]
            table.append(entry)
    flat = lax.axis_index("row") * n_col + lax.axis_index("col")
    here = flat.astype(jnp.int32)[None]
    rows_at = 2

    mine, other = low_partial(here, activations, basis, n_col)
    table = np.array(table, np.int32)
    flat = after(flat.astype(jnp.uint32), other)
    where = lax.dynamic_slice(table, (flat, jnp.uint32(0)), (1, table.shape[1]))[0]
    mine = mine + to_sibling(other)
    arrived = [to_chip(mine, s) for s in range(1, chips)]

    grads = out_grads.T
    moment = after(col_moment, mine)[:, None]
    if pad:
        grads = jnp.pad(grads, ((0, pad), (0, 0)))
        moment = jnp.pad(moment, ((0, pad), (0, 0)), constant_values=1.0)
    grads = after(grads, other)
    sends = cut(where, grads, [size for _, _, size in moves for _ in range(1, chips)], sends_at)
    arrived = lax.optimization_barrier((*arrived, *sends))
    sends, arrived = arrived[chips - 1 :], arrived[: chips - 1]
    sends = [sends[n * (chips - 1) : (n + 1) * (chips - 1)] for n in range(len(moves))]
    mine = encode(mine, *arrived)
    moments = after(row_moment, mine)[None]
    moments = [moments, to_sibling(moments)]

    def exchange(send, *others):
        return [to_chip(after(value, *others), s) for s, value in enumerate(sends[send], 1)]

    def pass_on(got, *others):
        got = [after(value, *others) for value in got]
        return [both for value in got for both in (value, to_sibling(value))]

    got = {0: exchange(0, mine)}
    held = join(where, mine, to_sibling(mine))
    sibling = to_sibling(after(grads, held))
    blocks, siblings = [held], []
    for hop in range(1, hops + 1):
        moving = [around(held)]
        if hop > 1:
            moving.append(to_sibling(held))
        if hop == 2:
            turned = turn_basis(after(basis, held))
            moving += turned
        if hop == max(hops - 1, 1):
            moving += got[0]
        moved = lax.optimization_barrier(tuple(moving))
        held = moved[0]
        blocks.append(held)
        siblings += moved[1:2] if hop > 1 else []
        if hop == max(hops - 1, 1):
            passed = {0: pass_on(got[0], held)}
            for move in (1, 2):
                got[move] = exchange(move, held)
    if 2 * hops != n_col:
        siblings.append(to_sibling(held))
    high, low = assemble(where, blocks + siblings, blocks_at)

    found = []

    def project_job(job, most):
        _, _, size, move, skip = jobs[job]
        part, col_next, sums, top = project(
            where, high, low, moment, most, [grads, sibling] + passed[move], skip,
            [] if job else moments, size, min(size, rows), starts_at + job, rows_at,
            0.0 if job else hidden * beta_two / (1.0 - beta_two),
        )
        found.append((part, col_next))
        return sums, top

    sums, top = project_job(0, jnp.zeros((1, rank), f32))
    sums = after(sums, *got[1], *got[2])
    passed[1] = pass_on(got[1], sums)
    hop, step = 0, 1
    while step < n_col:
        if hop == 0:
            arrived = [to_chip(sums, s) for s in range(1, chips)]
        else:
            arrived = [lax.ppermute(sums, "col", [(c, c ^ step) for c in range(n_col)])]
            step *= 2
        hop += 1
        if hop < len(jobs) and jobs[hop][3] in passed:
            _, top = project_job(hop, top)
            *arrived, top = lax.optimization_barrier((*arrived, top))
        sums = sum(arrived, sums)
        if hop == 1:
            passed[2] = pass_on(got[2], sums)
            for move in range(3, len(moves)):
                got[move] = exchange(move, sums)
        if hop == 3:
            for move in range(3, len(moves)):
                passed[move] = pass_on(got[move], sums)
    for job in range(len(found), len(jobs)):
        _, top = project_job(job, top)

    updated, row_next, col_next = update(
        where, sums, top, *turned, [part for part, _ in found], [col for _, col in found],
        rows, hidden, n_row, rows_at, order_at,
    )
    return (updated[:columns].T, row_next[0], col_next.reshape(-1)[:columns])


def solution(mesh):
    in_specs = (P("col", "row"), P("row", "col"), P("row", None), P("row"), P("col"))
    out_specs = (P("row", "col"), P("row"), P("col"))
    return jax.shard_map(
        functools.partial(per_device, mesh.shape["row"], mesh.shape["col"]),
        mesh=mesh, in_specs=in_specs, out_specs=out_specs, check_vma=False,
    )
```

time: 90.5 us -> 83.3 us (0.920)
  waiting for transfers between devices: 26.5 us -> 14.4 us
  starting transfers between devices: 19.7 us -> 22.4 us
  local copies, waits for them, and re-layouts: 2.33 us -> 3.99 us
    ppermute x5 -> x6, waiting for transfers between devices: 9.44 us -> 1.94 us  [to_chip(): return lax.ppermute(value, 'row', pairs)]
    ppermute x10 -> x7, waiting for transfers between devices: 13.2 us -> 10.6 us  [the longest x4 10.4 us: around(): return lax.ppermute(value, ('row', 'col'), pairs)]
    ppermute x5 -> x6, starting transfers between devices: 6.39 us -> 8.64 us  [to_chip(): return lax.ppermute(value, 'row', pairs)]
    unnamed x10 -> x8, local copies, waits for them, and re-layouts: 0.02 us -> 2.2 us
    ppermute x14 -> x11, waiting for transfers between devices: 3.88 us -> 1.85 us  [to_sibling(): return lax.ppermute(value, 'row', [(r, r ^ 1) for r in range(n_row)])]
    ppermute x10 -> x7, starting transfers between devices: 10.8 us -> 12 us  [the longest x4 6.27 us: around(): return lax.ppermute(value, ('row', 'col'), pairs)]
    pallas_call x4 -> x7, Pallas kernels: 16.6 us -> 17.7 us  [the longest x5 12.9 us: project(): pl.pallas_call(functools.partial(project_kernel, len(grads), skip, step,...]
    pallas_call x1, Pallas kernels: 2.1 us -> 1.16 us  [turn_basis(): pl.pallas_call(turn_kernel, out_shape=[jax.ShapeDtypeStruct((rank, rows),...]
  transfers between devices with their start and end apart: 29 -> 24, of which waited for: 19 -> 11; matrix products, arithmetic and copies ran while one was open for 0% -> 1% of each run, Pallas kernels for 19% -> 21%
where the time goes in v2:
time: 83.3 us; the launch traced here: 83.1 us
  Pallas kernels  40.6 us (49%)
  starting transfers between devices  22.4 us (27%)
  waiting for transfers between devices  14.4 us (17%)
  local copies, waits for them, and re-layouts  3.99 us (5%)
  other arithmetic  0.94 us (1%)
    pallas_call x1, Pallas kernels, update(): pl.pallas_call(functools.partial(update_kernel, float(hidden), len(parts)...  18.4 us
    pallas_call x5, Pallas kernels, project(): pl.pallas_call(functools.partial(project_kernel, len(grads), skip, step,...  12.9 us
    ppermute x4, waiting for transfers between devices, around(): return lax.ppermute(value, ('row', 'col'), pairs)  10.4 us
    ppermute x6, starting transfers between devices, to_chip(): return lax.ppermute(value, 'row', pairs)  8.64 us
    ppermute x4, starting transfers between devices, around(): return lax.ppermute(value, ('row', 'col'), pairs)  6.27 us
    ppermute x3, starting transfers between devices, per_device(): arrived = [lax.ppermute(sums, 'col', [(c, c ^ step) for c in range(n_col)])]  5.75 us
    pallas_call x1, Pallas kernels, low_partial(): pl.pallas_call(functools.partial(low_kernel, steps, n_col), out_shape=(ha...  4.31 us
    unnamed x8, local copies, waits for them, and re-layouts  2.2 us
  transfers between devices with their start and end apart: 24, of which 11 were waited for; matrix products, arithmetic and copies ran while one was open for 1% of the time, Pallas kernels for 21%

profile of v2, /device:TPU:0, one launch (start us, length us, event | category | flops | bytes accessed | tf_op | source)
XLA Modules:
  0.0 83.1 jit_solution(16332707920481789907)
XLA Ops:
  0.6 4.3 %low_partial.1 = (f32[128,256]{1,0:T(8,128)}, f32[128,256]{1,0:T(8,128)}) custom-call(s32[1]{0:T(128)} %bitcast.here_ref, bf16[128,2048]{1,0:T(8,128)(2,1)} %act_ref.1, f32[2048,512]{1,0:T(8,128)} %basis_ref.2), custom_call_target="tpu_custom_call" | custom-call | flops 536870912 | bytes 6291456 | tf_op jit(solution)/shard_map/low_partial/pallas_call | solution.py:65
  7.6 2.9 %collective-permute-start.1 = (f32[128,256]{1,0:T(8,128)S(1)}, f32[128,256]{1,0:T(8,128)S(1)}, u32[]{:S(2)}, u32[]{:S(2)}) collective-permute-start(f32[128,256]{1,0:T(8,128)S(1)} %add.19.refs_0_), channel_id=1, source_target_pairs={{0,16},{8,24},{16,0},{24,8},{1,17},{9,25},{17,1},{25,9},{2,18},{10... | collective-permute-start | bytes 393224 | tf_op jit(solution)/shard_map/ppermute | solution.py:434
  11.2 1.4 %cut.1 = (bf16[1376,256]{1,0:T(8,128)(2,1)S(1)}, bf16[688,256]{1,0:T(8,128)(2,1)S(1)}, bf16[256,256]{1,0:T(8,128)(2,1)S(1)}, bf16[432,256]{1,0:T(8,128)(2,1)S(1)}) custom-call(s32[27]{0:T(128)S(1)} %dynamic-slice_bitcast_fusion.where_ref, bf16[2752,256]{1,0:T(8,128)(2,1)S(1)} %bitcast.7), custom_call_target="tpu_custom_call" | custom-call | bytes 2818048 | tf_op jit(solution)/shard_map/cut/pallas_call | solution.py:215
  12.7 1.7 %collective-permute-done.1.refs_1_ = f32[128,256]{1,0:T(8,128)S(1)} collective-permute-done((f32[128,256]{1,0:T(8,128)S(1)}, f32[128,256]{1,0:T(8,128)S(1)}, u32[]{:S(2)}, u32[]{:S(2)}) %collective-permute-start.1) | collective-permute-done | bytes 131104 | tf_op jit(solution)/shard_map/ppermute | solution.py:434
  14.5 1.8 %collective-permute-start.8 = (bf16[1376,256]{1,0:T(8,128)(2,1)S(1)}, bf16[1376,256]{1,0:T(8,128)(2,1)S(1)}, u32[]{:S(2)}, u32[]{:S(2)}) collective-permute-start(bf16[1376,256]{1,0:T(8,128)(2,1)S(1)} %get-tuple-element.80), channel_id=1, source_target_pairs={{0,16},{8,24},{16,0},{24,8},{1,17},{9,25},{17,1},{25,9},{2,18},{10... | collective-permute-start | bytes 2113544 | tf_op jit(solution)/shard_map/ppermute | solution.py:434
  17.1 1.6 %collective-permute-start.3 = (bf16[144,512]{1,0:T(8,128)(2,1)S(1)}, bf16[144,512]{1,0:T(8,128)(2,1)S(1)}, u32[]{:S(2)}, u32[]{:S(2)}) collective-permute-start(bf16[144,512]{1,0:T(8,128)(2,1)S(1)} %join.1.refs_0_), channel_id=1, source_target_pairs={{0,2},{2,4},{4,6},{6,7},{7,5},{5,3},{3,1},{1,0},{8,9},{10,8},{12,1... | collective-permute-start | bytes 442376 | tf_op jit(solution)/shard_map/ppermute | solution.py:441
  18.7 3.6 %collective-permute-done.3.refs_1_ = bf16[144,512]{1,0:T(8,128)(2,1)S(1)} collective-permute-done((bf16[144,512]{1,0:T(8,128)(2,1)S(1)}, bf16[144,512]{1,0:T(8,128)(2,1)S(1)}, u32[]{:S(2)}, u32[]{:S(2)}) %collective-permute-start.3) | collective-permute-done | bytes 147488 | tf_op jit(solution)/shard_map/ppermute | solution.py:441
  22.2 1.6 %collective-permute-start.4 = (bf16[144,512]{1,0:T(8,128)(2,1)S(1)}, bf16[144,512]{1,0:T(8,128)(2,1)S(1)}, u32[]{:S(2)}, u32[]{:S(2)}) collective-permute-start(bf16[144,512]{1,0:T(8,128)(2,1)S(1)} %collective-permute-done.3.refs_1_), channel_id=1, source_target_pairs={{0,2},{2,4},{4,6},{6,7},{7,5},{5,3},{3,1},{1,0},{8,9},{10,8},{12,1... | collective-permute-start | bytes 442376 | tf_op jit(solution)/shard_map/ppermute | solution.py:441
  23.8 2.2 %copy-done.1 = f32[2048,512]{1,0:T(8,128)S(1)} copy-done((f32[2048,512]{1,0:T(8,128)S(1)}, f32[2048,512]{1,0:T(8,128)}, u32[]{:S(2)}) %copy-start.1) | copy-done | bytes 4194328
  27.4 1.5 %collective-permute-start.6 = (bf16[144,512]{1,0:T(8,128)(2,1)S(1)}, bf16[144,512]{1,0:T(8,128)(2,1)S(1)}, u32[]{:S(2)}, u32[]{:S(2)}) collective-permute-start(bf16[144,512]{1,0:T(8,128)(2,1)S(1)} %collective-permute-done.4.refs_2_), channel_id=1, source_target_pairs={{0,2},{2,4},{4,6},{6,7},{7,5},{5,3},{3,1},{1,0},{8,9},{10,8},{12,1... | collective-permute-start | bytes 442376 | tf_op jit(solution)/shard_map/ppermute | solution.py:441
  29.0 3.6 %collective-permute-done.6.refs_3_ = bf16[144,512]{1,0:T(8,128)(2,1)S(1)} collective-permute-done((bf16[144,512]{1,0:T(8,128)(2,1)S(1)}, bf16[144,512]{1,0:T(8,128)(2,1)S(1)}, u32[]{:S(2)}, u32[]{:S(2)}) %collective-permute-start.6) | collective-permute-done | bytes 147488 | tf_op jit(solution)/shard_map/ppermute | solution.py:441
  32.7 1.7 %collective-permute-start.14 = (bf16[688,256]{1,0:T(8,128)(2,1)S(1)}, bf16[688,256]{1,0:T(8,128)(2,1)S(1)}, u32[]{:S(2)}, u32[]{:S(2)}) collective-permute-start(bf16[688,256]{1,0:T(8,128)(2,1)S(1)} %get-tuple-element.94), channel_id=1, source_target_pairs={{0,16},{8,24},{16,0},{24,8},{1,17},{9,25},{17,1},{25,9},{2,18},{10... | collective-permute-start | bytes 1056776 | tf_op jit(solution)/shard_map/ppermute | solution.py:434
  34.7 1.6 %collective-permute-start.9 = (bf16[144,512]{1,0:T(8,128)(2,1)S(1)}, bf16[144,512]{1,0:T(8,128)(2,1)S(1)}, u32[]{:S(2)}, u32[]{:S(2)}) collective-permute-start(bf16[144,512]{1,0:T(8,128)(2,1)S(1)} %collective-permute-done.6.refs_3_), channel_id=1, source_target_pairs={{0,2},{2,4},{4,6},{6,7},{7,5},{5,3},{3,1},{1,0},{8,9},{10,8},{12,1... | collective-permute-start | bytes 442376 | tf_op jit(solution)/shard_map/ppermute | solution.py:441
  36.8 3.0 %collective-permute-done.9.refs_4_ = bf16[144,512]{1,0:T(8,128)(2,1)S(1)} collective-permute-done((bf16[144,512]{1,0:T(8,128)(2,1)S(1)}, bf16[144,512]{1,0:T(8,128)(2,1)S(1)}, u32[]{:S(2)}, u32[]{:S(2)}) %collective-permute-start.9) | collective-permute-done | bytes 147488 | tf_op jit(solution)/shard_map/ppermute | solution.py:441
  40.2 1.7 %assemble.1 = (bf16[1024,512]{1,0:T(8,128)(2,1)S(1)}, bf16[1024,512]{1,0:T(8,128)(2,1)S(1)}) custom-call(s32[27]{0:T(128)S(1)} %dynamic-slice_bitcast_fusion.where_ref, bf16[144,512]{1,0:T(8,128)(2,1)S(1)} %join.1.refs_0_, bf16[144,512]{1,0:T(8,128)(2,1)S(1)} %collective-permute-done.3.refs_1_, bf16[144,512]{1,0:T(8,128)(2,1)S(1)} %collective-permute-done.4.refs_2_, ...), custom_call_target="tpu_custom_call" | custom-call | tf_op jit(solution)/shard_map/assemble/pallas_call | solution.py:190
  42.0 4.7 %project.5 = (f32[1376,512]{1,0:T(8,128)S(1)}, f32[2,768]{1,0:T(2,128)S(1)}, f32[1,512]{1,0:T(1,128)S(1)}, f32[1,512]{1,0:T(1,128)S(1)}) custom-call(s32[27]{0:T(128)S(1)} %dynamic-slice_bitcast_fusion.where_ref, bf16[1024,512]{1,0:T(8,128)(2,1)S(1)} %get-tuple-element.86.high_ref, bf16[1024,512]{1,0:T(8,128)(2,1)S(1)} %get-tuple-element.87.low_ref, ...), custom_call_target="tpu_custom_call" | custom-call | tf_op jit(solution)/shard_map/project/pallas_call | solution.py:285
  48.5 2.1 %project.6 = (f32[384,512]{1,0:T(8,128)S(1)}, f32[1,384]{1,0:T(1,128)S(1)}, f32[1,512]{1,0:T(1,128)}, f32[1,512]{1,0:T(1,128)S(1)}) custom-call(s32[27]{0:T(128)S(1)} %dynamic-slice_bitcast_fusion.where_ref, bf16[1024,512]{1,0:T(8,128)(2,1)S(1)} %get-tuple-element.86.high_ref, bf16[1024,512]{1,0:T(8,128)(2,1)S(1)} %get-tuple-element.87.low_ref, ...), custom_call_target="tpu_custom_call" | custom-call | tf_op jit(solution)/shard_map/project/pallas_call | solution.py:285
  51.8 1.5 %collective-permute-start.18 = (f32[1,512]{1,0:T(1,128)S(1)}, f32[1,512]{1,0:T(1,128)S(1)}, u32[]{:S(2)}, u32[]{:S(2)}) collective-permute-start(f32[1,512]{1,0:T(1,128)S(1)} %add.20), channel_id=1, source_target_pairs={{0,1},{1,0},{2,3},{3,2},{4,5},{5,4},{6,7},{7,6},{8,9},{9,8},{10,11... | collective-permute-start | bytes 6152 | tf_op jit(solution)/shard_map/ppermute | solution.py:546
  53.3 2.0 %project.7 = (f32[304,512]{1,0:T(8,128)S(1)}, f32[1,384]{1,0:T(1,128)S(1)}, f32[1,512]{1,0:T(1,128)}, f32[1,512]{1,0:T(1,128)S(1)}) custom-call(s32[27]{0:T(128)S(1)} %dynamic-slice_bitcast_fusion.where_ref, bf16[1024,512]{1,0:T(8,128)(2,1)S(1)} %get-tuple-element.86.high_ref, bf16[1024,512]{1,0:T(8,128)(2,1)S(1)} %get-tuple-element.87.low_ref, ...), custom_call_target="tpu_custom_call" | custom-call | tf_op jit(solution)/shard_map/project/pallas_call | solution.py:285
  55.4 1.6 %collective-permute-start.19 = (f32[1,512]{1,0:T(1,128)S(1)}, f32[1,512]{1,0:T(1,128)S(1)}, u32[]{:S(2)}, u32[]{:S(2)}) collective-permute-start(f32[1,512]{1,0:T(1,128)S(1)} %add.21), channel_id=1, source_target_pairs={{0,2},{1,3},{2,0},{3,1},{4,6},{5,7},{6,4},{7,5},{8,10},{9,11},{10,... | collective-permute-start | bytes 6152 | tf_op jit(solution)/shard_map/ppermute | solution.py:546
  57.0 1.9 %project.8 = (f32[256,512]{1,0:T(8,128)S(1)}, f32[1,256]{1,0:T(1,128)S(1)}, f32[1,512]{1,0:T(1,128)}, f32[1,512]{1,0:T(1,128)S(1)}) custom-call(s32[27]{0:T(128)S(1)} %dynamic-slice_bitcast_fusion.where_ref, bf16[1024,512]{1,0:T(8,128)(2,1)S(1)} %get-tuple-element.86.high_ref, bf16[1024,512]{1,0:T(8,128)(2,1)S(1)} %get-tuple-element.87.low_ref, ...), custom_call_target="tpu_custom_call" | custom-call | tf_op jit(solution)/shard_map/project/pallas_call | solution.py:285
  59.1 2.7 %collective-permute-start.21 = (f32[1,512]{1,0:T(1,128)S(1)}, f32[1,512]{1,0:T(1,128)S(1)}, u32[]{:S(2)}, u32[]{:S(2)}) collective-permute-start(f32[1,512]{1,0:T(1,128)S(1)} %add.22), channel_id=1, source_target_pairs={{0,4},{1,5},{2,6},{3,7},{4,0},{5,1},{6,2},{7,3},{8,12},{9,13},{10,... | collective-permute-start | bytes 6152 | tf_op jit(solution)/shard_map/ppermute | solution.py:546
  61.7 2.2 %project.9 = (f32[432,512]{1,0:T(8,128)S(1)}, f32[1,512]{1,0:T(1,128)S(1)}, f32[1,512]{1,0:T(1,128)}, f32[1,512]{1,0:T(1,128)S(1)}) custom-call(s32[27]{0:T(128)S(1)} %dynamic-slice_bitcast_fusion.where_ref, bf16[1024,512]{1,0:T(8,128)(2,1)S(1)} %get-tuple-element.86.high_ref, bf16[1024,512]{1,0:T(8,128)(2,1)S(1)} %get-tuple-element.87.low_ref, ...), custom_call_target="tpu_custom_call" | custom-call | tf_op jit(solution)/shard_map/project/pallas_call | solution.py:285
  64.0 18.4 %update.1 = (f32[2752,2048]{1,0:T(8,128)}, f32[1,128]{1,0:T(1,128)}, f32[4,688]{1,0:T(4,128)S(1)}) custom-call(s32[27]{0:T(128)S(1)} %dynamic-slice_bitcast_fusion.where_ref, f32[1,512]{1,0:T(1,128)S(1)} %add.23.sums_ref, f32[1,512]{1,0:T(1,128)S(1)} %get-tuple-element.115.most_ref, bf16[512,2048]{1,0:T(8,128)(2,1)S(1)} %get-tuple-element.76.high_ref, ...), custom_call_target="tpu_custom_call" | custom-call | flops 11542724608 | bytes 22544384 | tf_op jit(solution)/shard_map/update/pallas_call | solution.py:373
  (53 shorter events, 11.0 us)
Async XLA Ops:
  5.0 1.7 %collective-permute-start = (f32[128,256]{1,0:T(8,128)}, f32[128,256]{1,0:T(8,128)S(1)}, u32[]{:S(2)}, u32[]{:S(2)}) collective-permute-start(f32[128,256]{1,0:T(8,128)} %get-tuple-element.66), channel_id=1, source_target_pairs={{0,8},{8,0},{16,24},{24,16},{1,9},{9,1},{17,25},{25,17},{2,10},{10... | collective-permute-start | bytes 393224 | tf_op jit(solution)/shard_map/ppermute | solution.py:430
  7.6 6.7 %collective-permute-start.1 = (f32[128,256]{1,0:T(8,128)S(1)}, f32[128,256]{1,0:T(8,128)S(1)}, u32[]{:S(2)}, u32[]{:S(2)}) collective-permute-start(f32[128,256]{1,0:T(8,128)S(1)} %add.19.refs_0_), channel_id=1, source_target_pairs={{0,16},{8,24},{16,0},{24,8},{1,17},{9,25},{17,1},{25,9},{2,18},{10... | collective-permute-start | bytes 393224 | tf_op jit(solution)/shard_map/ppermute | solution.py:434
  14.4 1.9 %collective-permute-start.2 = (bf16[144,256]{1,0:T(8,128)(2,1)S(1)}, bf16[144,256]{1,0:T(8,128)(2,1)S(1)}, u32[]{:S(2)}, u32[]{:S(2)}) collective-permute-start(bf16[144,256]{1,0:T(8,128)(2,1)S(1)} %encode.1.mine_ref), channel_id=1, source_target_pairs={{0,8},{8,0},{16,24},{24,16},{1,9},{9,1},{17,25},{25,17},{2,10},{10... | collective-permute-start | bytes 221192 | tf_op jit(solution)/shard_map/ppermute | solution.py:430
  14.5 18.2 %collective-permute-start.8 = (bf16[1376,256]{1,0:T(8,128)(2,1)S(1)}, bf16[1376,256]{1,0:T(8,128)(2,1)S(1)}, u32[]{:S(2)}, u32[]{:S(2)}) collective-permute-start(bf16[1376,256]{1,0:T(8,128)(2,1)S(1)} %get-tuple-element.80), channel_id=1, source_target_pairs={{0,16},{8,24},{16,0},{24,8},{1,17},{9,25},{17,1},{25,9},{2,18},{10... | collective-permute-start | bytes 2113544 | tf_op jit(solution)/shard_map/ppermute | solution.py:434
  16.9 25.1 %collective-permute-start.11 = (bf16[2752,256]{1,0:T(8,128)(2,1)S(1)}, bf16[2752,256]{1,0:T(8,128)(2,1)S(1)}, u32[]{:S(2)}, u32[]{:S(2)}) collective-permute-start(bf16[2752,256]{1,0:T(8,128)(2,1)S(1)} %bitcast.8), channel_id=1, source_target_pairs={{0,8},{8,0},{16,24},{24,16},{1,9},{9,1},{17,25},{25,17},{2,10},{10... | collective-permute-start | bytes 4227080 | tf_op jit(solution)/shard_map/ppermute | solution.py:430
  17.1 5.1 %collective-permute-start.3 = (bf16[144,512]{1,0:T(8,128)(2,1)S(1)}, bf16[144,512]{1,0:T(8,128)(2,1)S(1)}, u32[]{:S(2)}, u32[]{:S(2)}) collective-permute-start(bf16[144,512]{1,0:T(8,128)(2,1)S(1)} %join.1.refs_0_), channel_id=1, source_target_pairs={{0,2},{2,4},{4,6},{6,7},{7,5},{5,3},{3,1},{1,0},{8,9},{10,8},{12,1... | collective-permute-start | bytes 442376 | tf_op jit(solution)/shard_map/ppermute | solution.py:441
  22.2 4.9 %collective-permute-start.5 = (bf16[144,512]{1,0:T(8,128)(2,1)S(1)}, bf16[144,512]{1,0:T(8,128)(2,1)S(1)}, u32[]{:S(2)}, u32[]{:S(2)}) collective-permute-start(bf16[144,512]{1,0:T(8,128)(2,1)S(1)} %collective-permute-done.3.refs_1_), channel_id=1, source_target_pairs={{0,8},{8,0},{16,24},{24,16},{1,9},{9,1},{17,25},{25,17},{2,10},{10... | collective-permute-start | bytes 442376 | tf_op jit(solution)/shard_map/ppermute | solution.py:430
  22.2 5.1 %collective-permute-start.4 = (bf16[144,512]{1,0:T(8,128)(2,1)S(1)}, bf16[144,512]{1,0:T(8,128)(2,1)S(1)}, u32[]{:S(2)}, u32[]{:S(2)}) collective-permute-start(bf16[144,512]{1,0:T(8,128)(2,1)S(1)} %collective-permute-done.3.refs_1_), channel_id=1, source_target_pairs={{0,2},{2,4},{4,6},{6,7},{7,5},{5,3},{3,1},{1,0},{8,9},{10,8},{12,1... | collective-permute-start | bytes 442376 | tf_op jit(solution)/shard_map/ppermute | solution.py:441
  27.4 1.6 %collective-permute-start.7 = (bf16[144,512]{1,0:T(8,128)(2,1)S(1)}, bf16[144,512]{1,0:T(8,128)(2,1)S(1)}, u32[]{:S(2)}, u32[]{:S(2)}) collective-permute-start(bf16[144,512]{1,0:T(8,128)(2,1)S(1)} %collective-permute-done.4.refs_2_), channel_id=1, source_target_pairs={{0,8},{8,0},{16,24},{24,16},{1,9},{9,1},{17,25},{25,17},{2,10},{10... | collective-permute-start | bytes 442376 | tf_op jit(solution)/shard_map/ppermute | solution.py:430
  27.4 5.1 %collective-permute-start.6 = (bf16[144,512]{1,0:T(8,128)(2,1)S(1)}, bf16[144,512]{1,0:T(8,128)(2,1)S(1)}, u32[]{:S(2)}, u32[]{:S(2)}) collective-permute-start(bf16[144,512]{1,0:T(8,128)(2,1)S(1)} %collective-permute-done.4.refs_2_), channel_id=1, source_target_pairs={{0,2},{2,4},{4,6},{6,7},{7,5},{5,3},{3,1},{1,0},{8,9},{10,8},{12,1... | collective-permute-start | bytes 442376 | tf_op jit(solution)/shard_map/ppermute | solution.py:441
  32.7 9.3 %collective-permute-start.12 = (bf16[1376,256]{1,0:T(8,128)(2,1)S(1)}, bf16[1376,256]{1,0:T(8,128)(2,1)S(1)}, u32[]{:S(2)}, u32[]{:S(2)}) collective-permute-start(bf16[1376,256]{1,0:T(8,128)(2,1)S(1)} %collective-permute-done.8.refs_2_), channel_id=1, source_target_pairs={{0,8},{8,0},{16,24},{24,16},{1,9},{9,1},{17,25},{25,17},{2,10},{10... | collective-permute-start | bytes 2113544 | tf_op jit(solution)/shard_map/ppermute | solution.py:430
  32.7 14.0 %collective-permute-start.14 = (bf16[688,256]{1,0:T(8,128)(2,1)S(1)}, bf16[688,256]{1,0:T(8,128)(2,1)S(1)}, u32[]{:S(2)}, u32[]{:S(2)}) collective-permute-start(bf16[688,256]{1,0:T(8,128)(2,1)S(1)} %get-tuple-element.94), channel_id=1, source_target_pairs={{0,16},{8,24},{16,0},{24,8},{1,17},{9,25},{17,1},{25,9},{2,18},{10... | collective-permute-start | bytes 1056776 | tf_op jit(solution)/shard_map/ppermute | solution.py:434
  34.4 1.8 %collective-permute-start.10 = (bf16[144,512]{1,0:T(8,128)(2,1)S(1)}, bf16[144,512]{1,0:T(8,128)(2,1)S(1)}, u32[]{:S(2)}, u32[]{:S(2)}) collective-permute-start(bf16[144,512]{1,0:T(8,128)(2,1)S(1)} %collective-permute-done.6.refs_3_), channel_id=1, source_target_pairs={{0,8},{8,0},{16,24},{24,16},{1,9},{9,1},{17,25},{25,17},{2,10},{10... | collective-permute-start | bytes 442376 | tf_op jit(solution)/shard_map/ppermute | solution.py:430
  34.7 5.1 %collective-permute-start.9 = (bf16[144,512]{1,0:T(8,128)(2,1)S(1)}, bf16[144,512]{1,0:T(8,128)(2,1)S(1)}, u32[]{:S(2)}, u32[]{:S(2)}) collective-permute-start(bf16[144,512]{1,0:T(8,128)(2,1)S(1)} %collective-permute-done.6.refs_3_), channel_id=1, source_target_pairs={{0,2},{2,4},{4,6},{6,7},{7,5},{5,3},{3,1},{1,0},{8,9},{10,8},{12,1... | collective-permute-start | bytes 442376 | tf_op jit(solution)/shard_map/ppermute | solution.py:441
  36.2 10.4 %collective-permute-start.15 = (bf16[256,256]{1,0:T(8,128)(2,1)S(1)}, bf16[256,256]{1,0:T(8,128)(2,1)S(1)}, u32[]{:S(2)}, u32[]{:S(2)}) collective-permute-start(bf16[256,256]{1,0:T(8,128)(2,1)S(1)} %get-tuple-element.96), channel_id=1, source_target_pairs={{0,16},{8,24},{16,0},{24,8},{1,17},{9,25},{17,1},{25,9},{2,18},{10... | collective-permute-start | bytes 393224 | tf_op jit(solution)/shard_map/ppermute | solution.py:434
  39.8 2.1 %collective-permute-start.13 = (f32[1,128]{1,0:T(1,128)S(1)}, f32[1,128]{1,0:T(1,128)S(1)}, u32[]{:S(2)}, u32[]{:S(2)}) collective-permute-start(f32[1,128]{1,0:T(1,128)S(1)} %bitcast.14), channel_id=1, source_target_pairs={{0,8},{8,0},{16,24},{24,16},{1,9},{9,1},{17,25},{25,17},{2,10},{10... | collective-permute-start | bytes 1544 | tf_op jit(solution)/shard_map/ppermute | solution.py:430
  46.7 1.9 %collective-permute-start.17 = (bf16[688,256]{1,0:T(8,128)(2,1)S(1)}, bf16[688,256]{1,0:T(8,128)(2,1)S(1)}, u32[]{:S(2)}, u32[]{:S(2)}) collective-permute-start(bf16[688,256]{1,0:T(8,128)(2,1)S(1)} %collective-permute-done.14.refs_2_), channel_id=1, source_target_pairs={{0,8},{8,0},{16,24},{24,16},{1,9},{9,1},{17,25},{25,17},{2,10},{10... | collective-permute-start | bytes 1056776 | tf_op jit(solution)/shard_map/ppermute | solution.py:430
  47.2 3.6 %collective-permute-start.16 = (f32[1,512]{1,0:T(1,128)S(1)}, f32[1,512]{1,0:T(1,128)S(1)}, u32[]{:S(2)}, u32[]{:S(2)}) collective-permute-start(f32[1,512]{1,0:T(1,128)S(1)} %get-tuple-element.97), channel_id=1, source_target_pairs={{0,16},{8,24},{16,0},{24,8},{1,17},{9,25},{17,1},{25,9},{2,18},{10... | collective-permute-start | bytes 6152 | tf_op jit(solution)/shard_map/ppermute | solution.py:434
  50.8 8.1 %collective-permute-start.22 = (bf16[432,256]{1,0:T(8,128)(2,1)S(1)}, bf16[432,256]{1,0:T(8,128)(2,1)S(1)}, u32[]{:S(2)}, u32[]{:S(2)}) collective-permute-start(bf16[432,256]{1,0:T(8,128)(2,1)S(1)} %get-tuple-element.111), channel_id=1, source_target_pairs={{0,16},{8,24},{16,0},{24,8},{1,17},{9,25},{17,1},{25,9},{2,18},{10... | collective-permute-start | bytes 663560 | tf_op jit(solution)/shard_map/ppermute | solution.py:434
  51.8 5.2 %collective-permute-start.20 = (bf16[256,256]{1,0:T(8,128)(2,1)S(1)}, bf16[256,256]{1,0:T(8,128)(2,1)S(1)}, u32[]{:S(2)}, u32[]{:S(2)}) collective-permute-start(bf16[256,256]{1,0:T(8,128)(2,1)S(1)} %collective-permute-done.15.refs_2_), channel_id=1, source_target_pairs={{0,8},{8,0},{16,24},{24,16},{1,9},{9,1},{17,25},{25,17},{2,10},{10... | collective-permute-start | bytes 393224 | tf_op jit(solution)/shard_map/ppermute | solution.py:430
  51.8 3.6 %collective-permute-start.18 = (f32[1,512]{1,0:T(1,128)S(1)}, f32[1,512]{1,0:T(1,128)S(1)}, u32[]{:S(2)}, u32[]{:S(2)}) collective-permute-start(f32[1,512]{1,0:T(1,128)S(1)} %add.20), channel_id=1, source_target_pairs={{0,1},{1,0},{2,3},{3,2},{4,5},{5,4},{6,7},{7,6},{8,9},{9,8},{10,11... | collective-permute-start | bytes 6152 | tf_op jit(solution)/shard_map/ppermute | solution.py:546
  55.4 3.6 %collective-permute-start.19 = (f32[1,512]{1,0:T(1,128)S(1)}, f32[1,512]{1,0:T(1,128)S(1)}, u32[]{:S(2)}, u32[]{:S(2)}) collective-permute-start(f32[1,512]{1,0:T(1,128)S(1)} %add.21), channel_id=1, source_target_pairs={{0,2},{1,3},{2,0},{3,1},{4,6},{5,7},{6,4},{7,5},{8,10},{9,11},{10,... | collective-permute-start | bytes 6152 | tf_op jit(solution)/shard_map/ppermute | solution.py:546
  59.0 2.7 %collective-permute-start.23 = (bf16[432,256]{1,0:T(8,128)(2,1)S(1)}, bf16[432,256]{1,0:T(8,128)(2,1)S(1)}, u32[]{:S(2)}, u32[]{:S(2)}) collective-permute-start(bf16[432,256]{1,0:T(8,128)(2,1)S(1)} %collective-permute-done.22.refs_2_), channel_id=1, source_target_pairs={{0,8},{8,0},{16,24},{24,16},{1,9},{9,1},{17,25},{25,17},{2,10},{10... | collective-permute-start | bytes 663560 | tf_op jit(solution)/shard_map/ppermute | solution.py:430
  59.1 4.9 %collective-permute-start.21 = (f32[1,512]{1,0:T(1,128)S(1)}, f32[1,512]{1,0:T(1,128)S(1)}, u32[]{:S(2)}, u32[]{:S(2)}) collective-permute-start(f32[1,512]{1,0:T(1,128)S(1)} %add.22), channel_id=1, source_target_pairs={{0,4},{1,5},{2,6},{3,7},{4,0},{5,1},{6,2},{7,3},{8,12},{9,13},{10,... | collective-permute-start | bytes 6152 | tf_op jit(solution)/shard_map/ppermute | solution.py:546
  (4 other events, 59.8 us)

commit v3 on v2

--- a/solution.py
+++ b/solution.py
@@ -175,27 +175,31 @@
     )(where, mine, other)
 
 
-def assemble_kernel(blocks, offset, where_ref, *refs):
-    high_ref, low_ref = refs[blocks:]
-    for b, ref in enumerate(refs[:blocks]):
+def assemble_kernel(offsets, where_ref, *refs):
+    high_ref, low_ref = refs[len(refs) - 2 :]
+    for offset, ref in zip(offsets, refs):
         tokens = ref.shape[0] - TOP_ROWS
-        rows = pl.ds(pl.multiple_of(where_ref[offset + b] * tokens, tokens), tokens)
+        rows = pl.ds(pl.multiple_of(where_ref[offset] * tokens, tokens), tokens)
         high_ref[rows, :], low_ref[rows, :] = split(decode(ref))
 
 
-def assemble(where, found, offset):
-    blocks = len(found)
-    rows, rank = found[0].shape
-    shape = (blocks * (rows - TOP_ROWS), rank)
-    return pl.pallas_call(
-        functools.partial(assemble_kernel, blocks, offset),
-        out_shape=[jax.ShapeDtypeStruct(shape, bf16)] * 2,
-        in_specs=[SMEM] + [VMEM] * blocks,
+def assemble(where, found, offsets, tokens, previous=()):
+    rank = found[0].shape[1]
+    first = 1 + len(found)
+    return pl.pallas_call(
+        functools.partial(assemble_kernel, offsets),
+        out_shape=[jax.ShapeDtypeStruct((tokens, rank), bf16)] * 2,
+        in_specs=[SMEM] + [VMEM] * (len(found) + len(previous)),
         out_specs=[VMEM] * 2,
+        input_output_aliases={first + n: n for n in range(len(previous))},
         compiler_params=pltpu.CompilerParams(vmem_limit_bytes=4 * MIB),
-        cost_estimate=pl.CostEstimate(flops=0, bytes_accessed=0, transcendentals=0),
+        cost_estimate=pl.CostEstimate(
+            flops=0,
+            bytes_accessed=0 if previous else 8 * tokens * rank,
+            transcendentals=0,
+        ),
         name="assemble",
-    )(where, *found)
+    )(where, *found, *previous)
 
 
 def cut_kernel(starts_at, counts, where_ref, grads_ref, *refs):
@@ -315,61 +319,68 @@
     count, parts, rows_at, order_at, where_ref, sums_ref, most_ref, high_ref, small_ref, *refs
 ):
     part_refs, col_refs = refs[:parts], refs[parts : 2 * parts]
-    out_ref, rownext_ref, colnext_ref, lhs_ref, lhs_small_ref, scale_ref = refs[2 * parts :]
+    out_ref, rownext_ref, colnext_ref, lhs_ref, lhs_small_ref, slot_ref, sem = refs[2 * parts :]
     tiles, tile, rank = lhs_ref.shape
-    step = pl.program_id(0)
-
-    @pl.when(step == 0)
-    def _():
-        row_next = (1.0 - beta_two) * (sums_ref[...] / count + epsilon)
-        rows = rownext_ref.shape[1]
-        held = jnp.zeros((1, rows), f32)
-        for r in range(rank // rows):
-            held = jnp.where(where_ref[rows_at] == r, row_next[:, r * rows : (r + 1) * rows], held)
-        rownext_ref[...] = held
-        scale = scale_alpha * lax.rsqrt(row_next) * jnp.sqrt(
-            jnp.mean(row_next, axis=1, keepdims=True)
-        )
-        strip = colnext_ref.shape[1]
-        for n, begin, size, ref, row in segments(col_refs, part_refs, tile):
-            strip = pl.ds(where_ref[order_at + n], 1)
-            colnext_ref[strip, begin : begin + size] = ref[row // tile : row // tile + 1, :size]
-        top = jnp.maximum(jnp.max(scale * most_ref[...], axis=1, keepdims=True), 1e-30)
-        scale_ref[0:1, :] = scale
-        scale_ref[1:2, :] = jnp.broadcast_to(2.0**7 / top, (1, rank))
-        scale_ref[2:3, :] = jnp.broadcast_to(top * 2.0**-27, (1, rank))
-
+    wide = slot_ref.shape[2]
+    row_next = (1.0 - beta_two) * (sums_ref[...] / count + epsilon)
+    scale = scale_alpha * lax.rsqrt(row_next) * jnp.sqrt(
+        jnp.mean(row_next, axis=1, keepdims=True)
+    )
+    top = jnp.maximum(jnp.max(scale * most_ref[...], axis=1, keepdims=True), 1e-30)
+    grow = scale * (2.0**7 / top)
+    shrink = top * 2.0**-27
+
+    def prepare(number):
+        for n, begin, size, ref, row in segments(part_refs, part_refs, tile):
+            if n != number:
+                continue
+            part = ref[row : row + size, :]
+            value = part * scale
+            high = value.astype(bf16)
+            at = slice(begin, begin + size)
+            lhs_ref[number, at, :] = high
+            lhs_small_ref[number, at, :rank] = (part * grow).astype(f8)
+            lhs_small_ref[number, at, rank:] = (
+                (value - high.astype(f32)) * (2.0**15 / top)
+            ).astype(f8)
+
+    prepare(0)
+    copies = [None, None]
     for number in range(tiles):
-
-        @pl.when(step == number)
-        def _():
-            for n, begin, size, ref, row in segments(part_refs, part_refs, tile):
-                if n != number:
-                    continue
-                value = ref[row : row + size, :] * scale_ref[0:1, :]
-                high = value.astype(bf16)
-                grow = scale_ref[1:2, :]
-                at = slice(begin, begin + size)
-                lhs_ref[number, at, :] = high
-                lhs_small_ref[number, at, :rank] = (value * grow).astype(f8)
-                lhs_small_ref[number, at, rank:] = (
-                    (value - high.astype(f32)) * (grow * 2.0**8)
-                ).astype(f8)
-
-    now = step % tiles
-    lanes = pl.ds(pl.multiple_of(step // tiles * out_ref.shape[1], 128), out_ref.shape[1])
-    out_ref[...] = jnp.dot(
-        lhs_ref[now], high_ref[:, lanes], preferred_element_type=f32
-    ) + scale_ref[2:3, 0:1] * jnp.dot(
-        lhs_small_ref[now], small_ref[:, lanes], preferred_element_type=f32
-    )
+        strip = pl.ds(pl.multiple_of(where_ref[order_at + number] * tile, 8), tile)
+        for half in range(HALVES):
+            slot = (number * HALVES + half) % 2
+            lanes = slice(half * wide, (half + 1) * wide)
+            if copies[slot] is not None:
+                copies[slot].wait()
+            if half == 0 and number + 1 < tiles:
+                prepare(number + 1)
+            slot_ref[slot] = jnp.dot(
+                lhs_ref[number], high_ref[:, lanes], preferred_element_type=f32
+            ) + shrink * jnp.dot(
+                lhs_small_ref[number], small_ref[:, lanes], preferred_element_type=f32
+            )
+            copies[slot] = pltpu.make_async_copy(
+                slot_ref.at[slot], out_ref.at[strip, pl.ds(half * wide, wide)], sem.at[slot]
+            )
+            copies[slot].start()
+
+    rows = rownext_ref.shape[1]
+    held = jnp.zeros((1, rows), f32)
+    for r in range(rank // rows):
+        held = jnp.where(where_ref[rows_at] == r, row_next[:, r * rows : (r + 1) * rows], held)
+    rownext_ref[...] = held
+    for n, begin, size, ref, row in segments(col_refs, part_refs, tile):
+        strip = pl.ds(where_ref[order_at + n], 1)
+        colnext_ref[strip, begin : begin + size] = ref[row // tile : row // tile + 1, :size]
+    for copy in copies:
+        copy.wait()
 
 
 def update(where, sums, most, high, small, parts, cols, strip, hidden, n_row, rows_at, order_at):
     rank, rows = high.shape
     columns = sum(part.shape[0] for part in parts)
     tiles = columns // strip
-    wide = rows // HALVES
     return pl.pallas_call(
         functools.partial(update_kernel, float(hidden), len(parts), rows_at, order_at),
         out_shape=[
@@ -377,21 +388,14 @@
             jax.ShapeDtypeStruct((1, rank // n_row), f32),
             jax.ShapeDtypeStruct((tiles, strip), f32),
         ],
-        grid_spec=pltpu.PrefetchScalarGridSpec(
-            num_scalar_prefetch=1,
-            grid=(tiles * HALVES,),
-            in_specs=[VMEM] * (4 + 2 * len(parts)),
-            out_specs=[
-                pl.BlockSpec((strip, wide), lambda i, s: (s[order_at + i % tiles], i // tiles)),
-                pl.BlockSpec((1, rank // n_row), lambda i, s: (0, 0)),
-                pl.BlockSpec((tiles, strip), lambda i, s: (0, 0)),
-            ],
-            scratch_shapes=[
-                pltpu.VMEM((tiles, strip, rank), bf16),
-                pltpu.VMEM((tiles, strip, 2 * rank), f8),
-                pltpu.VMEM((8, rank), f32),
-            ],
-        ),
+        in_specs=[SMEM] + [VMEM] * (4 + 2 * len(parts)),
+        out_specs=[pl.BlockSpec(memory_space=pl.ANY), VMEM, VMEM],
+        scratch_shapes=[
+            pltpu.VMEM((tiles, strip, rank), bf16),
+            pltpu.VMEM((tiles, strip, 2 * rank), f8),
+            pltpu.VMEM((2, strip, rows // HALVES), f32),
+            pltpu.SemaphoreType.DMA((2,)),
+        ],
         compiler_params=pltpu.CompilerParams(vmem_limit_bytes=28 * MIB),
         cost_estimate=pl.CostEstimate(
             flops=4 * columns * rank * rows, bytes_accessed=4 * columns * rows, transcendentals=0
@@ -402,7 +406,7 @@
 
 def per_device(n_row, n_col, activations, out_grads, basis, row_moment, col_moment):
     chips = n_row // CORES
-    columns = col_moment.shape[0]
+    columns, tokens = col_moment.shape[0], activations.shape[0] * n_col
     hidden = columns * n_col
     rank = basis.shape[1]
     width = -(-columns // (32 * chips)) * 32
@@ -511,7 +515,15 @@
             moving += turned
         if hop == max(hops - 1, 1):
             moving += got[0]
+        if hop == hops:
+            known = [(block, n) for n, block in enumerate(blocks)]
+            known += [(block, hops + 1 + n) for n, block in enumerate(siblings)]
+            early = assemble(
+                where, [block for block, _ in known], [blocks_at + n for _, n in known], tokens
+            )
+            moving += early
         moved = lax.optimization_barrier(tuple(moving))
+        early = moved[-2:]
         held = moved[0]
         blocks.append(held)
         siblings += moved[1:2] if hop > 1 else []
@@ -521,7 +533,13 @@
                 got[move] = exchange(move, held)
     if 2 * hops != n_col:
         siblings.append(to_sibling(held))
-    high, low = assemble(where, blocks + siblings, blocks_at)
+    known = len(known)
+    late = [(held, hops)] + [
+        (block, hops + 1 + n) for n, block in enumerate(siblings) if hops + n >= known
+    ]
+    high, low = assemble(
+        where, [block for block, _ in late], [blocks_at + n for _, n in late], tokens, early
+    )
 
     found = []
 

time: 83.3 us -> 83.5 us (level)
    pallas_call x1 -> x2, Pallas kernels: 1.7 us -> 2.26 us  [assemble(): pl.pallas_call(functools.partial(assemble_kernel, offsets), out_shape=[ja...]
  transfers between devices with their start and end apart: 24 -> 24, of which waited for: 11 -> 11; matrix products, arithmetic and copies ran while one was open for 1% -> 1% of each run, Pallas kernels for 21% -> 22%
where the time goes in v3:
time: 83.5 us; the launch traced here: 83.2 us
  Pallas kernels  41.3 us (49%)
  starting transfers between devices  22.1 us (26%)
  waiting for transfers between devices  14.1 us (17%)
  local copies, waits for them, and re-layouts  3.99 us (5%)
  other arithmetic  0.94 us (1%)
    pallas_call x1, Pallas kernels, update(): pl.pallas_call(functools.partial(update_kernel, float(hidden), len(parts)...  18.6 us
    pallas_call x5, Pallas kernels, project(): pl.pallas_call(functools.partial(project_kernel, len(grads), skip, step,...  12.9 us
    ppermute x4, waiting for transfers between devices, around(): return lax.ppermute(value, ('row', 'col'), pairs)  9.94 us
    ppermute x6, starting transfers between devices, to_chip(): return lax.ppermute(value, 'row', pairs)  8.33 us
    ppermute x4, starting transfers between devices, around(): return lax.ppermute(value, ('row', 'col'), pairs)  6.27 us
    ppermute x3, starting transfers between devices, per_device(): arrived = [lax.ppermute(sums, 'col', [(c, c ^ step) for c in range(n_col)])]  5.75 us
    pallas_call x1, Pallas kernels, low_partial(): pl.pallas_call(functools.partial(low_kernel, steps, n_col), out_shape=(ha...  4.31 us
    pallas_call x2, Pallas kernels, assemble(): pl.pallas_call(functools.partial(assemble_kernel, offsets), out_shape=[ja...  2.26 us
  transfers between devices with their start and end apart: 24, of which 11 were waited for; matrix products, arithmetic and copies ran while one was open for 1% of the time, Pallas kernels for 22%

profile of v3, /device:TPU:0, one launch (start us, length us, event | category | flops | bytes accessed | tf_op | source)
XLA Modules:
  0.0 83.2 jit_solution(8927740309637968279)
XLA Ops:
  0.6 4.3 %low_partial.1 = (f32[128,256]{1,0:T(8,128)}, f32[128,256]{1,0:T(8,128)}) custom-call(s32[1]{0:T(128)} %bitcast.here_ref, bf16[128,2048]{1,0:T(8,128)(2,1)} %act_ref.1, f32[2048,512]{1,0:T(8,128)} %basis_ref.2), custom_call_target="tpu_custom_call" | custom-call | flops 536870912 | bytes 6291456 | tf_op jit(solution)/shard_map/low_partial/pallas_call | solution.py:65
  7.6 2.9 %collective-permute-start.1 = (f32[128,256]{1,0:T(8,128)S(1)}, f32[128,256]{1,0:T(8,128)S(1)}, u32[]{:S(2)}, u32[]{:S(2)}) collective-permute-start(f32[128,256]{1,0:T(8,128)S(1)} %add.19.refs_0_), channel_id=1, source_target_pairs={{0,16},{8,24},{16,0},{24,8},{1,17},{9,25},{17,1},{25,9},{2,18},{10... | collective-permute-start | bytes 393224 | tf_op jit(solution)/shard_map/ppermute | solution.py:438
  11.2 1.4 %cut.1 = (bf16[1376,256]{1,0:T(8,128)(2,1)S(1)}, bf16[688,256]{1,0:T(8,128)(2,1)S(1)}, bf16[256,256]{1,0:T(8,128)(2,1)S(1)}, bf16[432,256]{1,0:T(8,128)(2,1)S(1)}) custom-call(s32[27]{0:T(128)S(1)} %dynamic-slice_bitcast_fusion.where_ref, bf16[2752,256]{1,0:T(8,128)(2,1)S(1)} %bitcast.7), custom_call_target="tpu_custom_call" | custom-call | bytes 2818048 | tf_op jit(solution)/shard_map/cut/pallas_call | solution.py:219
  12.7 1.7 %collective-permute-done.1.refs_1_ = f32[128,256]{1,0:T(8,128)S(1)} collective-permute-done((f32[128,256]{1,0:T(8,128)S(1)}, f32[128,256]{1,0:T(8,128)S(1)}, u32[]{:S(2)}, u32[]{:S(2)}) %collective-permute-start.1) | collective-permute-done | bytes 131104 | tf_op jit(solution)/shard_map/ppermute | solution.py:438
  14.5 1.8 %collective-permute-start.8 = (bf16[1376,256]{1,0:T(8,128)(2,1)S(1)}, bf16[1376,256]{1,0:T(8,128)(2,1)S(1)}, u32[]{:S(2)}, u32[]{:S(2)}) collective-permute-start(bf16[1376,256]{1,0:T(8,128)(2,1)S(1)} %get-tuple-element.84), channel_id=1, source_target_pairs={{0,16},{8,24},{16,0},{24,8},{1,17},{9,25},{17,1},{25,9},{2,18},{10... | collective-permute-start | bytes 2113544 | tf_op jit(solution)/shard_map/ppermute | solution.py:438
  17.1 1.6 %collective-permute-start.3 = (bf16[144,512]{1,0:T(8,128)(2,1)S(1)}, bf16[144,512]{1,0:T(8,128)(2,1)S(1)}, u32[]{:S(2)}, u32[]{:S(2)}) collective-permute-start(bf16[144,512]{1,0:T(8,128)(2,1)S(1)} %join.1.refs_0_), channel_id=1, source_target_pairs={{0,2},{2,4},{4,6},{6,7},{7,5},{5,3},{3,1},{1,0},{8,9},{10,8},{12,1... | collective-permute-start | bytes 442376 | tf_op jit(solution)/shard_map/ppermute | solution.py:445
  18.7 3.6 %collective-permute-done.3.refs_1_ = bf16[144,512]{1,0:T(8,128)(2,1)S(1)} collective-permute-done((bf16[144,512]{1,0:T(8,128)(2,1)S(1)}, bf16[144,512]{1,0:T(8,128)(2,1)S(1)}, u32[]{:S(2)}, u32[]{:S(2)}) %collective-permute-start.3) | collective-permute-done | bytes 147488 | tf_op jit(solution)/shard_map/ppermute | solution.py:445
  22.2 1.6 %collective-permute-start.4 = (bf16[144,512]{1,0:T(8,128)(2,1)S(1)}, bf16[144,512]{1,0:T(8,128)(2,1)S(1)}, u32[]{:S(2)}, u32[]{:S(2)}) collective-permute-start(bf16[144,512]{1,0:T(8,128)(2,1)S(1)} %collective-permute-done.3.refs_1_), channel_id=1, source_target_pairs={{0,2},{2,4},{4,6},{6,7},{7,5},{5,3},{3,1},{1,0},{8,9},{10,8},{12,1... | collective-permute-start | bytes 442376 | tf_op jit(solution)/shard_map/ppermute | solution.py:445
  23.8 2.2 %copy-done.1 = f32[2048,512]{1,0:T(8,128)S(1)} copy-done((f32[2048,512]{1,0:T(8,128)S(1)}, f32[2048,512]{1,0:T(8,128)}, u32[]{:S(2)}) %copy-start.1) | copy-done | bytes 4194328
  27.4 1.5 %collective-permute-start.6 = (bf16[144,512]{1,0:T(8,128)(2,1)S(1)}, bf16[144,512]{1,0:T(8,128)(2,1)S(1)}, u32[]{:S(2)}, u32[]{:S(2)}) collective-permute-start(bf16[144,512]{1,0:T(8,128)(2,1)S(1)} %collective-permute-done.4.refs_2_), channel_id=1, source_target_pairs={{0,2},{2,4},{4,6},{6,7},{7,5},{5,3},{3,1},{1,0},{8,9},{10,8},{12,1... | collective-permute-start | bytes 442376 | tf_op jit(solution)/shard_map/ppermute | solution.py:445
  29.0 3.6 %collective-permute-done.6.refs_3_ = bf16[144,512]{1,0:T(8,128)(2,1)S(1)} collective-permute-done((bf16[144,512]{1,0:T(8,128)(2,1)S(1)}, bf16[144,512]{1,0:T(8,128)(2,1)S(1)}, u32[]{:S(2)}, u32[]{:S(2)}) %collective-permute-start.6) | collective-permute-done | bytes 147488 | tf_op jit(solution)/shard_map/ppermute | solution.py:445
  32.7 1.7 %collective-permute-start.14 = (bf16[688,256]{1,0:T(8,128)(2,1)S(1)}, bf16[688,256]{1,0:T(8,128)(2,1)S(1)}, u32[]{:S(2)}, u32[]{:S(2)}) collective-permute-start(bf16[688,256]{1,0:T(8,128)(2,1)S(1)} %get-tuple-element.102), channel_id=1, source_target_pairs={{0,16},{8,24},{16,0},{24,8},{1,17},{9,25},{17,1},{25,9},{2,18},{10... | collective-permute-start | bytes 1056776 | tf_op jit(solution)/shard_map/ppermute | solution.py:438
  34.7 1.6 %collective-permute-start.9 = (bf16[144,512]{1,0:T(8,128)(2,1)S(1)}, bf16[144,512]{1,0:T(8,128)(2,1)S(1)}, u32[]{:S(2)}, u32[]{:S(2)}) collective-permute-start(bf16[144,512]{1,0:T(8,128)(2,1)S(1)} %collective-permute-done.6.refs_3_), channel_id=1, source_target_pairs={{0,2},{2,4},{4,6},{6,7},{7,5},{5,3},{3,1},{1,0},{8,9},{10,8},{12,1... | collective-permute-start | bytes 442376 | tf_op jit(solution)/shard_map/ppermute | solution.py:445
  37.2 2.6 %collective-permute-done.9.refs_0_ = bf16[144,512]{1,0:T(8,128)(2,1)S(1)} collective-permute-done((bf16[144,512]{1,0:T(8,128)(2,1)S(1)}, bf16[144,512]{1,0:T(8,128)(2,1)S(1)}, u32[]{:S(2)}, u32[]{:S(2)}) %collective-permute-start.9) | collective-permute-done | bytes 147488 | tf_op jit(solution)/shard_map/ppermute | solution.py:445
  39.8 1.4 %assemble.2 = (bf16[1024,512]{1,0:T(8,128)(2,1)S(1)}, bf16[1024,512]{1,0:T(8,128)(2,1)S(1)}) custom-call(s32[27]{0:T(128)S(1)} %dynamic-slice_bitcast_fusion.where_ref, bf16[144,512]{1,0:T(8,128)(2,1)S(1)} %join.1.refs_0_, bf16[144,512]{1,0:T(8,128)(2,1)S(1)} %collective-permute-done.3.refs_1_, bf16[144,512]{1,0:T(8,128)(2,1)S(1)} %collective-permute-done.4.refs_2_, ...), custom_call_target="tpu_custom_call" | custom-call | bytes 4194304 | tf_op jit(solution)/shard_map/assemble/pallas_call | solution.py:189
  42.1 4.7 %project.5 = (f32[1376,512]{1,0:T(8,128)S(1)}, f32[2,768]{1,0:T(2,128)S(1)}, f32[1,512]{1,0:T(1,128)S(1)}, f32[1,512]{1,0:T(1,128)S(1)}) custom-call(s32[27]{0:T(128)S(1)} %dynamic-slice_bitcast_fusion.where_ref, bf16[1024,512]{1,0:T(8,128)(2,1)S(1)} %get-tuple-element.94.high_ref, bf16[1024,512]{1,0:T(8,128)(2,1)S(1)} %get-tuple-element.95.low_ref, ...), custom_call_target="tpu_custom_call" | custom-call | tf_op jit(solution)/shard_map/project/pallas_call | solution.py:289
  48.7 2.1 %project.6 = (f32[384,512]{1,0:T(8,128)S(1)}, f32[1,384]{1,0:T(1,128)S(1)}, f32[1,512]{1,0:T(1,128)}, f32[1,512]{1,0:T(1,128)S(1)}) custom-call(s32[27]{0:T(128)S(1)} %dynamic-slice_bitcast_fusion.where_ref, bf16[1024,512]{1,0:T(8,128)(2,1)S(1)} %get-tuple-element.94.high_ref, bf16[1024,512]{1,0:T(8,128)(2,1)S(1)} %get-tuple-element.95.low_ref, ...), custom_call_target="tpu_custom_call" | custom-call | tf_op jit(solution)/shard_map/project/pallas_call | solution.py:289
  51.8 1.5 %collective-permute-start.18 = (f32[1,512]{1,0:T(1,128)S(1)}, f32[1,512]{1,0:T(1,128)S(1)}, u32[]{:S(2)}, u32[]{:S(2)}) collective-permute-start(f32[1,512]{1,0:T(1,128)S(1)} %add.20), channel_id=1, source_target_pairs={{0,1},{1,0},{2,3},{3,2},{4,5},{5,4},{6,7},{7,6},{8,9},{9,8},{10,11... | collective-permute-start | bytes 6152 | tf_op jit(solution)/shard_map/ppermute | solution.py:564
  53.3 2.0 %project.7 = (f32[304,512]{1,0:T(8,128)S(1)}, f32[1,384]{1,0:T(1,128)S(1)}, f32[1,512]{1,0:T(1,128)}, f32[1,512]{1,0:T(1,128)S(1)}) custom-call(s32[27]{0:T(128)S(1)} %dynamic-slice_bitcast_fusion.where_ref, bf16[1024,512]{1,0:T(8,128)(2,1)S(1)} %get-tuple-element.94.high_ref, bf16[1024,512]{1,0:T(8,128)(2,1)S(1)} %get-tuple-element.95.low_ref, ...), custom_call_target="tpu_custom_call" | custom-call | tf_op jit(solution)/shard_map/project/pallas_call | solution.py:289
  55.4 1.6 %collective-permute-start.19 = (f32[1,512]{1,0:T(1,128)S(1)}, f32[1,512]{1,0:T(1,128)S(1)}, u32[]{:S(2)}, u32[]{:S(2)}) collective-permute-start(f32[1,512]{1,0:T(1,128)S(1)} %add.21), channel_id=1, source_target_pairs={{0,2},{1,3},{2,0},{3,1},{4,6},{5,7},{6,4},{7,5},{8,10},{9,11},{10,... | collective-permute-start | bytes 6152 | tf_op jit(solution)/shard_map/ppermute | solution.py:564
  57.0 1.9 %project.8 = (f32[256,512]{1,0:T(8,128)S(1)}, f32[1,256]{1,0:T(1,128)S(1)}, f32[1,512]{1,0:T(1,128)}, f32[1,512]{1,0:T(1,128)S(1)}) custom-call(s32[27]{0:T(128)S(1)} %dynamic-slice_bitcast_fusion.where_ref, bf16[1024,512]{1,0:T(8,128)(2,1)S(1)} %get-tuple-element.94.high_ref, bf16[1024,512]{1,0:T(8,128)(2,1)S(1)} %get-tuple-element.95.low_ref, ...), custom_call_target="tpu_custom_call" | custom-call | tf_op jit(solution)/shard_map/project/pallas_call | solution.py:289
  59.1 2.7 %collective-permute-start.21 = (f32[1,512]{1,0:T(1,128)S(1)}, f32[1,512]{1,0:T(1,128)S(1)}, u32[]{:S(2)}, u32[]{:S(2)}) collective-permute-start(f32[1,512]{1,0:T(1,128)S(1)} %add.22), channel_id=1, source_target_pairs={{0,4},{1,5},{2,6},{3,7},{4,0},{5,1},{6,2},{7,3},{8,12},{9,13},{10,... | collective-permute-start | bytes 6152 | tf_op jit(solution)/shard_map/ppermute | solution.py:564
  61.7 2.2 %project.9 = (f32[432,512]{1,0:T(8,128)S(1)}, f32[1,512]{1,0:T(1,128)S(1)}, f32[1,512]{1,0:T(1,128)}, f32[1,512]{1,0:T(1,128)S(1)}) custom-call(s32[27]{0:T(128)S(1)} %dynamic-slice_bitcast_fusion.where_ref, bf16[1024,512]{1,0:T(8,128)(2,1)S(1)} %get-tuple-element.94.high_ref, bf16[1024,512]{1,0:T(8,128)(2,1)S(1)} %get-tuple-element.95.low_ref, ...), custom_call_target="tpu_custom_call" | custom-call | tf_op jit(solution)/shard_map/project/pallas_call | solution.py:289
  64.0 18.6 %update.1 = (f32[2752,2048]{1,0:T(8,128)}, f32[1,128]{1,0:T(1,128)}, f32[4,688]{1,0:T(4,128)S(1)}) custom-call(s32[27]{0:T(128)S(1)} %dynamic-slice_bitcast_fusion.where_ref, f32[1,512]{1,0:T(1,128)S(1)} %add.23.sums_ref, f32[1,512]{1,0:T(1,128)S(1)} %get-tuple-element.123.most_ref, bf16[512,2048]{1,0:T(8,128)(2,1)S(1)} %get-tuple-element.80.high_ref, ...), custom_call_target="tpu_custom_call" | custom-call | flops 11542724608 | bytes 22544384 | tf_op jit(solution)/shard_map/update/pallas_call | solution.py:384
  (54 shorter events, 11.7 us)
Async XLA Ops:
  5.0 1.7 %collective-permute-start = (f32[128,256]{1,0:T(8,128)}, f32[128,256]{1,0:T(8,128)S(1)}, u32[]{:S(2)}, u32[]{:S(2)}) collective-permute-start(f32[128,256]{1,0:T(8,128)} %get-tuple-element.70), channel_id=1, source_target_pairs={{0,8},{8,0},{16,24},{24,16},{1,9},{9,1},{17,25},{25,17},{2,10},{10... | collective-permute-start | bytes 393224 | tf_op jit(solution)/shard_map/ppermute | solution.py:434
  7.6 6.7 %collective-permute-start.1 = (f32[128,256]{1,0:T(8,128)S(1)}, f32[128,256]{1,0:T(8,128)S(1)}, u32[]{:S(2)}, u32[]{:S(2)}) collective-permute-start(f32[128,256]{1,0:T(8,128)S(1)} %add.19.refs_0_), channel_id=1, source_target_pairs={{0,16},{8,24},{16,0},{24,8},{1,17},{9,25},{17,1},{25,9},{2,18},{10... | collective-permute-start | bytes 393224 | tf_op jit(solution)/shard_map/ppermute | solution.py:438
  14.4 1.9 %collective-permute-start.2 = (bf16[144,256]{1,0:T(8,128)(2,1)S(1)}, bf16[144,256]{1,0:T(8,128)(2,1)S(1)}, u32[]{:S(2)}, u32[]{:S(2)}) collective-permute-start(bf16[144,256]{1,0:T(8,128)(2,1)S(1)} %encode.1.mine_ref), channel_id=1, source_target_pairs={{0,8},{8,0},{16,24},{24,16},{1,9},{9,1},{17,25},{25,17},{2,10},{10... | collective-permute-start | bytes 221192 | tf_op jit(solution)/shard_map/ppermute | solution.py:434
  14.5 18.2 %collective-permute-start.8 = (bf16[1376,256]{1,0:T(8,128)(2,1)S(1)}, bf16[1376,256]{1,0:T(8,128)(2,1)S(1)}, u32[]{:S(2)}, u32[]{:S(2)}) collective-permute-start(bf16[1376,256]{1,0:T(8,128)(2,1)S(1)} %get-tuple-element.84), channel_id=1, source_target_pairs={{0,16},{8,24},{16,0},{24,8},{1,17},{9,25},{17,1},{25,9},{2,18},{10... | collective-permute-start | bytes 2113544 | tf_op jit(solution)/shard_map/ppermute | solution.py:438
  16.9 25.2 %collective-permute-start.11 = (bf16[2752,256]{1,0:T(8,128)(2,1)S(1)}, bf16[2752,256]{1,0:T(8,128)(2,1)S(1)}, u32[]{:S(2)}, u32[]{:S(2)}) collective-permute-start(bf16[2752,256]{1,0:T(8,128)(2,1)S(1)} %bitcast.8), channel_id=1, source_target_pairs={{0,8},{8,0},{16,24},{24,16},{1,9},{9,1},{17,25},{25,17},{2,10},{10... | collective-permute-start | bytes 4227080 | tf_op jit(solution)/shard_map/ppermute | solution.py:434
  17.1 5.1 %collective-permute-start.3 = (bf16[144,512]{1,0:T(8,128)(2,1)S(1)}, bf16[144,512]{1,0:T(8,128)(2,1)S(1)}, u32[]{:S(2)}, u32[]{:S(2)}) collective-permute-start(bf16[144,512]{1,0:T(8,128)(2,1)S(1)} %join.1.refs_0_), channel_id=1, source_target_pairs={{0,2},{2,4},{4,6},{6,7},{7,5},{5,3},{3,1},{1,0},{8,9},{10,8},{12,1... | collective-permute-start | bytes 442376 | tf_op jit(solution)/shard_map/ppermute | solution.py:445
  22.2 4.9 %collective-permute-start.5 = (bf16[144,512]{1,0:T(8,128)(2,1)S(1)}, bf16[144,512]{1,0:T(8,128)(2,1)S(1)}, u32[]{:S(2)}, u32[]{:S(2)}) collective-permute-start(bf16[144,512]{1,0:T(8,128)(2,1)S(1)} %collective-permute-done.3.refs_1_), channel_id=1, source_target_pairs={{0,8},{8,0},{16,24},{24,16},{1,9},{9,1},{17,25},{25,17},{2,10},{10... | collective-permute-start | bytes 442376 | tf_op jit(solution)/shard_map/ppermute | solution.py:434
  22.2 5.1 %collective-permute-start.4 = (bf16[144,512]{1,0:T(8,128)(2,1)S(1)}, bf16[144,512]{1,0:T(8,128)(2,1)S(1)}, u32[]{:S(2)}, u32[]{:S(2)}) collective-permute-start(bf16[144,512]{1,0:T(8,128)(2,1)S(1)} %collective-permute-done.3.refs_1_), channel_id=1, source_target_pairs={{0,2},{2,4},{4,6},{6,7},{7,5},{5,3},{3,1},{1,0},{8,9},{10,8},{12,1... | collective-permute-start | bytes 442376 | tf_op jit(solution)/shard_map/ppermute | solution.py:445
  27.4 1.6 %collective-permute-start.7 = (bf16[144,512]{1,0:T(8,128)(2,1)S(1)}, bf16[144,512]{1,0:T(8,128)(2,1)S(1)}, u32[]{:S(2)}, u32[]{:S(2)}) collective-permute-start(bf16[144,512]{1,0:T(8,128)(2,1)S(1)} %collective-permute-done.4.refs_2_), channel_id=1, source_target_pairs={{0,8},{8,0},{16,24},{24,16},{1,9},{9,1},{17,25},{25,17},{2,10},{10... | collective-permute-start | bytes 442376 | tf_op jit(solution)/shard_map/ppermute | solution.py:434
  27.4 5.1 %collective-permute-start.6 = (bf16[144,512]{1,0:T(8,128)(2,1)S(1)}, bf16[144,512]{1,0:T(8,128)(2,1)S(1)}, u32[]{:S(2)}, u32[]{:S(2)}) collective-permute-start(bf16[144,512]{1,0:T(8,128)(2,1)S(1)} %collective-permute-done.4.refs_2_), channel_id=1, source_target_pairs={{0,2},{2,4},{4,6},{6,7},{7,5},{5,3},{3,1},{1,0},{8,9},{10,8},{12,1... | collective-permute-start | bytes 442376 | tf_op jit(solution)/shard_map/ppermute | solution.py:445
  32.7 9.4 %collective-permute-start.12 = (bf16[1376,256]{1,0:T(8,128)(2,1)S(1)}, bf16[1376,256]{1,0:T(8,128)(2,1)S(1)}, u32[]{:S(2)}, u32[]{:S(2)}) collective-permute-start(bf16[1376,256]{1,0:T(8,128)(2,1)S(1)} %collective-permute-done.8.refs_2_), channel_id=1, source_target_pairs={{0,8},{8,0},{16,24},{24,16},{1,9},{9,1},{17,25},{25,17},{2,10},{10... | collective-permute-start | bytes 2113544 | tf_op jit(solution)/shard_map/ppermute | solution.py:434
  32.7 14.1 %collective-permute-start.14 = (bf16[688,256]{1,0:T(8,128)(2,1)S(1)}, bf16[688,256]{1,0:T(8,128)(2,1)S(1)}, u32[]{:S(2)}, u32[]{:S(2)}) collective-permute-start(bf16[688,256]{1,0:T(8,128)(2,1)S(1)} %get-tuple-element.102), channel_id=1, source_target_pairs={{0,16},{8,24},{16,0},{24,8},{1,17},{9,25},{17,1},{25,9},{2,18},{10... | collective-permute-start | bytes 1056776 | tf_op jit(solution)/shard_map/ppermute | solution.py:438
  34.4 1.8 %collective-permute-start.10 = (bf16[144,512]{1,0:T(8,128)(2,1)S(1)}, bf16[144,512]{1,0:T(8,128)(2,1)S(1)}, u32[]{:S(2)}, u32[]{:S(2)}) collective-permute-start(bf16[144,512]{1,0:T(8,128)(2,1)S(1)} %collective-permute-done.6.refs_3_), channel_id=1, source_target_pairs={{0,8},{8,0},{16,24},{24,16},{1,9},{9,1},{17,25},{25,17},{2,10},{10... | collective-permute-start | bytes 442376 | tf_op jit(solution)/shard_map/ppermute | solution.py:434
  34.7 5.1 %collective-permute-start.9 = (bf16[144,512]{1,0:T(8,128)(2,1)S(1)}, bf16[144,512]{1,0:T(8,128)(2,1)S(1)}, u32[]{:S(2)}, u32[]{:S(2)}) collective-permute-start(bf16[144,512]{1,0:T(8,128)(2,1)S(1)} %collective-permute-done.6.refs_3_), channel_id=1, source_target_pairs={{0,2},{2,4},{4,6},{6,7},{7,5},{5,3},{3,1},{1,0},{8,9},{10,8},{12,1... | collective-permute-start | bytes 442376 | tf_op jit(solution)/shard_map/ppermute | solution.py:445
  36.2 10.6 %collective-permute-start.15 = (bf16[256,256]{1,0:T(8,128)(2,1)S(1)}, bf16[256,256]{1,0:T(8,128)(2,1)S(1)}, u32[]{:S(2)}, u32[]{:S(2)}) collective-permute-start(bf16[256,256]{1,0:T(8,128)(2,1)S(1)} %get-tuple-element.104), channel_id=1, source_target_pairs={{0,16},{8,24},{16,0},{24,8},{1,17},{9,25},{17,1},{25,9},{2,18},{10... | collective-permute-start | bytes 393224 | tf_op jit(solution)/shard_map/ppermute | solution.py:438
  39.8 2.3 %collective-permute-start.13 = (f32[1,128]{1,0:T(1,128)S(1)}, f32[1,128]{1,0:T(1,128)S(1)}, u32[]{:S(2)}, u32[]{:S(2)}) collective-permute-start(f32[1,128]{1,0:T(1,128)S(1)} %bitcast.14), channel_id=1, source_target_pairs={{0,8},{8,0},{16,24},{24,16},{1,9},{9,1},{17,25},{25,17},{2,10},{10... | collective-permute-start | bytes 1544 | tf_op jit(solution)/shard_map/ppermute | solution.py:434
  46.8 1.9 %collective-permute-start.17 = (bf16[688,256]{1,0:T(8,128)(2,1)S(1)}, bf16[688,256]{1,0:T(8,128)(2,1)S(1)}, u32[]{:S(2)}, u32[]{:S(2)}) collective-permute-start(bf16[688,256]{1,0:T(8,128)(2,1)S(1)} %collective-permute-done.14.refs_2_), channel_id=1, source_target_pairs={{0,8},{8,0},{16,24},{24,16},{1,9},{9,1},{17,25},{25,17},{2,10},{10... | collective-permute-start | bytes 1056776 | tf_op jit(solution)/shard_map/ppermute | solution.py:434
  47.4 3.6 %collective-permute-start.16 = (f32[1,512]{1,0:T(1,128)S(1)}, f32[1,512]{1,0:T(1,128)S(1)}, u32[]{:S(2)}, u32[]{:S(2)}) collective-permute-start(f32[1,512]{1,0:T(1,128)S(1)} %get-tuple-element.105), channel_id=1, source_target_pairs={{0,16},{8,24},{16,0},{24,8},{1,17},{9,25},{17,1},{25,9},{2,18},{10... | collective-permute-start | bytes 6152 | tf_op jit(solution)/shard_map/ppermute | solution.py:438
  51.0 8.0 %collective-permute-start.22 = (bf16[432,256]{1,0:T(8,128)(2,1)S(1)}, bf16[432,256]{1,0:T(8,128)(2,1)S(1)}, u32[]{:S(2)}, u32[]{:S(2)}) collective-permute-start(bf16[432,256]{1,0:T(8,128)(2,1)S(1)} %get-tuple-element.119), channel_id=1, source_target_pairs={{0,16},{8,24},{16,0},{24,8},{1,17},{9,25},{17,1},{25,9},{2,18},{10... | collective-permute-start | bytes 663560 | tf_op jit(solution)/shard_map/ppermute | solution.py:438
  51.8 5.2 %collective-permute-start.20 = (bf16[256,256]{1,0:T(8,128)(2,1)S(1)}, bf16[256,256]{1,0:T(8,128)(2,1)S(1)}, u32[]{:S(2)}, u32[]{:S(2)}) collective-permute-start(bf16[256,256]{1,0:T(8,128)(2,1)S(1)} %collective-permute-done.15.refs_2_), channel_id=1, source_target_pairs={{0,8},{8,0},{16,24},{24,16},{1,9},{9,1},{17,25},{25,17},{2,10},{10... | collective-permute-start | bytes 393224 | tf_op jit(solution)/shard_map/ppermute | solution.py:434
  51.8 3.6 %collective-permute-start.18 = (f32[1,512]{1,0:T(1,128)S(1)}, f32[1,512]{1,0:T(1,128)S(1)}, u32[]{:S(2)}, u32[]{:S(2)}) collective-permute-start(f32[1,512]{1,0:T(1,128)S(1)} %add.20), channel_id=1, source_target_pairs={{0,1},{1,0},{2,3},{3,2},{4,5},{5,4},{6,7},{7,6},{8,9},{9,8},{10,11... | collective-permute-start | bytes 6152 | tf_op jit(solution)/shard_map/ppermute | solution.py:564
  55.4 3.6 %collective-permute-start.19 = (f32[1,512]{1,0:T(1,128)S(1)}, f32[1,512]{1,0:T(1,128)S(1)}, u32[]{:S(2)}, u32[]{:S(2)}) collective-permute-start(f32[1,512]{1,0:T(1,128)S(1)} %add.21), channel_id=1, source_target_pairs={{0,2},{1,3},{2,0},{3,1},{4,6},{5,7},{6,4},{7,5},{8,10},{9,11},{10,... | collective-permute-start | bytes 6152 | tf_op jit(solution)/shard_map/ppermute | solution.py:564
  59.0 2.7 %collective-permute-start.23 = (bf16[432,256]{1,0:T(8,128)(2,1)S(1)}, bf16[432,256]{1,0:T(8,128)(2,1)S(1)}, u32[]{:S(2)}, u32[]{:S(2)}) collective-permute-start(bf16[432,256]{1,0:T(8,128)(2,1)S(1)} %collective-permute-done.22.refs_2_), channel_id=1, source_target_pairs={{0,8},{8,0},{16,24},{24,16},{1,9},{9,1},{17,25},{25,17},{2,10},{10... | collective-permute-start | bytes 663560 | tf_op jit(solution)/shard_map/ppermute | solution.py:434
  59.1 4.9 %collective-permute-start.21 = (f32[1,512]{1,0:T(1,128)S(1)}, f32[1,512]{1,0:T(1,128)S(1)}, u32[]{:S(2)}, u32[]{:S(2)}) collective-permute-start(f32[1,512]{1,0:T(1,128)S(1)} %add.22), channel_id=1, source_target_pairs={{0,4},{1,5},{2,6},{3,7},{4,0},{5,1},{6,2},{7,3},{8,12},{9,13},{10,... | collective-permute-start | bytes 6152 | tf_op jit(solution)/shard_map/ppermute | solution.py:564
  (4 other events, 56.8 us)

commit v4 on v2

--- a/solution.py
+++ b/solution.py
@@ -33,16 +33,20 @@
     return max(t for t in range(unit, most + 1, unit) if size % t == 0)
 
 
-def low_kernel(steps, n_col, here_ref, act_ref, basis_ref, mine_ref, other_ref, kept_ref, sem):
+def low_kernel(
+    steps, n_col, here_ref, acts_ref, basis_ref, mine_ref, other_ref, act_ref, kept_ref, sem
+):
     depth = basis_ref.shape[0]
     tile = depth // steps
     half = mine_ref.shape[1]
-    copies = []
+    copies, first = [], pltpu.make_async_copy(acts_ref, act_ref, sem.at[steps])
+    first.start()
     for n in range(steps):
         at = pl.ds(n * tile, tile)
         copies.append(pltpu.make_async_copy(basis_ref.at[at, :], kept_ref.at[at, :], sem.at[n]))
     for copy in copies:
         copy.start()
+    first.wait()
     total = None
     for n in range(steps):
         copies[n].wait()
@@ -65,19 +69,13 @@
     return pl.pallas_call(
         functools.partial(low_kernel, steps, n_col),
         out_shape=(half, half),
-        grid_spec=pltpu.PrefetchScalarGridSpec(
-            num_scalar_prefetch=1,
-            grid=(1,),
-            in_specs=[
-                pl.BlockSpec((tokens, depth), lambda i, s: (0, 0)),
-                pl.BlockSpec(memory_space=pl.ANY),
-            ],
-            out_specs=[VMEM] * 2,
-            scratch_shapes=[
-                pltpu.VMEM((depth, rank), f32),
-                pltpu.SemaphoreType.DMA((steps,)),
-            ],
-        ),
+        in_specs=[SMEM] + [pl.BlockSpec(memory_space=pl.ANY)] * 2,
+        out_specs=[VMEM] * 2,
+        scratch_shapes=[
+            pltpu.VMEM((tokens, depth), bf16),
+            pltpu.VMEM((depth, rank), f32),
+            pltpu.SemaphoreType.DMA((steps + 1,)),
+        ],
         compiler_params=pltpu.CompilerParams(vmem_limit_bytes=60 * MIB),
         cost_estimate=pl.CostEstimate(
             flops=4 * tokens * depth * rank, bytes_accessed=6 * depth * rank, transcendentals=0
@@ -112,6 +110,22 @@
         cost_estimate=pl.CostEstimate(flops=0, bytes_accessed=8 * rows * rank, transcendentals=0),
         name="turn_basis",
     )(basis)
+
+
+def add_kernel(first_ref, second_ref, out_ref):
+    out_ref[...] = first_ref[...] + second_ref[...]
+
+
+def add(first, second):
+    return pl.pallas_call(
+        add_kernel,
+        out_shape=jax.ShapeDtypeStruct(first.shape, f32),
+        in_specs=[VMEM] * 2,
+        out_specs=VMEM,
+        compiler_params=pltpu.CompilerParams(vmem_limit_bytes=4 * MIB),
+        cost_estimate=pl.CostEstimate(flops=0, bytes_accessed=0, transcendentals=0),
+        name="add",
+    )(first, second)
 
 
 def encode_kernel(*refs):
@@ -474,7 +488,7 @@
     table = np.array(table, np.int32)
     flat = after(flat.astype(jnp.uint32), other)
     where = lax.dynamic_slice(table, (flat, jnp.uint32(0)), (1, table.shape[1]))[0]
-    mine = mine + to_sibling(other)
+    mine = add(mine, to_sibling(other))
     arrived = [to_chip(mine, s) for s in range(1, chips)]
 
     grads = out_grads.T

time: 83.3 us -> 82.4 us (0.989)
  other arithmetic: 0.94 us -> 0.02 us
  local copies, waits for them, and re-layouts: 3.99 us -> 4.89 us
    add x1 -> x0, other arithmetic: 0.92 us -> none  [per_device(): mine = mine + to_sibling(other)]
    unnamed x8 -> x10, local copies, waits for them, and re-layouts: 2.2 us -> 3.1 us
    pallas_call x1, Pallas kernels: 4.31 us -> 3.43 us  [low_partial(): pl.pallas_call(functools.partial(low_kernel, steps, n_col), out_shape=(ha...]
  transfers between devices with their start and end apart: 24 -> 24, of which waited for: 11 -> 11; matrix products, arithmetic and copies ran while one was open for 1% -> 1% of each run, Pallas kernels for 21% -> 22%
where the time goes in v4:
time: 82.4 us; the launch traced here: 82.2 us
  Pallas kernels  39.8 us (48%)
  starting transfers between devices  22.4 us (27%)
  waiting for transfers between devices  14.4 us (17%)
  local copies, waits for them, and re-layouts  4.89 us (6%)
    pallas_call x1, Pallas kernels, update(): pl.pallas_call(functools.partial(update_kernel, float(hidden), len(parts)...  18.5 us
    pallas_call x5, Pallas kernels, project(): pl.pallas_call(functools.partial(project_kernel, len(grads), skip, step,...  12.9 us
    ppermute x4, waiting for transfers between devices, around(): return lax.ppermute(value, ('row', 'col'), pairs)  10.4 us
    ppermute x6, starting transfers between devices, to_chip(): return lax.ppermute(value, 'row', pairs)  8.67 us
    ppermute x4, starting transfers between devices, around(): return lax.ppermute(value, ('row', 'col'), pairs)  6.27 us
    ppermute x3, starting transfers between devices, per_device(): arrived = [lax.ppermute(sums, 'col', [(c, c ^ step) for c in range(n_col)])]  5.75 us
    pallas_call x1, Pallas kernels, low_partial(): pl.pallas_call(functools.partial(low_kernel, steps, n_col), out_shape=(ha...  3.43 us
    unnamed x10, local copies, waits for them, and re-layouts  3.1 us
  transfers between devices with their start and end apart: 24, of which 11 were waited for; matrix products, arithmetic and copies ran while one was open for 1% of the time, Pallas kernels for 22%

profile of v4, /device:TPU:0, one launch (start us, length us, event | category | flops | bytes accessed | tf_op | source)
XLA Modules:
  0.0 82.2 jit_solution(15976328238088375161)
XLA Ops:
  0.6 3.4 %low_partial.1 = (f32[128,256]{1,0:T(8,128)}, f32[128,256]{1,0:T(8,128)}) custom-call(s32[1]{0:T(128)} %bitcast.here_ref, bf16[128,2048]{1,0:T(8,128)(2,1)} %acts_ref.1, f32[2048,512]{1,0:T(8,128)} %basis_ref.2), custom_call_target="tpu_custom_call" | custom-call | flops 536870912 | bytes 6291456 | tf_op jit(solution)/shard_map/low_partial/pallas_call | solution.py:69
  6.7 2.9 %collective-permute-start.1 = (f32[128,256]{1,0:T(8,128)S(1)}, f32[128,256]{1,0:T(8,128)S(1)}, u32[]{:S(2)}, u32[]{:S(2)}) collective-permute-start(f32[128,256]{1,0:T(8,128)S(1)} %add.21.refs_0_), channel_id=1, source_target_pairs={{0,16},{8,24},{16,0},{24,8},{1,17},{9,25},{17,1},{25,9},{2,18},{10... | collective-permute-start | bytes 393224 | tf_op jit(solution)/shard_map/ppermute | solution.py:448
  10.3 1.4 %cut.1 = (bf16[1376,256]{1,0:T(8,128)(2,1)S(1)}, bf16[688,256]{1,0:T(8,128)(2,1)S(1)}, bf16[256,256]{1,0:T(8,128)(2,1)S(1)}, bf16[432,256]{1,0:T(8,128)(2,1)S(1)}) custom-call(s32[27]{0:T(128)S(1)} %dynamic-slice_bitcast_fusion.where_ref, bf16[2752,256]{1,0:T(8,128)(2,1)S(1)} %bitcast.7), custom_call_target="tpu_custom_call" | custom-call | bytes 2818048 | tf_op jit(solution)/shard_map/cut/pallas_call | solution.py:229
  11.8 1.7 %collective-permute-done.1.refs_1_ = f32[128,256]{1,0:T(8,128)S(1)} collective-permute-done((f32[128,256]{1,0:T(8,128)S(1)}, f32[128,256]{1,0:T(8,128)S(1)}, u32[]{:S(2)}, u32[]{:S(2)}) %collective-permute-start.1) | collective-permute-done | bytes 131104 | tf_op jit(solution)/shard_map/ppermute | solution.py:448
  13.6 1.8 %collective-permute-start.8 = (bf16[1376,256]{1,0:T(8,128)(2,1)S(1)}, bf16[1376,256]{1,0:T(8,128)(2,1)S(1)}, u32[]{:S(2)}, u32[]{:S(2)}) collective-permute-start(bf16[1376,256]{1,0:T(8,128)(2,1)S(1)} %get-tuple-element.80), channel_id=1, source_target_pairs={{0,16},{8,24},{16,0},{24,8},{1,17},{9,25},{17,1},{25,9},{2,18},{10... | collective-permute-start | bytes 2113544 | tf_op jit(solution)/shard_map/ppermute | solution.py:448
  16.2 1.6 %collective-permute-start.3 = (bf16[144,512]{1,0:T(8,128)(2,1)S(1)}, bf16[144,512]{1,0:T(8,128)(2,1)S(1)}, u32[]{:S(2)}, u32[]{:S(2)}) collective-permute-start(bf16[144,512]{1,0:T(8,128)(2,1)S(1)} %join.1.refs_0_), channel_id=1, source_target_pairs={{0,2},{2,4},{4,6},{6,7},{7,5},{5,3},{3,1},{1,0},{8,9},{10,8},{12,1... | collective-permute-start | bytes 442376 | tf_op jit(solution)/shard_map/ppermute | solution.py:455
  17.8 3.6 %collective-permute-done.3.refs_1_ = bf16[144,512]{1,0:T(8,128)(2,1)S(1)} collective-permute-done((bf16[144,512]{1,0:T(8,128)(2,1)S(1)}, bf16[144,512]{1,0:T(8,128)(2,1)S(1)}, u32[]{:S(2)}, u32[]{:S(2)}) %collective-permute-start.3) | collective-permute-done | bytes 147488 | tf_op jit(solution)/shard_map/ppermute | solution.py:455
  21.4 1.6 %collective-permute-start.4 = (bf16[144,512]{1,0:T(8,128)(2,1)S(1)}, bf16[144,512]{1,0:T(8,128)(2,1)S(1)}, u32[]{:S(2)}, u32[]{:S(2)}) collective-permute-start(bf16[144,512]{1,0:T(8,128)(2,1)S(1)} %collective-permute-done.3.refs_1_), channel_id=1, source_target_pairs={{0,2},{2,4},{4,6},{6,7},{7,5},{5,3},{3,1},{1,0},{8,9},{10,8},{12,1... | collective-permute-start | bytes 442376 | tf_op jit(solution)/shard_map/ppermute | solution.py:455
  22.9 2.2 %copy-done.1 = f32[2048,512]{1,0:T(8,128)S(1)} copy-done((f32[2048,512]{1,0:T(8,128)S(1)}, f32[2048,512]{1,0:T(8,128)}, u32[]{:S(2)}) %copy-start.1) | copy-done | bytes 4194328
  26.6 1.5 %collective-permute-start.6 = (bf16[144,512]{1,0:T(8,128)(2,1)S(1)}, bf16[144,512]{1,0:T(8,128)(2,1)S(1)}, u32[]{:S(2)}, u32[]{:S(2)}) collective-permute-start(bf16[144,512]{1,0:T(8,128)(2,1)S(1)} %collective-permute-done.4.refs_2_), channel_id=1, source_target_pairs={{0,2},{2,4},{4,6},{6,7},{7,5},{5,3},{3,1},{1,0},{8,9},{10,8},{12,1... | collective-permute-start | bytes 442376 | tf_op jit(solution)/shard_map/ppermute | solution.py:455
  28.1 3.6 %collective-permute-done.6.refs_3_ = bf16[144,512]{1,0:T(8,128)(2,1)S(1)} collective-permute-done((bf16[144,512]{1,0:T(8,128)(2,1)S(1)}, bf16[144,512]{1,0:T(8,128)(2,1)S(1)}, u32[]{:S(2)}, u32[]{:S(2)}) %collective-permute-start.6) | collective-permute-done | bytes 147488 | tf_op jit(solution)/shard_map/ppermute | solution.py:455
  31.8 1.7 %collective-permute-start.14 = (bf16[688,256]{1,0:T(8,128)(2,1)S(1)}, bf16[688,256]{1,0:T(8,128)(2,1)S(1)}, u32[]{:S(2)}, u32[]{:S(2)}) collective-permute-start(bf16[688,256]{1,0:T(8,128)(2,1)S(1)} %get-tuple-element.94), channel_id=1, source_target_pairs={{0,16},{8,24},{16,0},{24,8},{1,17},{9,25},{17,1},{25,9},{2,18},{10... | collective-permute-start | bytes 1056776 | tf_op jit(solution)/shard_map/ppermute | solution.py:448
  33.8 1.6 %collective-permute-start.9 = (bf16[144,512]{1,0:T(8,128)(2,1)S(1)}, bf16[144,512]{1,0:T(8,128)(2,1)S(1)}, u32[]{:S(2)}, u32[]{:S(2)}) collective-permute-start(bf16[144,512]{1,0:T(8,128)(2,1)S(1)} %collective-permute-done.6.refs_3_), channel_id=1, source_target_pairs={{0,2},{2,4},{4,6},{6,7},{7,5},{5,3},{3,1},{1,0},{8,9},{10,8},{12,1... | collective-permute-start | bytes 442376 | tf_op jit(solution)/shard_map/ppermute | solution.py:455
  35.9 3.0 %collective-permute-done.9.refs_4_ = bf16[144,512]{1,0:T(8,128)(2,1)S(1)} collective-permute-done((bf16[144,512]{1,0:T(8,128)(2,1)S(1)}, bf16[144,512]{1,0:T(8,128)(2,1)S(1)}, u32[]{:S(2)}, u32[]{:S(2)}) %collective-permute-start.9) | collective-permute-done | bytes 147488 | tf_op jit(solution)/shard_map/ppermute | solution.py:455
  39.4 1.7 %assemble.1 = (bf16[1024,512]{1,0:T(8,128)(2,1)S(1)}, bf16[1024,512]{1,0:T(8,128)(2,1)S(1)}) custom-call(s32[27]{0:T(128)S(1)} %dynamic-slice_bitcast_fusion.where_ref, bf16[144,512]{1,0:T(8,128)(2,1)S(1)} %join.1.refs_0_, bf16[144,512]{1,0:T(8,128)(2,1)S(1)} %collective-permute-done.3.refs_1_, bf16[144,512]{1,0:T(8,128)(2,1)S(1)} %collective-permute-done.4.refs_2_, ...), custom_call_target="tpu_custom_call" | custom-call | tf_op jit(solution)/shard_map/assemble/pallas_call | solution.py:204
  41.1 4.7 %project.5 = (f32[1376,512]{1,0:T(8,128)S(1)}, f32[2,768]{1,0:T(2,128)S(1)}, f32[1,512]{1,0:T(1,128)S(1)}, f32[1,512]{1,0:T(1,128)S(1)}) custom-call(s32[27]{0:T(128)S(1)} %dynamic-slice_bitcast_fusion.where_ref, bf16[1024,512]{1,0:T(8,128)(2,1)S(1)} %get-tuple-element.86.high_ref, bf16[1024,512]{1,0:T(8,128)(2,1)S(1)} %get-tuple-element.87.low_ref, ...), custom_call_target="tpu_custom_call" | custom-call | tf_op jit(solution)/shard_map/project/pallas_call | solution.py:299
  47.6 2.1 %project.6 = (f32[384,512]{1,0:T(8,128)S(1)}, f32[1,384]{1,0:T(1,128)S(1)}, f32[1,512]{1,0:T(1,128)}, f32[1,512]{1,0:T(1,128)S(1)}) custom-call(s32[27]{0:T(128)S(1)} %dynamic-slice_bitcast_fusion.where_ref, bf16[1024,512]{1,0:T(8,128)(2,1)S(1)} %get-tuple-element.86.high_ref, bf16[1024,512]{1,0:T(8,128)(2,1)S(1)} %get-tuple-element.87.low_ref, ...), custom_call_target="tpu_custom_call" | custom-call | tf_op jit(solution)/shard_map/project/pallas_call | solution.py:299
  50.9 1.5 %collective-permute-start.18 = (f32[1,512]{1,0:T(1,128)S(1)}, f32[1,512]{1,0:T(1,128)S(1)}, u32[]{:S(2)}, u32[]{:S(2)}) collective-permute-start(f32[1,512]{1,0:T(1,128)S(1)} %add.17), channel_id=1, source_target_pairs={{0,1},{1,0},{2,3},{3,2},{4,5},{5,4},{6,7},{7,6},{8,9},{9,8},{10,11... | collective-permute-start | bytes 6152 | tf_op jit(solution)/shard_map/ppermute | solution.py:560
  52.4 2.0 %project.7 = (f32[304,512]{1,0:T(8,128)S(1)}, f32[1,384]{1,0:T(1,128)S(1)}, f32[1,512]{1,0:T(1,128)}, f32[1,512]{1,0:T(1,128)S(1)}) custom-call(s32[27]{0:T(128)S(1)} %dynamic-slice_bitcast_fusion.where_ref, bf16[1024,512]{1,0:T(8,128)(2,1)S(1)} %get-tuple-element.86.high_ref, bf16[1024,512]{1,0:T(8,128)(2,1)S(1)} %get-tuple-element.87.low_ref, ...), custom_call_target="tpu_custom_call" | custom-call | tf_op jit(solution)/shard_map/project/pallas_call | solution.py:299
  54.5 1.6 %collective-permute-start.19 = (f32[1,512]{1,0:T(1,128)S(1)}, f32[1,512]{1,0:T(1,128)S(1)}, u32[]{:S(2)}, u32[]{:S(2)}) collective-permute-start(f32[1,512]{1,0:T(1,128)S(1)} %add.18), channel_id=1, source_target_pairs={{0,2},{1,3},{2,0},{3,1},{4,6},{5,7},{6,4},{7,5},{8,10},{9,11},{10,... | collective-permute-start | bytes 6152 | tf_op jit(solution)/shard_map/ppermute | solution.py:560
  56.1 1.9 %project.8 = (f32[256,512]{1,0:T(8,128)S(1)}, f32[1,256]{1,0:T(1,128)S(1)}, f32[1,512]{1,0:T(1,128)}, f32[1,512]{1,0:T(1,128)S(1)}) custom-call(s32[27]{0:T(128)S(1)} %dynamic-slice_bitcast_fusion.where_ref, bf16[1024,512]{1,0:T(8,128)(2,1)S(1)} %get-tuple-element.86.high_ref, bf16[1024,512]{1,0:T(8,128)(2,1)S(1)} %get-tuple-element.87.low_ref, ...), custom_call_target="tpu_custom_call" | custom-call | tf_op jit(solution)/shard_map/project/pallas_call | solution.py:299
  58.2 2.7 %collective-permute-start.21 = (f32[1,512]{1,0:T(1,128)S(1)}, f32[1,512]{1,0:T(1,128)S(1)}, u32[]{:S(2)}, u32[]{:S(2)}) collective-permute-start(f32[1,512]{1,0:T(1,128)S(1)} %add.19), channel_id=1, source_target_pairs={{0,4},{1,5},{2,6},{3,7},{4,0},{5,1},{6,2},{7,3},{8,12},{9,13},{10,... | collective-permute-start | bytes 6152 | tf_op jit(solution)/shard_map/ppermute | solution.py:560
  60.8 2.2 %project.9 = (f32[432,512]{1,0:T(8,128)S(1)}, f32[1,512]{1,0:T(1,128)S(1)}, f32[1,512]{1,0:T(1,128)}, f32[1,512]{1,0:T(1,128)S(1)}) custom-call(s32[27]{0:T(128)S(1)} %dynamic-slice_bitcast_fusion.where_ref, bf16[1024,512]{1,0:T(8,128)(2,1)S(1)} %get-tuple-element.86.high_ref, bf16[1024,512]{1,0:T(8,128)(2,1)S(1)} %get-tuple-element.87.low_ref, ...), custom_call_target="tpu_custom_call" | custom-call | tf_op jit(solution)/shard_map/project/pallas_call | solution.py:299
  63.1 18.5 %update.1 = (f32[2752,2048]{1,0:T(8,128)}, f32[1,128]{1,0:T(1,128)}, f32[4,688]{1,0:T(4,128)S(1)}) custom-call(s32[27]{0:T(128)S(1)} %dynamic-slice_bitcast_fusion.where_ref, f32[1,512]{1,0:T(1,128)S(1)} %add.20.sums_ref, f32[1,512]{1,0:T(1,128)S(1)} %get-tuple-element.115.most_ref, bf16[512,2048]{1,0:T(8,128)(2,1)S(1)} %get-tuple-element.76.high_ref, ...), custom_call_target="tpu_custom_call" | custom-call | flops 11542724608 | bytes 22544384 | tf_op jit(solution)/shard_map/update/pallas_call | solution.py:387
  (55 shorter events, 11.0 us)
Async XLA Ops:
  4.1 1.7 %collective-permute-start = (f32[128,256]{1,0:T(8,128)}, f32[128,256]{1,0:T(8,128)S(1)}, u32[]{:S(2)}, u32[]{:S(2)}) collective-permute-start(f32[128,256]{1,0:T(8,128)} %get-tuple-element.66), channel_id=1, source_target_pairs={{0,8},{8,0},{16,24},{24,16},{1,9},{9,1},{17,25},{25,17},{2,10},{10... | collective-permute-start | bytes 393224 | tf_op jit(solution)/shard_map/ppermute | solution.py:444
  6.7 6.7 %collective-permute-start.1 = (f32[128,256]{1,0:T(8,128)S(1)}, f32[128,256]{1,0:T(8,128)S(1)}, u32[]{:S(2)}, u32[]{:S(2)}) collective-permute-start(f32[128,256]{1,0:T(8,128)S(1)} %add.21.refs_0_), channel_id=1, source_target_pairs={{0,16},{8,24},{16,0},{24,8},{1,17},{9,25},{17,1},{25,9},{2,18},{10... | collective-permute-start | bytes 393224 | tf_op jit(solution)/shard_map/ppermute | solution.py:448
  13.5 1.9 %collective-permute-start.2 = (bf16[144,256]{1,0:T(8,128)(2,1)S(1)}, bf16[144,256]{1,0:T(8,128)(2,1)S(1)}, u32[]{:S(2)}, u32[]{:S(2)}) collective-permute-start(bf16[144,256]{1,0:T(8,128)(2,1)S(1)} %encode.1.mine_ref), channel_id=1, source_target_pairs={{0,8},{8,0},{16,24},{24,16},{1,9},{9,1},{17,25},{25,17},{2,10},{10... | collective-permute-start | bytes 221192 | tf_op jit(solution)/shard_map/ppermute | solution.py:444
  13.6 18.2 %collective-permute-start.8 = (bf16[1376,256]{1,0:T(8,128)(2,1)S(1)}, bf16[1376,256]{1,0:T(8,128)(2,1)S(1)}, u32[]{:S(2)}, u32[]{:S(2)}) collective-permute-start(bf16[1376,256]{1,0:T(8,128)(2,1)S(1)} %get-tuple-element.80), channel_id=1, source_target_pairs={{0,16},{8,24},{16,0},{24,8},{1,17},{9,25},{17,1},{25,9},{2,18},{10... | collective-permute-start | bytes 2113544 | tf_op jit(solution)/shard_map/ppermute | solution.py:448
  16.0 25.1 %collective-permute-start.11 = (bf16[2752,256]{1,0:T(8,128)(2,1)S(1)}, bf16[2752,256]{1,0:T(8,128)(2,1)S(1)}, u32[]{:S(2)}, u32[]{:S(2)}) collective-permute-start(bf16[2752,256]{1,0:T(8,128)(2,1)S(1)} %bitcast.8), channel_id=1, source_target_pairs={{0,8},{8,0},{16,24},{24,16},{1,9},{9,1},{17,25},{25,17},{2,10},{10... | collective-permute-start | bytes 4227080 | tf_op jit(solution)/shard_map/ppermute | solution.py:444
  16.2 5.1 %collective-permute-start.3 = (bf16[144,512]{1,0:T(8,128)(2,1)S(1)}, bf16[144,512]{1,0:T(8,128)(2,1)S(1)}, u32[]{:S(2)}, u32[]{:S(2)}) collective-permute-start(bf16[144,512]{1,0:T(8,128)(2,1)S(1)} %join.1.refs_0_), channel_id=1, source_target_pairs={{0,2},{2,4},{4,6},{6,7},{7,5},{5,3},{3,1},{1,0},{8,9},{10,8},{12,1... | collective-permute-start | bytes 442376 | tf_op jit(solution)/shard_map/ppermute | solution.py:455
  21.4 4.9 %collective-permute-start.5 = (bf16[144,512]{1,0:T(8,128)(2,1)S(1)}, bf16[144,512]{1,0:T(8,128)(2,1)S(1)}, u32[]{:S(2)}, u32[]{:S(2)}) collective-permute-start(bf16[144,512]{1,0:T(8,128)(2,1)S(1)} %collective-permute-done.3.refs_1_), channel_id=1, source_target_pairs={{0,8},{8,0},{16,24},{24,16},{1,9},{9,1},{17,25},{25,17},{2,10},{10... | collective-permute-start | bytes 442376 | tf_op jit(solution)/shard_map/ppermute | solution.py:444
  21.4 5.1 %collective-permute-start.4 = (bf16[144,512]{1,0:T(8,128)(2,1)S(1)}, bf16[144,512]{1,0:T(8,128)(2,1)S(1)}, u32[]{:S(2)}, u32[]{:S(2)}) collective-permute-start(bf16[144,512]{1,0:T(8,128)(2,1)S(1)} %collective-permute-done.3.refs_1_), channel_id=1, source_target_pairs={{0,2},{2,4},{4,6},{6,7},{7,5},{5,3},{3,1},{1,0},{8,9},{10,8},{12,1... | collective-permute-start | bytes 442376 | tf_op jit(solution)/shard_map/ppermute | solution.py:455
  26.5 1.6 %collective-permute-start.7 = (bf16[144,512]{1,0:T(8,128)(2,1)S(1)}, bf16[144,512]{1,0:T(8,128)(2,1)S(1)}, u32[]{:S(2)}, u32[]{:S(2)}) collective-permute-start(bf16[144,512]{1,0:T(8,128)(2,1)S(1)} %collective-permute-done.4.refs_2_), channel_id=1, source_target_pairs={{0,8},{8,0},{16,24},{24,16},{1,9},{9,1},{17,25},{25,17},{2,10},{10... | collective-permute-start | bytes 442376 | tf_op jit(solution)/shard_map/ppermute | solution.py:444
  26.6 5.1 %collective-permute-start.6 = (bf16[144,512]{1,0:T(8,128)(2,1)S(1)}, bf16[144,512]{1,0:T(8,128)(2,1)S(1)}, u32[]{:S(2)}, u32[]{:S(2)}) collective-permute-start(bf16[144,512]{1,0:T(8,128)(2,1)S(1)} %collective-permute-done.4.refs_2_), channel_id=1, source_target_pairs={{0,2},{2,4},{4,6},{6,7},{7,5},{5,3},{3,1},{1,0},{8,9},{10,8},{12,1... | collective-permute-start | bytes 442376 | tf_op jit(solution)/shard_map/ppermute | solution.py:455
  31.8 9.3 %collective-permute-start.12 = (bf16[1376,256]{1,0:T(8,128)(2,1)S(1)}, bf16[1376,256]{1,0:T(8,128)(2,1)S(1)}, u32[]{:S(2)}, u32[]{:S(2)}) collective-permute-start(bf16[1376,256]{1,0:T(8,128)(2,1)S(1)} %collective-permute-done.8.refs_2_), channel_id=1, source_target_pairs={{0,8},{8,0},{16,24},{24,16},{1,9},{9,1},{17,25},{25,17},{2,10},{10... | collective-permute-start | bytes 2113544 | tf_op jit(solution)/shard_map/ppermute | solution.py:444
  31.8 14.0 %collective-permute-start.14 = (bf16[688,256]{1,0:T(8,128)(2,1)S(1)}, bf16[688,256]{1,0:T(8,128)(2,1)S(1)}, u32[]{:S(2)}, u32[]{:S(2)}) collective-permute-start(bf16[688,256]{1,0:T(8,128)(2,1)S(1)} %get-tuple-element.94), channel_id=1, source_target_pairs={{0,16},{8,24},{16,0},{24,8},{1,17},{9,25},{17,1},{25,9},{2,18},{10... | collective-permute-start | bytes 1056776 | tf_op jit(solution)/shard_map/ppermute | solution.py:448
  33.6 1.8 %collective-permute-start.10 = (bf16[144,512]{1,0:T(8,128)(2,1)S(1)}, bf16[144,512]{1,0:T(8,128)(2,1)S(1)}, u32[]{:S(2)}, u32[]{:S(2)}) collective-permute-start(bf16[144,512]{1,0:T(8,128)(2,1)S(1)} %collective-permute-done.6.refs_3_), channel_id=1, source_target_pairs={{0,8},{8,0},{16,24},{24,16},{1,9},{9,1},{17,25},{25,17},{2,10},{10... | collective-permute-start | bytes 442376 | tf_op jit(solution)/shard_map/ppermute | solution.py:444
  33.8 5.1 %collective-permute-start.9 = (bf16[144,512]{1,0:T(8,128)(2,1)S(1)}, bf16[144,512]{1,0:T(8,128)(2,1)S(1)}, u32[]{:S(2)}, u32[]{:S(2)}) collective-permute-start(bf16[144,512]{1,0:T(8,128)(2,1)S(1)} %collective-permute-done.6.refs_3_), channel_id=1, source_target_pairs={{0,2},{2,4},{4,6},{6,7},{7,5},{5,3},{3,1},{1,0},{8,9},{10,8},{12,1... | collective-permute-start | bytes 442376 | tf_op jit(solution)/shard_map/ppermute | solution.py:455
  35.4 10.4 %collective-permute-start.15 = (bf16[256,256]{1,0:T(8,128)(2,1)S(1)}, bf16[256,256]{1,0:T(8,128)(2,1)S(1)}, u32[]{:S(2)}, u32[]{:S(2)}) collective-permute-start(bf16[256,256]{1,0:T(8,128)(2,1)S(1)} %get-tuple-element.96), channel_id=1, source_target_pairs={{0,16},{8,24},{16,0},{24,8},{1,17},{9,25},{17,1},{25,9},{2,18},{10... | collective-permute-start | bytes 393224 | tf_op jit(solution)/shard_map/ppermute | solution.py:448
  38.9 2.1 %collective-permute-start.13 = (f32[1,128]{1,0:T(1,128)S(1)}, f32[1,128]{1,0:T(1,128)S(1)}, u32[]{:S(2)}, u32[]{:S(2)}) collective-permute-start(f32[1,128]{1,0:T(1,128)S(1)} %bitcast.14), channel_id=1, source_target_pairs={{0,8},{8,0},{16,24},{24,16},{1,9},{9,1},{17,25},{25,17},{2,10},{10... | collective-permute-start | bytes 1544 | tf_op jit(solution)/shard_map/ppermute | solution.py:444
  45.8 1.8 %collective-permute-start.17 = (bf16[688,256]{1,0:T(8,128)(2,1)S(1)}, bf16[688,256]{1,0:T(8,128)(2,1)S(1)}, u32[]{:S(2)}, u32[]{:S(2)}) collective-permute-start(bf16[688,256]{1,0:T(8,128)(2,1)S(1)} %collective-permute-done.14.refs_2_), channel_id=1, source_target_pairs={{0,8},{8,0},{16,24},{24,16},{1,9},{9,1},{17,25},{25,17},{2,10},{10... | collective-permute-start | bytes 1056776 | tf_op jit(solution)/shard_map/ppermute | solution.py:444
  46.3 3.6 %collective-permute-start.16 = (f32[1,512]{1,0:T(1,128)S(1)}, f32[1,512]{1,0:T(1,128)S(1)}, u32[]{:S(2)}, u32[]{:S(2)}) collective-permute-start(f32[1,512]{1,0:T(1,128)S(1)} %get-tuple-element.97), channel_id=1, source_target_pairs={{0,16},{8,24},{16,0},{24,8},{1,17},{9,25},{17,1},{25,9},{2,18},{10... | collective-permute-start | bytes 6152 | tf_op jit(solution)/shard_map/ppermute | solution.py:448
  49.9 8.2 %collective-permute-start.22 = (bf16[432,256]{1,0:T(8,128)(2,1)S(1)}, bf16[432,256]{1,0:T(8,128)(2,1)S(1)}, u32[]{:S(2)}, u32[]{:S(2)}) collective-permute-start(bf16[432,256]{1,0:T(8,128)(2,1)S(1)} %get-tuple-element.111), channel_id=1, source_target_pairs={{0,16},{8,24},{16,0},{24,8},{1,17},{9,25},{17,1},{25,9},{2,18},{10... | collective-permute-start | bytes 663560 | tf_op jit(solution)/shard_map/ppermute | solution.py:448
  50.9 5.2 %collective-permute-start.20 = (bf16[256,256]{1,0:T(8,128)(2,1)S(1)}, bf16[256,256]{1,0:T(8,128)(2,1)S(1)}, u32[]{:S(2)}, u32[]{:S(2)}) collective-permute-start(bf16[256,256]{1,0:T(8,128)(2,1)S(1)} %collective-permute-done.15.refs_2_), channel_id=1, source_target_pairs={{0,8},{8,0},{16,24},{24,16},{1,9},{9,1},{17,25},{25,17},{2,10},{10... | collective-permute-start | bytes 393224 | tf_op jit(solution)/shard_map/ppermute | solution.py:444
  50.9 3.6 %collective-permute-start.18 = (f32[1,512]{1,0:T(1,128)S(1)}, f32[1,512]{1,0:T(1,128)S(1)}, u32[]{:S(2)}, u32[]{:S(2)}) collective-permute-start(f32[1,512]{1,0:T(1,128)S(1)} %add.17), channel_id=1, source_target_pairs={{0,1},{1,0},{2,3},{3,2},{4,5},{5,4},{6,7},{7,6},{8,9},{9,8},{10,11... | collective-permute-start | bytes 6152 | tf_op jit(solution)/shard_map/ppermute | solution.py:560
  54.5 3.6 %collective-permute-start.19 = (f32[1,512]{1,0:T(1,128)S(1)}, f32[1,512]{1,0:T(1,128)S(1)}, u32[]{:S(2)}, u32[]{:S(2)}) collective-permute-start(f32[1,512]{1,0:T(1,128)S(1)} %add.18), channel_id=1, source_target_pairs={{0,2},{1,3},{2,0},{3,1},{4,6},{5,7},{6,4},{7,5},{8,10},{9,11},{10,... | collective-permute-start | bytes 6152 | tf_op jit(solution)/shard_map/ppermute | solution.py:560
  58.1 2.7 %collective-permute-start.23 = (bf16[432,256]{1,0:T(8,128)(2,1)S(1)}, bf16[432,256]{1,0:T(8,128)(2,1)S(1)}, u32[]{:S(2)}, u32[]{:S(2)}) collective-permute-start(bf16[432,256]{1,0:T(8,128)(2,1)S(1)} %collective-permute-done.22.refs_2_), channel_id=1, source_target_pairs={{0,8},{8,0},{16,24},{24,16},{1,9},{9,1},{17,25},{25,17},{2,10},{10... | collective-permute-start | bytes 663560 | tf_op jit(solution)/shard_map/ppermute | solution.py:444
  58.2 4.9 %collective-permute-start.21 = (f32[1,512]{1,0:T(1,128)S(1)}, f32[1,512]{1,0:T(1,128)S(1)}, u32[]{:S(2)}, u32[]{:S(2)}) collective-permute-start(f32[1,512]{1,0:T(1,128)S(1)} %add.19), channel_id=1, source_target_pairs={{0,4},{1,5},{2,6},{3,7},{4,0},{5,1},{6,2},{7,3},{8,12},{9,13},{10,... | collective-permute-start | bytes 6152 | tf_op jit(solution)/shard_map/ppermute | solution.py:560
  (5 other events, 59.8 us)

commit v5 on v4

--- a/solution.py
+++ b/solution.py
@@ -247,13 +247,6 @@
     out_ref, colnext_ref, sums_ref, top_ref = refs[len(refs) - 4 :]
     grads, moments = refs[:pieces], refs[pieces : len(refs) - 4]
     rows, rank = out_ref.shape
-    tokens = grads[0].shape[1]
-    order = [
-        pl.ds(pl.multiple_of(where_ref[rows_at + p] * tokens, tokens), tokens)
-        for p in range(pieces)
-    ]
-    high = jnp.concatenate([high_ref[at, :] for at in order], axis=0)
-    low = jnp.concatenate([low_ref[at, :] for at in order], axis=0)
     sums = jnp.zeros((1, rank), f32)
     if first:
         lanes = moments[0].shape[1]
@@ -270,8 +263,8 @@
         grad = jnp.concatenate(
             [g[at, :] for g in grads[:2]] + [g[there, :] for g in grads[2:]], axis=1
         )
-        total = jnp.dot(grad, high, preferred_element_type=f32) + jnp.dot(
-            grad, low, preferred_element_type=f32
+        total = jnp.dot(grad, high_ref[...], preferred_element_type=f32) + jnp.dot(
+            grad, low_ref[...], preferred_element_type=f32
         )
         squares = total * total
         sums = sums + jnp.sum(squares, axis=0, keepdims=True)
@@ -469,7 +462,10 @@
             order = [p] + [p - way * s for s in range(1, hops + 1)]
             order += [p + way * s for s in range(1, hops + 1) if 2 * s != n_col]
             blocks_at = len(entry)
-            entry += [ring[i % n_col] for i in order]
+            each = n_col // n_row
+            sources = entry[2:]
+            order = [ring[i % n_col] for i in order]
+            entry += [sources.index(block // each) * each + block % each for block in order]
             starts_at = len(entry)
             entry += [((x + j) % chips * width + at) // 16 for j, at, *_ in jobs]
             sends_at = len(entry)

time: 82.4 us -> 82.4 us (level)
  no operation moved by 1% of the time
where the time goes in v5:
time: 82.4 us; the launch traced here: 82.2 us
  Pallas kernels  39.7 us (48%)
  starting transfers between devices  22.4 us (27%)
  waiting for transfers between devices  14.4 us (17%)
  local copies, waits for them, and re-layouts  4.89 us (6%)
    pallas_call x1, Pallas kernels, update(): pl.pallas_call(functools.partial(update_kernel, float(hidden), len(parts)...  18.5 us
    pallas_call x5, Pallas kernels, project(): pl.pallas_call(functools.partial(project_kernel, len(grads), skip, step,...  12.8 us
    ppermute x4, waiting for transfers between devices, around(): return lax.ppermute(value, ('row', 'col'), pairs)  10.4 us
    ppermute x6, starting transfers between devices, to_chip(): return lax.ppermute(value, 'row', pairs)  8.67 us
    ppermute x4, starting transfers between devices, around(): return lax.ppermute(value, ('row', 'col'), pairs)  6.27 us
    ppermute x3, starting transfers between devices, per_device(): arrived = [lax.ppermute(sums, 'col', [(c, c ^ step) for c in range(n_col)])]  5.76 us
    pallas_call x1, Pallas kernels, low_partial(): pl.pallas_call(functools.partial(low_kernel, steps, n_col), out_shape=(ha...  3.43 us
    unnamed x10, local copies, waits for them, and re-layouts  3.1 us
  transfers between devices with their start and end apart: 24, of which 11 were waited for; matrix products, arithmetic and copies ran while one was open for 1% of the time, Pallas kernels for 22%

profile of v5, /device:TPU:0, one launch (start us, length us, event | category | flops | bytes accessed | tf_op | source)
XLA Modules:
  0.0 82.2 jit_solution(13561021983994529884)
XLA Ops:
  0.6 3.4 %low_partial.1 = (f32[128,256]{1,0:T(8,128)}, f32[128,256]{1,0:T(8,128)}) custom-call(s32[1]{0:T(128)} %bitcast.here_ref, bf16[128,2048]{1,0:T(8,128)(2,1)} %acts_ref.1, f32[2048,512]{1,0:T(8,128)} %basis_ref.2), custom_call_target="tpu_custom_call" | custom-call | flops 536870912 | bytes 6291456 | tf_op jit(solution)/shard_map/low_partial/pallas_call | solution.py:69
  6.7 2.9 %collective-permute-start.1 = (f32[128,256]{1,0:T(8,128)S(1)}, f32[128,256]{1,0:T(8,128)S(1)}, u32[]{:S(2)}, u32[]{:S(2)}) collective-permute-start(f32[128,256]{1,0:T(8,128)S(1)} %add.21.refs_0_), channel_id=1, source_target_pairs={{0,16},{8,24},{16,0},{24,8},{1,17},{9,25},{17,1},{25,9},{2,18},{10... | collective-permute-start | bytes 393224 | tf_op jit(solution)/shard_map/ppermute | solution.py:441
  10.3 1.4 %cut.1 = (bf16[1376,256]{1,0:T(8,128)(2,1)S(1)}, bf16[688,256]{1,0:T(8,128)(2,1)S(1)}, bf16[256,256]{1,0:T(8,128)(2,1)S(1)}, bf16[432,256]{1,0:T(8,128)(2,1)S(1)}) custom-call(s32[27]{0:T(128)S(1)} %dynamic-slice_bitcast_fusion.where_ref, bf16[2752,256]{1,0:T(8,128)(2,1)S(1)} %bitcast.7), custom_call_target="tpu_custom_call" | custom-call | bytes 2818048 | tf_op jit(solution)/shard_map/cut/pallas_call | solution.py:229
  11.8 1.7 %collective-permute-done.1.refs_1_ = f32[128,256]{1,0:T(8,128)S(1)} collective-permute-done((f32[128,256]{1,0:T(8,128)S(1)}, f32[128,256]{1,0:T(8,128)S(1)}, u32[]{:S(2)}, u32[]{:S(2)}) %collective-permute-start.1) | collective-permute-done | bytes 131104 | tf_op jit(solution)/shard_map/ppermute | solution.py:441
  13.6 1.8 %collective-permute-start.8 = (bf16[1376,256]{1,0:T(8,128)(2,1)S(1)}, bf16[1376,256]{1,0:T(8,128)(2,1)S(1)}, u32[]{:S(2)}, u32[]{:S(2)}) collective-permute-start(bf16[1376,256]{1,0:T(8,128)(2,1)S(1)} %get-tuple-element.80), channel_id=1, source_target_pairs={{0,16},{8,24},{16,0},{24,8},{1,17},{9,25},{17,1},{25,9},{2,18},{10... | collective-permute-start | bytes 2113544 | tf_op jit(solution)/shard_map/ppermute | solution.py:441
  16.2 1.6 %collective-permute-start.3 = (bf16[144,512]{1,0:T(8,128)(2,1)S(1)}, bf16[144,512]{1,0:T(8,128)(2,1)S(1)}, u32[]{:S(2)}, u32[]{:S(2)}) collective-permute-start(bf16[144,512]{1,0:T(8,128)(2,1)S(1)} %join.1.refs_0_), channel_id=1, source_target_pairs={{0,2},{2,4},{4,6},{6,7},{7,5},{5,3},{3,1},{1,0},{8,9},{10,8},{12,1... | collective-permute-start | bytes 442376 | tf_op jit(solution)/shard_map/ppermute | solution.py:448
  17.8 3.6 %collective-permute-done.3.refs_1_ = bf16[144,512]{1,0:T(8,128)(2,1)S(1)} collective-permute-done((bf16[144,512]{1,0:T(8,128)(2,1)S(1)}, bf16[144,512]{1,0:T(8,128)(2,1)S(1)}, u32[]{:S(2)}, u32[]{:S(2)}) %collective-permute-start.3) | collective-permute-done | bytes 147488 | tf_op jit(solution)/shard_map/ppermute | solution.py:448
  21.4 1.6 %collective-permute-start.4 = (bf16[144,512]{1,0:T(8,128)(2,1)S(1)}, bf16[144,512]{1,0:T(8,128)(2,1)S(1)}, u32[]{:S(2)}, u32[]{:S(2)}) collective-permute-start(bf16[144,512]{1,0:T(8,128)(2,1)S(1)} %collective-permute-done.3.refs_1_), channel_id=1, source_target_pairs={{0,2},{2,4},{4,6},{6,7},{7,5},{5,3},{3,1},{1,0},{8,9},{10,8},{12,1... | collective-permute-start | bytes 442376 | tf_op jit(solution)/shard_map/ppermute | solution.py:448
  22.9 2.2 %copy-done.1 = f32[2048,512]{1,0:T(8,128)S(1)} copy-done((f32[2048,512]{1,0:T(8,128)S(1)}, f32[2048,512]{1,0:T(8,128)}, u32[]{:S(2)}) %copy-start.1) | copy-done | bytes 4194328
  26.6 1.5 %collective-permute-start.6 = (bf16[144,512]{1,0:T(8,128)(2,1)S(1)}, bf16[144,512]{1,0:T(8,128)(2,1)S(1)}, u32[]{:S(2)}, u32[]{:S(2)}) collective-permute-start(bf16[144,512]{1,0:T(8,128)(2,1)S(1)} %collective-permute-done.4.refs_2_), channel_id=1, source_target_pairs={{0,2},{2,4},{4,6},{6,7},{7,5},{5,3},{3,1},{1,0},{8,9},{10,8},{12,1... | collective-permute-start | bytes 442376 | tf_op jit(solution)/shard_map/ppermute | solution.py:448
  28.1 3.6 %collective-permute-done.6.refs_3_ = bf16[144,512]{1,0:T(8,128)(2,1)S(1)} collective-permute-done((bf16[144,512]{1,0:T(8,128)(2,1)S(1)}, bf16[144,512]{1,0:T(8,128)(2,1)S(1)}, u32[]{:S(2)}, u32[]{:S(2)}) %collective-permute-start.6) | collective-permute-done | bytes 147488 | tf_op jit(solution)/shard_map/ppermute | solution.py:448
  31.8 1.7 %collective-permute-start.14 = (bf16[688,256]{1,0:T(8,128)(2,1)S(1)}, bf16[688,256]{1,0:T(8,128)(2,1)S(1)}, u32[]{:S(2)}, u32[]{:S(2)}) collective-permute-start(bf16[688,256]{1,0:T(8,128)(2,1)S(1)} %get-tuple-element.94), channel_id=1, source_target_pairs={{0,16},{8,24},{16,0},{24,8},{1,17},{9,25},{17,1},{25,9},{2,18},{10... | collective-permute-start | bytes 1056776 | tf_op jit(solution)/shard_map/ppermute | solution.py:441
  33.8 1.6 %collective-permute-start.9 = (bf16[144,512]{1,0:T(8,128)(2,1)S(1)}, bf16[144,512]{1,0:T(8,128)(2,1)S(1)}, u32[]{:S(2)}, u32[]{:S(2)}) collective-permute-start(bf16[144,512]{1,0:T(8,128)(2,1)S(1)} %collective-permute-done.6.refs_3_), channel_id=1, source_target_pairs={{0,2},{2,4},{4,6},{6,7},{7,5},{5,3},{3,1},{1,0},{8,9},{10,8},{12,1... | collective-permute-start | bytes 442376 | tf_op jit(solution)/shard_map/ppermute | solution.py:448
  35.9 3.0 %collective-permute-done.9.refs_4_ = bf16[144,512]{1,0:T(8,128)(2,1)S(1)} collective-permute-done((bf16[144,512]{1,0:T(8,128)(2,1)S(1)}, bf16[144,512]{1,0:T(8,128)(2,1)S(1)}, u32[]{:S(2)}, u32[]{:S(2)}) %collective-permute-start.9) | collective-permute-done | bytes 147488 | tf_op jit(solution)/shard_map/ppermute | solution.py:448
  39.4 1.7 %assemble.1 = (bf16[1024,512]{1,0:T(8,128)(2,1)S(1)}, bf16[1024,512]{1,0:T(8,128)(2,1)S(1)}) custom-call(s32[27]{0:T(128)S(1)} %dynamic-slice_bitcast_fusion.where_ref, bf16[144,512]{1,0:T(8,128)(2,1)S(1)} %join.1.refs_0_, bf16[144,512]{1,0:T(8,128)(2,1)S(1)} %collective-permute-done.3.refs_1_, bf16[144,512]{1,0:T(8,128)(2,1)S(1)} %collective-permute-done.4.refs_2_, ...), custom_call_target="tpu_custom_call" | custom-call | tf_op jit(solution)/shard_map/assemble/pallas_call | solution.py:204
  41.1 4.6 %project.5 = (f32[1376,512]{1,0:T(8,128)S(1)}, f32[2,768]{1,0:T(2,128)S(1)}, f32[1,512]{1,0:T(1,128)S(1)}, f32[1,512]{1,0:T(1,128)S(1)}) custom-call(s32[27]{0:T(128)S(1)} %dynamic-slice_bitcast_fusion.where_ref, bf16[1024,512]{1,0:T(8,128)(2,1)S(1)} %get-tuple-element.86.high_ref, bf16[1024,512]{1,0:T(8,128)(2,1)S(1)} %get-tuple-element.87.low_ref, ...), custom_call_target="tpu_custom_call" | custom-call | tf_op jit(solution)/shard_map/project/pallas_call | solution.py:292
  47.6 2.1 %project.6 = (f32[384,512]{1,0:T(8,128)S(1)}, f32[1,384]{1,0:T(1,128)S(1)}, f32[1,512]{1,0:T(1,128)}, f32[1,512]{1,0:T(1,128)S(1)}) custom-call(s32[27]{0:T(128)S(1)} %dynamic-slice_bitcast_fusion.where_ref, bf16[1024,512]{1,0:T(8,128)(2,1)S(1)} %get-tuple-element.86.high_ref, bf16[1024,512]{1,0:T(8,128)(2,1)S(1)} %get-tuple-element.87.low_ref, ...), custom_call_target="tpu_custom_call" | custom-call | tf_op jit(solution)/shard_map/project/pallas_call | solution.py:292
  50.9 1.5 %collective-permute-start.18 = (f32[1,512]{1,0:T(1,128)S(1)}, f32[1,512]{1,0:T(1,128)S(1)}, u32[]{:S(2)}, u32[]{:S(2)}) collective-permute-start(f32[1,512]{1,0:T(1,128)S(1)} %add.17), channel_id=1, source_target_pairs={{0,1},{1,0},{2,3},{3,2},{4,5},{5,4},{6,7},{7,6},{8,9},{9,8},{10,11... | collective-permute-start | bytes 6152 | tf_op jit(solution)/shard_map/ppermute | solution.py:556
  52.4 2.0 %project.7 = (f32[304,512]{1,0:T(8,128)S(1)}, f32[1,384]{1,0:T(1,128)S(1)}, f32[1,512]{1,0:T(1,128)}, f32[1,512]{1,0:T(1,128)S(1)}) custom-call(s32[27]{0:T(128)S(1)} %dynamic-slice_bitcast_fusion.where_ref, bf16[1024,512]{1,0:T(8,128)(2,1)S(1)} %get-tuple-element.86.high_ref, bf16[1024,512]{1,0:T(8,128)(2,1)S(1)} %get-tuple-element.87.low_ref, ...), custom_call_target="tpu_custom_call" | custom-call | tf_op jit(solution)/shard_map/project/pallas_call | solution.py:292
  54.5 1.6 %collective-permute-start.19 = (f32[1,512]{1,0:T(1,128)S(1)}, f32[1,512]{1,0:T(1,128)S(1)}, u32[]{:S(2)}, u32[]{:S(2)}) collective-permute-start(f32[1,512]{1,0:T(1,128)S(1)} %add.18), channel_id=1, source_target_pairs={{0,2},{1,3},{2,0},{3,1},{4,6},{5,7},{6,4},{7,5},{8,10},{9,11},{10,... | collective-permute-start | bytes 6152 | tf_op jit(solution)/shard_map/ppermute | solution.py:556
  56.1 1.9 %project.8 = (f32[256,512]{1,0:T(8,128)S(1)}, f32[1,256]{1,0:T(1,128)S(1)}, f32[1,512]{1,0:T(1,128)}, f32[1,512]{1,0:T(1,128)S(1)}) custom-call(s32[27]{0:T(128)S(1)} %dynamic-slice_bitcast_fusion.where_ref, bf16[1024,512]{1,0:T(8,128)(2,1)S(1)} %get-tuple-element.86.high_ref, bf16[1024,512]{1,0:T(8,128)(2,1)S(1)} %get-tuple-element.87.low_ref, ...), custom_call_target="tpu_custom_call" | custom-call | tf_op jit(solution)/shard_map/project/pallas_call | solution.py:292
  58.2 2.7 %collective-permute-start.21 = (f32[1,512]{1,0:T(1,128)S(1)}, f32[1,512]{1,0:T(1,128)S(1)}, u32[]{:S(2)}, u32[]{:S(2)}) collective-permute-start(f32[1,512]{1,0:T(1,128)S(1)} %add.19), channel_id=1, source_target_pairs={{0,4},{1,5},{2,6},{3,7},{4,0},{5,1},{6,2},{7,3},{8,12},{9,13},{10,... | collective-permute-start | bytes 6152 | tf_op jit(solution)/shard_map/ppermute | solution.py:556
  60.8 2.2 %project.9 = (f32[432,512]{1,0:T(8,128)S(1)}, f32[1,512]{1,0:T(1,128)S(1)}, f32[1,512]{1,0:T(1,128)}, f32[1,512]{1,0:T(1,128)S(1)}) custom-call(s32[27]{0:T(128)S(1)} %dynamic-slice_bitcast_fusion.where_ref, bf16[1024,512]{1,0:T(8,128)(2,1)S(1)} %get-tuple-element.86.high_ref, bf16[1024,512]{1,0:T(8,128)(2,1)S(1)} %get-tuple-element.87.low_ref, ...), custom_call_target="tpu_custom_call" | custom-call | tf_op jit(solution)/shard_map/project/pallas_call | solution.py:292
  63.1 18.5 %update.1 = (f32[2752,2048]{1,0:T(8,128)}, f32[1,128]{1,0:T(1,128)}, f32[4,688]{1,0:T(4,128)S(1)}) custom-call(s32[27]{0:T(128)S(1)} %dynamic-slice_bitcast_fusion.where_ref, f32[1,512]{1,0:T(1,128)S(1)} %add.20.sums_ref, f32[1,512]{1,0:T(1,128)S(1)} %get-tuple-element.115.most_ref, bf16[512,2048]{1,0:T(8,128)(2,1)S(1)} %get-tuple-element.76.high_ref, ...), custom_call_target="tpu_custom_call" | custom-call | flops 11542724608 | bytes 22544384 | tf_op jit(solution)/shard_map/update/pallas_call | solution.py:380
  (55 shorter events, 11.0 us)
Async XLA Ops:
  4.1 1.7 %collective-permute-start = (f32[128,256]{1,0:T(8,128)}, f32[128,256]{1,0:T(8,128)S(1)}, u32[]{:S(2)}, u32[]{:S(2)}) collective-permute-start(f32[128,256]{1,0:T(8,128)} %get-tuple-element.66), channel_id=1, source_target_pairs={{0,8},{8,0},{16,24},{24,16},{1,9},{9,1},{17,25},{25,17},{2,10},{10... | collective-permute-start | bytes 393224 | tf_op jit(solution)/shard_map/ppermute | solution.py:437
  6.7 6.7 %collective-permute-start.1 = (f32[128,256]{1,0:T(8,128)S(1)}, f32[128,256]{1,0:T(8,128)S(1)}, u32[]{:S(2)}, u32[]{:S(2)}) collective-permute-start(f32[128,256]{1,0:T(8,128)S(1)} %add.21.refs_0_), channel_id=1, source_target_pairs={{0,16},{8,24},{16,0},{24,8},{1,17},{9,25},{17,1},{25,9},{2,18},{10... | collective-permute-start | bytes 393224 | tf_op jit(solution)/shard_map/ppermute | solution.py:441
  13.5 1.9 %collective-permute-start.2 = (bf16[144,256]{1,0:T(8,128)(2,1)S(1)}, bf16[144,256]{1,0:T(8,128)(2,1)S(1)}, u32[]{:S(2)}, u32[]{:S(2)}) collective-permute-start(bf16[144,256]{1,0:T(8,128)(2,1)S(1)} %encode.1.mine_ref), channel_id=1, source_target_pairs={{0,8},{8,0},{16,24},{24,16},{1,9},{9,1},{17,25},{25,17},{2,10},{10... | collective-permute-start | bytes 221192 | tf_op jit(solution)/shard_map/ppermute | solution.py:437
  13.6 18.2 %collective-permute-start.8 = (bf16[1376,256]{1,0:T(8,128)(2,1)S(1)}, bf16[1376,256]{1,0:T(8,128)(2,1)S(1)}, u32[]{:S(2)}, u32[]{:S(2)}) collective-permute-start(bf16[1376,256]{1,0:T(8,128)(2,1)S(1)} %get-tuple-element.80), channel_id=1, source_target_pairs={{0,16},{8,24},{16,0},{24,8},{1,17},{9,25},{17,1},{25,9},{2,18},{10... | collective-permute-start | bytes 2113544 | tf_op jit(solution)/shard_map/ppermute | solution.py:441
  16.0 25.1 %collective-permute-start.11 = (bf16[2752,256]{1,0:T(8,128)(2,1)S(1)}, bf16[2752,256]{1,0:T(8,128)(2,1)S(1)}, u32[]{:S(2)}, u32[]{:S(2)}) collective-permute-start(bf16[2752,256]{1,0:T(8,128)(2,1)S(1)} %bitcast.8), channel_id=1, source_target_pairs={{0,8},{8,0},{16,24},{24,16},{1,9},{9,1},{17,25},{25,17},{2,10},{10... | collective-permute-start | bytes 4227080 | tf_op jit(solution)/shard_map/ppermute | solution.py:437
  16.2 5.1 %collective-permute-start.3 = (bf16[144,512]{1,0:T(8,128)(2,1)S(1)}, bf16[144,512]{1,0:T(8,128)(2,1)S(1)}, u32[]{:S(2)}, u32[]{:S(2)}) collective-permute-start(bf16[144,512]{1,0:T(8,128)(2,1)S(1)} %join.1.refs_0_), channel_id=1, source_target_pairs={{0,2},{2,4},{4,6},{6,7},{7,5},{5,3},{3,1},{1,0},{8,9},{10,8},{12,1... | collective-permute-start | bytes 442376 | tf_op jit(solution)/shard_map/ppermute | solution.py:448
  21.4 4.9 %collective-permute-start.5 = (bf16[144,512]{1,0:T(8,128)(2,1)S(1)}, bf16[144,512]{1,0:T(8,128)(2,1)S(1)}, u32[]{:S(2)}, u32[]{:S(2)}) collective-permute-start(bf16[144,512]{1,0:T(8,128)(2,1)S(1)} %collective-permute-done.3.refs_1_), channel_id=1, source_target_pairs={{0,8},{8,0},{16,24},{24,16},{1,9},{9,1},{17,25},{25,17},{2,10},{10... | collective-permute-start | bytes 442376 | tf_op jit(solution)/shard_map/ppermute | solution.py:437
  21.4 5.1 %collective-permute-start.4 = (bf16[144,512]{1,0:T(8,128)(2,1)S(1)}, bf16[144,512]{1,0:T(8,128)(2,1)S(1)}, u32[]{:S(2)}, u32[]{:S(2)}) collective-permute-start(bf16[144,512]{1,0:T(8,128)(2,1)S(1)} %collective-permute-done.3.refs_1_), channel_id=1, source_target_pairs={{0,2},{2,4},{4,6},{6,7},{7,5},{5,3},{3,1},{1,0},{8,9},{10,8},{12,1... | collective-permute-start | bytes 442376 | tf_op jit(solution)/shard_map/ppermute | solution.py:448
  26.5 1.6 %collective-permute-start.7 = (bf16[144,512]{1,0:T(8,128)(2,1)S(1)}, bf16[144,512]{1,0:T(8,128)(2,1)S(1)}, u32[]{:S(2)}, u32[]{:S(2)}) collective-permute-start(bf16[144,512]{1,0:T(8,128)(2,1)S(1)} %collective-permute-done.4.refs_2_), channel_id=1, source_target_pairs={{0,8},{8,0},{16,24},{24,16},{1,9},{9,1},{17,25},{25,17},{2,10},{10... | collective-permute-start | bytes 442376 | tf_op jit(solution)/shard_map/ppermute | solution.py:437
  26.6 5.1 %collective-permute-start.6 = (bf16[144,512]{1,0:T(8,128)(2,1)S(1)}, bf16[144,512]{1,0:T(8,128)(2,1)S(1)}, u32[]{:S(2)}, u32[]{:S(2)}) collective-permute-start(bf16[144,512]{1,0:T(8,128)(2,1)S(1)} %collective-permute-done.4.refs_2_), channel_id=1, source_target_pairs={{0,2},{2,4},{4,6},{6,7},{7,5},{5,3},{3,1},{1,0},{8,9},{10,8},{12,1... | collective-permute-start | bytes 442376 | tf_op jit(solution)/shard_map/ppermute | solution.py:448
  31.8 9.3 %collective-permute-start.12 = (bf16[1376,256]{1,0:T(8,128)(2,1)S(1)}, bf16[1376,256]{1,0:T(8,128)(2,1)S(1)}, u32[]{:S(2)}, u32[]{:S(2)}) collective-permute-start(bf16[1376,256]{1,0:T(8,128)(2,1)S(1)} %collective-permute-done.8.refs_2_), channel_id=1, source_target_pairs={{0,8},{8,0},{16,24},{24,16},{1,9},{9,1},{17,25},{25,17},{2,10},{10... | collective-permute-start | bytes 2113544 | tf_op jit(solution)/shard_map/ppermute | solution.py:437
  31.8 14.0 %collective-permute-start.14 = (bf16[688,256]{1,0:T(8,128)(2,1)S(1)}, bf16[688,256]{1,0:T(8,128)(2,1)S(1)}, u32[]{:S(2)}, u32[]{:S(2)}) collective-permute-start(bf16[688,256]{1,0:T(8,128)(2,1)S(1)} %get-tuple-element.94), channel_id=1, source_target_pairs={{0,16},{8,24},{16,0},{24,8},{1,17},{9,25},{17,1},{25,9},{2,18},{10... | collective-permute-start | bytes 1056776 | tf_op jit(solution)/shard_map/ppermute | solution.py:441
  33.6 1.8 %collective-permute-start.10 = (bf16[144,512]{1,0:T(8,128)(2,1)S(1)}, bf16[144,512]{1,0:T(8,128)(2,1)S(1)}, u32[]{:S(2)}, u32[]{:S(2)}) collective-permute-start(bf16[144,512]{1,0:T(8,128)(2,1)S(1)} %collective-permute-done.6.refs_3_), channel_id=1, source_target_pairs={{0,8},{8,0},{16,24},{24,16},{1,9},{9,1},{17,25},{25,17},{2,10},{10... | collective-permute-start | bytes 442376 | tf_op jit(solution)/shard_map/ppermute | solution.py:437
  33.8 5.1 %collective-permute-start.9 = (bf16[144,512]{1,0:T(8,128)(2,1)S(1)}, bf16[144,512]{1,0:T(8,128)(2,1)S(1)}, u32[]{:S(2)}, u32[]{:S(2)}) collective-permute-start(bf16[144,512]{1,0:T(8,128)(2,1)S(1)} %collective-permute-done.6.refs_3_), channel_id=1, source_target_pairs={{0,2},{2,4},{4,6},{6,7},{7,5},{5,3},{3,1},{1,0},{8,9},{10,8},{12,1... | collective-permute-start | bytes 442376 | tf_op jit(solution)/shard_map/ppermute | solution.py:448
  35.4 10.4 %collective-permute-start.15 = (bf16[256,256]{1,0:T(8,128)(2,1)S(1)}, bf16[256,256]{1,0:T(8,128)(2,1)S(1)}, u32[]{:S(2)}, u32[]{:S(2)}) collective-permute-start(bf16[256,256]{1,0:T(8,128)(2,1)S(1)} %get-tuple-element.96), channel_id=1, source_target_pairs={{0,16},{8,24},{16,0},{24,8},{1,17},{9,25},{17,1},{25,9},{2,18},{10... | collective-permute-start | bytes 393224 | tf_op jit(solution)/shard_map/ppermute | solution.py:441
  38.9 2.1 %collective-permute-start.13 = (f32[1,128]{1,0:T(1,128)S(1)}, f32[1,128]{1,0:T(1,128)S(1)}, u32[]{:S(2)}, u32[]{:S(2)}) collective-permute-start(f32[1,128]{1,0:T(1,128)S(1)} %bitcast.14), channel_id=1, source_target_pairs={{0,8},{8,0},{16,24},{24,16},{1,9},{9,1},{17,25},{25,17},{2,10},{10... | collective-permute-start | bytes 1544 | tf_op jit(solution)/shard_map/ppermute | solution.py:437
  45.8 1.9 %collective-permute-start.17 = (bf16[688,256]{1,0:T(8,128)(2,1)S(1)}, bf16[688,256]{1,0:T(8,128)(2,1)S(1)}, u32[]{:S(2)}, u32[]{:S(2)}) collective-permute-start(bf16[688,256]{1,0:T(8,128)(2,1)S(1)} %collective-permute-done.14.refs_2_), channel_id=1, source_target_pairs={{0,8},{8,0},{16,24},{24,16},{1,9},{9,1},{17,25},{25,17},{2,10},{10... | collective-permute-start | bytes 1056776 | tf_op jit(solution)/shard_map/ppermute | solution.py:437
  46.3 3.6 %collective-permute-start.16 = (f32[1,512]{1,0:T(1,128)S(1)}, f32[1,512]{1,0:T(1,128)S(1)}, u32[]{:S(2)}, u32[]{:S(2)}) collective-permute-start(f32[1,512]{1,0:T(1,128)S(1)} %get-tuple-element.97), channel_id=1, source_target_pairs={{0,16},{8,24},{16,0},{24,8},{1,17},{9,25},{17,1},{25,9},{2,18},{10... | collective-permute-start | bytes 6152 | tf_op jit(solution)/shard_map/ppermute | solution.py:441
  49.9 8.2 %collective-permute-start.22 = (bf16[432,256]{1,0:T(8,128)(2,1)S(1)}, bf16[432,256]{1,0:T(8,128)(2,1)S(1)}, u32[]{:S(2)}, u32[]{:S(2)}) collective-permute-start(bf16[432,256]{1,0:T(8,128)(2,1)S(1)} %get-tuple-element.111), channel_id=1, source_target_pairs={{0,16},{8,24},{16,0},{24,8},{1,17},{9,25},{17,1},{25,9},{2,18},{10... | collective-permute-start | bytes 663560 | tf_op jit(solution)/shard_map/ppermute | solution.py:441
  50.9 5.2 %collective-permute-start.20 = (bf16[256,256]{1,0:T(8,128)(2,1)S(1)}, bf16[256,256]{1,0:T(8,128)(2,1)S(1)}, u32[]{:S(2)}, u32[]{:S(2)}) collective-permute-start(bf16[256,256]{1,0:T(8,128)(2,1)S(1)} %collective-permute-done.15.refs_2_), channel_id=1, source_target_pairs={{0,8},{8,0},{16,24},{24,16},{1,9},{9,1},{17,25},{25,17},{2,10},{10... | collective-permute-start | bytes 393224 | tf_op jit(solution)/shard_map/ppermute | solution.py:437
  50.9 3.6 %collective-permute-start.18 = (f32[1,512]{1,0:T(1,128)S(1)}, f32[1,512]{1,0:T(1,128)S(1)}, u32[]{:S(2)}, u32[]{:S(2)}) collective-permute-start(f32[1,512]{1,0:T(1,128)S(1)} %add.17), channel_id=1, source_target_pairs={{0,1},{1,0},{2,3},{3,2},{4,5},{5,4},{6,7},{7,6},{8,9},{9,8},{10,11... | collective-permute-start | bytes 6152 | tf_op jit(solution)/shard_map/ppermute | solution.py:556
  54.5 3.6 %collective-permute-start.19 = (f32[1,512]{1,0:T(1,128)S(1)}, f32[1,512]{1,0:T(1,128)S(1)}, u32[]{:S(2)}, u32[]{:S(2)}) collective-permute-start(f32[1,512]{1,0:T(1,128)S(1)} %add.18), channel_id=1, source_target_pairs={{0,2},{1,3},{2,0},{3,1},{4,6},{5,7},{6,4},{7,5},{8,10},{9,11},{10,... | collective-permute-start | bytes 6152 | tf_op jit(solution)/shard_map/ppermute | solution.py:556
  58.1 2.7 %collective-permute-start.23 = (bf16[432,256]{1,0:T(8,128)(2,1)S(1)}, bf16[432,256]{1,0:T(8,128)(2,1)S(1)}, u32[]{:S(2)}, u32[]{:S(2)}) collective-permute-start(bf16[432,256]{1,0:T(8,128)(2,1)S(1)} %collective-permute-done.22.refs_2_), channel_id=1, source_target_pairs={{0,8},{8,0},{16,24},{24,16},{1,9},{9,1},{17,25},{25,17},{2,10},{10... | collective-permute-start | bytes 663560 | tf_op jit(solution)/shard_map/ppermute | solution.py:437
  58.2 4.9 %collective-permute-start.21 = (f32[1,512]{1,0:T(1,128)S(1)}, f32[1,512]{1,0:T(1,128)S(1)}, u32[]{:S(2)}, u32[]{:S(2)}) collective-permute-start(f32[1,512]{1,0:T(1,128)S(1)} %add.19), channel_id=1, source_target_pairs={{0,4},{1,5},{2,6},{3,7},{4,0},{5,1},{6,2},{7,3},{8,12},{9,13},{10,... | collective-permute-start | bytes 6152 | tf_op jit(solution)/shard_map/ppermute | solution.py:556
  (5 other events, 59.8 us)
